TPU v7x, 128 devices: a whole 4x4x4 slice. The times are simulated.
128 devices in a mesh: dp: 8 (over y_lo, z), row: 2 (over y_hi), col: 8 (over x, core).
Axes of the slice: x: 4, y: 4 (y_hi: 2, y_lo: 2; y = y_hi * 2 + y_lo), z: 4, core: 2. Of those that a mesh axis runs over, the one named last changes fastest.
Arguments:
- tokens: bfloat16 [16384, 1536], P(('dp', 'row', 'col')), may hold values from -6 to 6
- cotangent: bfloat16 [16384, 1536], P(('dp', 'row', 'col')), may hold values from -6 to 6
- lengths: int32 [16, 4], P(('dp', 'row')), may hold values from 1 to 960, 1024 in all within a row
- routes: int32 [16384, 8], P(('dp', 'row', 'col')), may hold values from 0 to 39, all different within a row; in each aligned block of 128 rows (0 to 127, 128 to 255, ...) at most 51 rows name the same one
- norm_gains: float32 [2, 1536], replicated, may hold values from 0.5 to 1.5
- gain_first: float32 [2, 1536], replicated, may hold values from -96 to 96
- gain_second: float32 [2, 1536], replicated, may hold values from 589.824 to 7864.32
- router_w: float32 [1536, 40], replicated, may hold values from -0.078125 to 0.078125
- router_first: float32 [1536, 40], replicated, may hold values from -160 to 160
- router_second: float32 [1536, 40], replicated, may hold values from 1572.48 to 20966.4
- projection_weight: float32 [1536, 8, 320], P('dp', 'col'), may hold values from -0.15625 to 0.15625
- projection_first_moment: float32 [1536, 8, 320], P('dp', 'col'), may hold values from -64 to 64
- projection_second_moment: float32 [1536, 8, 320], P('dp', 'col'), may hold values from 311.296 to 4259.84
- w_proj: float32 [1536, 1536], P('col', 'dp'), may hold values from -1.25 to 1.25
- proj_first: float32 [1536, 1536], P('col', 'dp'), may hold values from -8 to 8
- proj_second: float32 [1536, 1536], P('col', 'dp'), may hold values from 4.9152 to 65.536
- w_gate_up: float32 [40, 1536, 2, 512], P('col', 'dp', None, 'row'), may hold values from -0.15625 to 0.15625
- gate_up_first: float32 [40, 1536, 2, 512], P('col', 'dp', None, 'row'), may hold values from -20 to 20
- gate_up_second: float32 [40, 1536, 2, 512], P('col', 'dp', None, 'row'), may hold values from 24.57 to 327.6
- w_down: float32 [40, 512, 1536], P('col', 'row', 'dp'), may hold values from -1 to 1
- down_first: float32 [40, 512, 1536], P('col', 'row', 'dp'), may hold values from -2.5 to 2.5
- down_second: float32 [40, 512, 1536], P('col', 'row', 'dp'), may hold values from 0.52416 to 7.2072
Outputs:
- output: bfloat16 [16384, 1536], P(('dp', 'row', 'col'))
- dtokens: float32 [16384, 1536], P(('dp', 'row', 'col'))
- gain_new: float32 [2, 1536], replicated
- gain_first_new: float32 [2, 1536], replicated
- gain_second_new: float32 [2, 1536], replicated
- router_new: float32 [1536, 40], replicated
- router_first_new: float32 [1536, 40], replicated
- router_second_new: float32 [1536, 40], replicated
- qkv_new: float32 [1536, 8, 320], P('dp', 'col')
- qkv_first_new: float32 [1536, 8, 320], P('dp', 'col')
- qkv_second_new: float32 [1536, 8, 320], P('dp', 'col')
- proj_new: float32 [1536, 1536], P('col', 'dp')
- proj_first_new: float32 [1536, 1536], P('col', 'dp')
- proj_second_new: float32 [1536, 1536], P('col', 'dp')
- gate_up_new: float32 [40, 1536, 2, 512], P('col', 'dp', None, 'row')
- gate_up_first_new: float32 [40, 1536, 2, 512], P('col', 'dp', None, 'row')
- gate_up_second_new: float32 [40, 1536, 2, 512], P('col', 'dp', None, 'row')
- down_new: float32 [40, 512, 1536], P('col', 'row', 'dp')
- down_first_new: float32 [40, 512, 1536], P('col', 'row', 'dp')
- down_second_new: float32 [40, 512, 1536], P('col', 'row', 'dp')
Inputs may be any that keep to these rules, and one draw needn't show every extreme that they name: `lengths`: each row sums to 1024; its largest entry is exactly 960. `routes`: A row names 8 different experts; among the rows of one device no expert is named by more than 51 rows, a bound that some block reaches.
All inputs are finite; a program needn't handle non-finite values.
Results may differ from a plain program's by a relative error of at most 0.025.
Values may be sent and summed in bfloat16 or wider, within the bound.
No kernel may reach another device: no remote copies, remote signals or barrier semaphores. Data moves between devices by JAX's collectives and lax.ppermute only.
A program may use at most 256 MiB of HBM per device.

v0:
```python
import jax
import jax.numpy as jnp
from jax import lax
from jax.sharding import PartitionSpec as P

HEAD_SIZE = 64
STEP = 10
QUERY_PER_KEY = 3


EXACT_MATH = lax.Precision.HIGHEST
NORM_EPS = 1e-05
NEG_FILL = -1e30
BETA_ONE = 0.9
BETA_TWO = 0.95
ADAM_EPS = 1e-08
DECAY_RATE = 0.1
RATE_GAIN = 0.5
RATE_ROUTER = 0.03
RATE_NARROW = 0.05
RATE_WIDE = 0.4


def inv_rms(values):
    return lax.rsqrt(jnp.mean(values * values, axis=-1, keepdims=True) + NORM_EPS)


def doc_index(lengths_row, token_places):
    doc_ends = jnp.cumsum(lengths_row)
    return jnp.sum((token_places[:, None] >= doc_ends[None, :]).astype(jnp.int32), axis=1)


def slot_ranks(route_rows, experts):
    flat_ids = route_rows.reshape(-1)
    route_hits = (flat_ids[:, None] == jnp.arange(experts, dtype=jnp.int32)[None, :]).astype(
        jnp.int32
    )
    earlier = jnp.cumsum(route_hits, axis=0) - route_hits
    return (flat_ids, jnp.sum(earlier * route_hits, axis=1))


def adamw(weight, gradient, moment_one, moment_two, step_rate, weight_decay):
    first_new = BETA_ONE * moment_one + (1.0 - BETA_ONE) * gradient
    second_new = BETA_TWO * moment_two + (1.0 - BETA_TWO) * gradient * gradient
    boost_one = 1.0 / (1.0 - BETA_ONE**STEP)
    boost_two = 1.0 / (1.0 - BETA_TWO**STEP)
    direction = first_new * boost_one / (jnp.sqrt(second_new * boost_two) + ADAM_EPS)
    return (weight - step_rate * (direction + weight_decay * weight), first_new, second_new)


def norm_back(values, inverse, gain_row, upstream):
    normalized = values * inverse
    scaled = upstream * gain_row
    grad_gain = jnp.sum(upstream * normalized, axis=0)
    grad_values = inverse * (
        scaled - normalized * jnp.mean(scaled * normalized, axis=-1, keepdims=True)
    )
    return (grad_values, grad_gain)


def to_experts(outgoing):
    spread = lax.all_to_all(outgoing, "col", split_axis=0, concat_axis=1, tiled=True)
    return lax.all_gather(spread, "row", axis=1, tiled=True)


def from_experts(partial_value):
    experts_dev = partial_value.shape[0]
    model_width = partial_value.shape[2]
    row_count = lax.axis_size("row")
    shaped = partial_value.reshape(experts_dev, row_count, -1, model_width)
    exchanged = lax.all_to_all(
        shaped.astype(jnp.bfloat16), "col", split_axis=2, concat_axis=0, tiled=True
    ).astype(shaped.dtype)
    summed = lax.psum_scatter(
        exchanged.astype(jnp.bfloat16), "row", scatter_dimension=1, tiled=True
    ).astype(jnp.float32)
    return summed.reshape(summed.shape[0], -1, model_width).astype(jnp.bfloat16)


def per_device(
    tokens,
    cotangent,
    lengths,
    routes,
    norm_gains,
    gain_first,
    gain_second,
    router_w,
    router_first,
    router_second,
    projection_weight,
    projection_first_moment,
    projection_second_moment,
    w_proj,
    proj_first,
    proj_second,
    w_gate_up,
    gate_up_first,
    gate_up_second,
    w_down,
    down_first,
    down_second,
):
    col_count = lax.axis_size("col")
    tok_dev, model_width = tokens.shape
    group_rows = tok_dev * col_count
    kv_dev = projection_weight.shape[1]
    experts = w_gate_up.shape[0] * col_count
    top_count = routes.shape[1]
    capacity = max(2, 2 * tok_dev * top_count // experts)
    query_span_width = QUERY_PER_KEY * HEAD_SIZE
    score_scale = HEAD_SIZE ** (-0.5)
    qkv_full, proj_full, gate_up_full, down_full = (
        lax.all_gather(projection_weight.astype(jnp.bfloat16), "dp", axis=0, tiled=True),
        lax.all_gather(w_proj.astype(jnp.bfloat16), "dp", axis=1, tiled=True),
        lax.all_gather(w_gate_up.astype(jnp.bfloat16), "dp", axis=1, tiled=True),
        lax.all_gather(w_down.astype(jnp.bfloat16), "dp", axis=2, tiled=True),
    )
    qkv_mat = qkv_full.reshape(model_width, -1)
    residual_in = tokens.astype(jnp.float32)
    inverse_one = inv_rms(residual_in)
    normalised_input = (residual_in * inverse_one * norm_gains[0]).astype(jnp.bfloat16)
    normed_all = lax.all_gather(normalised_input, "col", axis=0, tiled=True)
    projection_rows = (
        jnp.dot(normed_all, qkv_mat, preferred_element_type=jnp.float32)
        .astype(jnp.bfloat16)
        .reshape(group_rows, kv_dev, -1)
    )
    query_rows = projection_rows[:, :, :query_span_width].reshape(
        group_rows, kv_dev, QUERY_PER_KEY, HEAD_SIZE
    )
    key_rows = projection_rows[:, :, query_span_width : query_span_width + HEAD_SIZE]
    value_rows = projection_rows[:, :, query_span_width + HEAD_SIZE :]
    token_places = jnp.arange(group_rows, dtype=jnp.int32)
    document_index = doc_index(lengths[0], token_places)
    rows_per_block = min(512, group_rows)
    count_blocks = group_rows // rows_per_block
    query_blocks = query_rows.reshape(
        count_blocks, rows_per_block, kv_dev, QUERY_PER_KEY, HEAD_SIZE
    )
    doc_blocks = document_index.reshape(count_blocks, rows_per_block)
    spot_blocks = token_places.reshape(count_blocks, rows_per_block)

    def scores_of(query_blk, doc_blk, spot_blk):
        raw_scores = (
            jnp.einsum("ihgd,jhd->hgij", query_blk, key_rows, preferred_element_type=jnp.float32)
            * score_scale
        )
        allowed = (doc_blk[:, None] == document_index[None, :]) & (
            spot_blk[:, None] >= token_places[None, :]
        )
        return jnp.where(allowed[None, None], raw_scores, NEG_FILL)

    def attend_heads(block_args):
        query_blk, doc_blk, spot_blk = block_args
        scores = scores_of(query_blk, doc_blk, spot_blk)
        row_peak = jnp.max(scores, axis=-1, keepdims=True)
        exp_scores = jnp.exp(scores - row_peak)
        row_total = jnp.sum(exp_scores, axis=-1, keepdims=True)
        attn_probs = (exp_scores / row_total).astype(jnp.bfloat16)
        out_blk = jnp.einsum(
            "hgij,jhd->ihgd", attn_probs, value_rows, preferred_element_type=jnp.float32
        )
        return (out_blk.astype(jnp.bfloat16), (row_peak + jnp.log(row_total))[..., 0])

    visited_blocks, log_norms = lax.map(attend_heads, (query_blocks, doc_blocks, spot_blocks))
    attended = visited_blocks.reshape(group_rows, -1)
    part_rows = attended
    attn_out = lax.psum_scatter(
        jnp.dot(part_rows, proj_full, preferred_element_type=jnp.float32),
        "col",
        scatter_dimension=0,
        tiled=True,
    )
    residual = residual_in + attn_out
    inverse_two = inv_rms(residual)
    normed_two = (residual * inverse_two * norm_gains[1]).astype(jnp.bfloat16)
    router_low = router_w.astype(jnp.bfloat16)
    logits = jnp.dot(normed_two, router_low, preferred_element_type=jnp.float32)
    route_hits = routes[:, :, None] == jnp.arange(experts, dtype=jnp.int32)[None, None, :]
    chosen = jnp.sum(jnp.where(route_hits, logits[:, None, :], 0.0), axis=-1)
    gate_probs = jax.nn.softmax(chosen, axis=-1)
    flat_ids, slot_rank = slot_ranks(routes, experts)
    slot_index = flat_ids * capacity + slot_rank
    empty_slots = jnp.zeros((experts * capacity, model_width), jnp.bfloat16)
    outgoing = (
        empty_slots.at[slot_index]
        .set(jnp.repeat(normed_two, top_count, axis=0))
        .reshape(experts, capacity, model_width)
    )
    expert_in = to_experts(outgoing)
    gate_up = jnp.einsum(
        "esd,edkf->eskf", expert_in, gate_up_full, preferred_element_type=jnp.float32
    )
    gate_pre = gate_up[:, :, 0]
    up_pre = gate_up[:, :, 1]
    hidden = (jax.nn.silu(gate_pre) * up_pre).astype(jnp.bfloat16)
    partial_value = jnp.einsum(
        "esf,efd->esd", hidden, down_full, preferred_element_type=jnp.float32
    )
    returned = from_experts(partial_value)
    picked = (
        returned.reshape(experts * capacity, model_width)[slot_index]
        .reshape(tok_dev, top_count, model_width)
        .astype(jnp.float32)
    )
    mixture = jnp.sum(gate_probs[:, :, None] * picked, axis=1)
    output = (residual + mixture).astype(jnp.bfloat16)
    upstream = cotangent.astype(jnp.float32)
    dgate = jnp.sum(picked * upstream[:, None, :], axis=-1)
    dchosen = gate_probs * (dgate - jnp.sum(gate_probs * dgate, axis=-1, keepdims=True))
    dlogits = jnp.sum(jnp.where(route_hits, dchosen[:, :, None], 0.0), axis=1)
    dpicked_out = (gate_probs[:, :, None] * upstream[:, None, :]).astype(jnp.bfloat16)
    dout_slots = (
        empty_slots.at[slot_index]
        .set(dpicked_out.reshape(-1, model_width))
        .reshape(experts, capacity, model_width)
    )
    dexpert_out = to_experts(dout_slots)
    dhidden = jnp.einsum("esd,efd->esf", dexpert_out, down_full, preferred_element_type=jnp.float32)
    grad_down = jnp.einsum("esf,esd->efd", hidden, dexpert_out, preferred_element_type=jnp.float32)
    sigmoid_gate = jax.nn.sigmoid(gate_pre)
    dgate_pre = dhidden * up_pre * sigmoid_gate * (1.0 + gate_pre * (1.0 - sigmoid_gate))
    dup_pre = dhidden * gate_pre * sigmoid_gate
    dgate_up = jnp.stack([dgate_pre, dup_pre], axis=2).astype(jnp.bfloat16)
    grad_gate_up = jnp.einsum(
        "esd,eskf->edkf", expert_in, dgate_up, preferred_element_type=jnp.float32
    )
    dexpert_in = jnp.einsum(
        "eskf,edkf->esd", dgate_up, gate_up_full, preferred_element_type=jnp.float32
    )
    dreturned = from_experts(dexpert_in)
    dpicked_in = (
        dreturned.reshape(experts * capacity, model_width)[slot_index]
        .reshape(tok_dev, top_count, model_width)
        .astype(jnp.float32)
    )
    dnormed_two = jnp.sum(dpicked_in, axis=1) + jnp.dot(
        dlogits, router_low.astype(jnp.float32).T, precision=EXACT_MATH
    )
    grad_router = jnp.dot(normed_two.astype(jnp.float32).T, dlogits, precision=EXACT_MATH)
    dresid_norm, grad_gain_two = norm_back(residual, inverse_two, norm_gains[1], dnormed_two)
    dresidual = upstream + dresid_norm
    dattn_all = lax.all_gather(dresidual.astype(jnp.bfloat16), "col", axis=0, tiled=True)
    grad_proj = jnp.einsum("ia,ib->ab", attended, dattn_all, preferred_element_type=jnp.float32)
    dattended = jnp.einsum(
        "ib,ab->ia", dattn_all, proj_full, preferred_element_type=jnp.float32
    ).astype(jnp.bfloat16)

    def back_block(running, block_args):
        dkey_sum, dvalue_sum = running
        query_blk, doc_blk, spot_blk, norm_blk, dout_blk = block_args
        scores = scores_of(query_blk, doc_blk, spot_blk)
        attn_probs = jnp.exp(scores - norm_blk[..., None])
        probs_low = attn_probs.astype(jnp.bfloat16)
        dvalue_sum = dvalue_sum + jnp.einsum(
            "hgij,ihgd->jhd", probs_low, dout_blk, preferred_element_type=jnp.float32
        )
        dprobs = jnp.einsum(
            "ihgd,jhd->hgij", dout_blk, value_rows, preferred_element_type=jnp.float32
        )
        row_shift = jnp.sum(attn_probs * dprobs, axis=-1, keepdims=True)
        dscores = (attn_probs * (dprobs - row_shift)).astype(jnp.bfloat16)
        dquery = (
            jnp.einsum("hgij,jhd->ihgd", dscores, key_rows, preferred_element_type=jnp.float32)
            * score_scale
        )
        dkey_sum = (
            dkey_sum
            + jnp.einsum("hgij,ihgd->jhd", dscores, query_blk, preferred_element_type=jnp.float32)
            * score_scale
        )
        return ((dkey_sum, dvalue_sum), dquery.astype(jnp.bfloat16))

    zero_heads = jnp.zeros((group_rows, kv_dev, HEAD_SIZE), jnp.float32)
    (dkey_rows, dvalue_rows), dquery_blocks = lax.scan(
        back_block,
        (zero_heads, zero_heads),
        (
            query_blocks,
            doc_blocks,
            spot_blocks,
            log_norms,
            dattended.reshape(count_blocks, rows_per_block, kv_dev, QUERY_PER_KEY, HEAD_SIZE),
        ),
    )
    dqkv = jnp.concatenate(
        [
            dquery_blocks.reshape(group_rows, kv_dev, query_span_width),
            dkey_rows.astype(jnp.bfloat16),
            dvalue_rows.astype(jnp.bfloat16),
        ],
        axis=-1,
    ).reshape(group_rows, -1)
    grad_qkv = jnp.einsum(
        "ia,ib->ab", normed_all, dqkv, preferred_element_type=jnp.float32
    ).reshape(model_width, kv_dev, -1)
    part_rows = dqkv
    dnormed = lax.psum_scatter(
        jnp.einsum("ib,ab->ia", part_rows, qkv_mat, preferred_element_type=jnp.float32).astype(
            jnp.bfloat16
        ),
        "col",
        scatter_dimension=0,
        tiled=True,
    ).astype(jnp.float32)
    dtokens_norm, grad_gain_one = norm_back(residual_in, inverse_one, norm_gains[0], dnormed)
    dtokens = dresidual + dtokens_norm
    sum_qkv, sum_proj, sum_gate_up, sum_down = (
        lax.psum_scatter(
            grad_qkv.astype(jnp.bfloat16), "dp", scatter_dimension=0, tiled=True
        ).astype(jnp.float32),
        lax.psum_scatter(
            grad_proj.astype(jnp.bfloat16), "dp", scatter_dimension=1, tiled=True
        ).astype(jnp.float32),
        lax.psum_scatter(
            grad_gate_up.astype(jnp.bfloat16), "dp", scatter_dimension=1, tiled=True
        ).astype(jnp.float32),
        lax.psum_scatter(
            grad_down.astype(jnp.bfloat16), "dp", scatter_dimension=2, tiled=True
        ).astype(jnp.float32),
    )
    sum_qkv, sum_proj = (
        lax.psum(sum_qkv.astype(jnp.bfloat16), "row").astype(jnp.float32),
        lax.psum(sum_proj.astype(jnp.bfloat16), "row").astype(jnp.float32),
    )
    sum_gains, sum_router = lax.psum(
        (jnp.stack([grad_gain_one, grad_gain_two]), grad_router), ("dp", "row", "col")
    )
    gain_new, gain_first_new, gain_second_new = adamw(
        norm_gains, sum_gains, gain_first, gain_second, RATE_GAIN, 0.0
    )
    router_new, router_first_new, router_second_new = adamw(
        router_w, sum_router, router_first, router_second, RATE_ROUTER, DECAY_RATE
    )
    qkv_new, qkv_first_new, qkv_second_new = adamw(
        projection_weight,
        sum_qkv,
        projection_first_moment,
        projection_second_moment,
        RATE_NARROW,
        DECAY_RATE,
    )
    proj_new, proj_first_new, proj_second_new = adamw(
        w_proj, sum_proj, proj_first, proj_second, RATE_WIDE, DECAY_RATE
    )
    gate_up_new, gate_up_first_new, gate_up_second_new = adamw(
        w_gate_up, sum_gate_up, gate_up_first, gate_up_second, RATE_NARROW, DECAY_RATE
    )
    down_new, down_first_new, down_second_new = adamw(
        w_down, sum_down, down_first, down_second, RATE_WIDE, DECAY_RATE
    )
    return (
        output,
        dtokens,
        gain_new,
        gain_first_new,
        gain_second_new,
        router_new,
        router_first_new,
        router_second_new,
        qkv_new,
        qkv_first_new,
        qkv_second_new,
        proj_new,
        proj_first_new,
        proj_second_new,
        gate_up_new,
        gate_up_first_new,
        gate_up_second_new,
        down_new,
        down_first_new,
        down_second_new,
    )


def solution(mesh):
    placed = (
        P(("dp", "row", "col"), None),
        P(("dp", "row", "col"), None),
        P(("dp", "row"), None),
        P(("dp", "row", "col"), None),
        P(),
        P(),
        P(),
        P(),
        P(),
        P(),
        P("dp", "col", None),
        P("dp", "col", None),
        P("dp", "col", None),
        P("col", "dp"),
        P("col", "dp"),
        P("col", "dp"),
        P("col", "dp", None, "row"),
        P("col", "dp", None, "row"),
        P("col", "dp", None, "row"),
        P("col", "row", "dp"),
        P("col", "row", "dp"),
        P("col", "row", "dp"),
    )
    return jax.shard_map(
        per_device,
        mesh=mesh,
        in_specs=placed,
        out_specs=(
            P(("dp", "row", "col"), None),
            P(("dp", "row", "col"), None),
            P(),
            P(),
            P(),
            P(),
            P(),
            P(),
            P("dp", "col", None),
            P("dp", "col", None),
            P("dp", "col", None),
            P("col", "dp"),
            P("col", "dp"),
            P("col", "dp"),
            P("col", "dp", None, "row"),
            P("col", "dp", None, "row"),
            P("col", "dp", None, "row"),
            P("col", "row", "dp"),
            P("col", "row", "dp"),
            P("col", "row", "dp"),
        ),
        check_vma=False,
    )
```

profile of v0, /device:TPU:32, one launch (start us, length us, event | category | flops | bytes accessed | tf_op | source)
XLA Modules:
  0.0 1690.1 jit_solution(7896477528533555327)
XLA Ops:
  15.6 31.0 %all_gather.26 = bf16[192,1536]{0,1:T(8,128)(2,1)S(1)} all-gather(bf16[192,192]{0,1:T(8,128)(2,1)S(1)} %copy.235), channel_id=1, replica_groups=mesh['dp'=8,'row'=2,'col'=8] {'dp'}, dimensions={1}, use_global_device_ids=true | all-gather | bytes 663552 | tf_op jit(solution)/shard_map/all_gather | solution.py:115
  46.6 30.8 %all_gather.25 = bf16[1536,1,320]{2,0,1:T(8,128)(2,1)S(1)} all-gather(bf16[192,1,320]{2,0,1:T(8,128)(2,1)S(1)} %copy.305), channel_id=1, replica_groups=mesh['dp'=8,'row'=2,'col'=8] {'dp'}, dimensions={0}, use_global_device_ids=true | all-gather | bytes 1105920 | tf_op jit(solution)/shard_map/all_gather | solution.py:114
  114.6 28.1 %reduce-scatter.13.cloned.1.call-done = f32[128,1536]{1,0:T(8,128)} async-done(((f32[1024,1536]{1,0:T(8,128)}), f32[128,1536]{1,0:T(8,128)}) %reduce-scatter.13.cloned.1.call-update) | async-done | bytes 786448 | tf_op jit(solution)/shard_map/reduce_scatter | solution.py:169
  162.4 83.3 %all_to_all.72 = bf16[40,51,1536]{2,1,0:T(8,128)(2,1)S(1)} all-to-all(bf16[40,51,1536]{2,1,0:T(8,128)(2,1)} %reshape.541), channel_id=1, replica_groups=mesh['dp'=8,'row'=2,'col'=8] {'col'}, dimensions={0} | all-to-all | bytes 12533760 | tf_op jit(solution)/shard_map/all_to_all | solution.py:62
  280.7 83.4 %all_to_all.73 = bf16[40,51,1536]{2,1,0:T(8,128)(2,1)S(1)} all-to-all(bf16[40,51,1536]{2,1,0:T(8,128)(2,1)} %reshape.542), channel_id=1, replica_groups=mesh['dp'=8,'row'=2,'col'=8] {'col'}, dimensions={0} | all-to-all | bytes 12533760 | tf_op jit(solution)/shard_map/all_to_all | solution.py:62
  375.9 36.4 %all-gather.9.cloned.1.call-done = bf16[5,816,1536]{2,1,0:T(8,128)(2,1)} async-done(((bf16[5,408,1536]{2,1,0:T(8,128)(2,1)}), bf16[5,816,1536]{2,1,0:T(8,128)(2,1)}) %all-gather.9.cloned.1.call-update) | async-done | bytes 12533776 | tf_op jit(solution)/shard_map/all_gather | solution.py:63
  412.3 14.5 fusion.71
  426.8 35.4 %all-gather.13.cloned.1.call-done = bf16[5,256,1536]{1,2,0:T(8,128)(2,1)} async-done(((bf16[5,256,192]{1,2,0:T(8,128)(2,1)}), bf16[5,256,1536]{1,2,0:T(8,128)(2,1)}) %all-gather.13.cloned.1.call-update) | async-done | bytes 3932176 | tf_op jit(solution)/shard_map/all_gather | solution.py:117
  462.2 157.9 %all-gather.15.cloned.1.call-done = bf16[5,816,1536]{2,1,0:T(8,128)(2,1)} async-done(((bf16[5,408,1536]{2,1,0:T(8,128)(2,1)}), bf16[5,816,1536]{2,1,0:T(8,128)(2,1)}) %all-gather.15.cloned.1.call-update) | async-done | bytes 12533776 | tf_op jit(solution)/shard_map/all_gather | solution.py:63
  632.1 13.7 bitcast_convert_fusion
  645.7 57.1 %copy.253 = bf16[5,2,408,1536]{3,1,0,2:T(2,128)(2,1)S(1)} copy(bf16[5,2,408,1536]{3,2,1,0:T(8,128)(2,1)} %bitcast.390) | data formatting | bytes 25067520 | tf_op jit(solution)/shard_map/convert_element_type | solution.py:72
  702.8 145.1 %all_to_all.74 = bf16[5,2,408,1536]{3,1,0,2:T(2,128)(2,1)S(1)} all-to-all(bf16[5,2,408,1536]{3,1,0,2:T(2,128)(2,1)S(1)} %copy.253), channel_id=1, replica_groups=mesh['dp'=8,'row'=2,'col'=8] {'col'}, dimensions={2} | all-to-all | bytes 25067520 | tf_op jit(solution)/shard_map/all_to_all | solution.py:71
  876.7 57.1 %copy.245 = bf16[5,2,408,1536]{3,1,0,2:T(2,128)(2,1)S(1)} copy(bf16[5,2,408,1536]{3,2,1,0:T(8,128)(2,1)} %bitcast.383) | data formatting | bytes 25067520 | tf_op jit(solution)/shard_map/convert_element_type | solution.py:72
  933.8 143.7 %all_to_all.75 = bf16[5,2,408,1536]{3,1,0,2:T(2,128)(2,1)S(1)} all-to-all(bf16[5,2,408,1536]{3,1,0,2:T(2,128)(2,1)S(1)} %copy.245), channel_id=1, replica_groups=mesh['dp'=8,'row'=2,'col'=8] {'col'}, dimensions={2} | all-to-all | bytes 25067520 | tf_op jit(solution)/shard_map/all_to_all | solution.py:71
  1126.8 116.0 %reduce-scatter.15.cloned.1.call-done = bf16[40,1,51,1536]{3,0,2,1:T(8,128)(2,1)} async-done(((bf16[40,2,51,1536]{3,0,2,1:T(8,128)(2,1)}), bf16[40,1,51,1536]{3,0,2,1:T(8,128)(2,1)}) %reduce-scatter.15.cloned.1.call-update) | async-done | bytes 6266896 | tf_op jit(solution)/shard_map/reduce_scatter | solution.py:74
  1279.7 27.0 %all-gather.17.cloned.1.call-done = bf16[1024,1536]{1,0:T(8,128)(2,1)} async-done(((bf16[128,1536]{1,0:T(8,128)(2,1)}), bf16[1024,1536]{1,0:T(8,128)(2,1)}) %all-gather.17.cloned.1.call-update) | async-done | bytes 3145744 | tf_op jit(solution)/shard_map/all_gather | solution.py:244
  1319.6 21.8 %while.29 = (s32[]{:T(128)}, f32[1024,1,64]{0,2,1:T(8,128)S(1)}, f32[1024,1,64]{0,2,1:T(8,128)}, bf16[2,512,1,3,64]{1,4,3,2,0:T(8,128)(2,1)S(1)}, bf16[2,512,1,3...) while((s32[]{:T(128)}, f32[1024,1,64]{0,2,1:T(8,128)S(1)}, ...), condition=%wide.region_27.28_spmd.clone, body=%wide.region_25.27_spmd.clone.sunk | while | flops 1032321536 | bytes 53868776 | solution.py:276
  1360.3 14.4 fusion.77
  1379.2 17.4 %reduce-scatter.25.cloned.1.call-done = bf16[192,320]{1,0:T(8,128)(2,1)} async-done(((bf16[1536,320]{1,0:T(8,128)(2,1)}), bf16[192,320]{1,0:T(8,128)(2,1)}) %reduce-scatter.25.cloned.1.call-update) | async-done | bytes 122896
  1408.7 40.9 %reduce-scatter.23.cloned.1.call-done = bf16[5,256,192]{1,2,0:T(8,128)(2,1)} async-done(((bf16[5,256,1536]{1,2,0:T(8,128)(2,1)}), bf16[5,256,192]{1,2,0:T(8,128)(2,1)}) %reduce-scatter.23.cloned.1.call-update) | async-done | bytes 491536 | tf_op jit(solution)/shard_map/reduce_scatter | solution.py:319
  1453.7 85.4 %reduce-scatter.21.cloned.1.call-done = bf16[5,192,2,256]{3,1,2,0:T(8,128)(2,1)} async-done(((bf16[5,1536,2,256]{3,1,2,0:T(8,128)(2,1)}), bf16[5,192,2,256]{3,1,2,0:T(8,128)(2,1)}) %reduce-scatter.21.cloned.1.call-update) | async-done | bytes 983056 | tf_op jit(solution)/shard_map/reduce_scatter | solution.py:316
  1551.5 19.9 %all-reduce.4.cloned.1.call-done = f32[1536,40]{0,1:T(8,128)} async-done(((f32[1536,40]{0,1:T(8,128)}), f32[1536,40]{0,1:T(8,128)}) %all-reduce.4.cloned.1.call-update) | async-done | bytes 245776 | tf_op jit(solution)/shard_map/psum | solution.py:327
  1573.6 30.3 %all-reduce.6.cloned.1.call-done = (bf16[192,1,320]{0,2,1:T(8,128)(2,1)}, bf16[192,192]{1,0:T(8,128)(2,1)}) async-done(((bf16[192,1,320]{0,2,1:T(8,128)(2,1)}, bf16[192,192]{1,0:T(8,128)(2,1)}), (bf16[192,1,320]{0,2,1:T(8,128)(2,1)}, bf16[192,192]{1,0:T(8,128)(2,1)})) %all-reduce.6.cloned.1.call-update) | async-done | bytes 196624 | tf_op jit(solution)/shard_map/psum | solution.py:324
  1614.2 64.6 %psum.28 = f32[2,1536]{1,0:T(2,128)S(1)} all-reduce(f32[2,1536]{1,0:T(2,128)S(1)} %pad_maximum_fusion.1), channel_id=1, replica_groups=mesh['dp'=8,'row'=2,'col'=8] {'dp','row','col'}, use_global_device_ids=true, to_apply=%region_32.33 | all-reduce | flops 3072 | bytes 24576 | tf_op jit(solution)/shard_map/psum | solution.py:327
  (321 shorter events, 351.9 us)
Async XLA Ops:
  8.0 69.3 %all-gather.7.cloned.1.call-start = ((), (), s32[]{:S(2)}) async-start(), calls=%async_computation.12 | async-start | bytes 3538944 | tf_op jit(solution)/shard_map/all_gather | solution.py:123
  10.1 133.9 %copy-start.36 = (f32[1536]{0:T(1024)}, f32[1536]{0:T(1024)S(1)}, u32[]{:S(2)}) copy-start(f32[1536]{0:T(1024)S(1)} %get-tuple-element.460) | copy-start | bytes 18436
  12.6 130.0 %reduce-scatter.13.cloned.1.call-start = ((), (), s32[]{:S(2)}) async-start(), calls=%async_computation.13 | async-start | bytes 7077888 | tf_op jit(solution)/shard_map/reduce_scatter | solution.py:169
  99.1 276.7 %all-gather.11.cloned.1.call-start = ((), (), s32[]{:S(2)}) async-start(), calls=%async_computation.15 | async-start | bytes 8847360 | tf_op jit(solution)/shard_map/all_gather | solution.py:116
  101.7 310.6 %all-gather.9.cloned.1.call-start = ((), (), s32[]{:S(2)}) async-start(), calls=%async_computation.14 | async-start | bytes 18800640 | tf_op jit(solution)/shard_map/all_gather | solution.py:63
  257.3 205.0 %all-gather.13.cloned.1.call-start = ((), (), s32[]{:S(2)}) async-start(), calls=%async_computation.16 | async-start | bytes 4423680 | tf_op jit(solution)/shard_map/all_gather | solution.py:117
  259.3 360.9 %all-gather.15.cloned.1.call-start = ((), (), s32[]{:S(2)}) async-start(), calls=%async_computation.18 | async-start | bytes 18800640 | tf_op jit(solution)/shard_map/all_gather | solution.py:63
  375.6 721.6 %reduce-scatter.17.cloned.1.call-start = ((), (), s32[]{:S(2)}) async-start(), calls=%async_computation.19 | async-start | bytes 18800640 | tf_op jit(solution)/shard_map/reduce_scatter | solution.py:74
  632.1 235.7 %copy-start.16 = (bf16[5,816,256]{2,1,0:T(8,128)(2,1)}, bf16[5,816,256]{2,1,0:T(8,128)(2,1)S(1)}, u32[]{:S(2)}) copy-start(bf16[5,816,256]{2,1,0:T(8,128)(2,1)S(1)} %get-tuple-element.536) | copy-start | bytes 6266884
  867.3 375.5 %reduce-scatter.15.cloned.1.call-start = ((), (), s32[]{:S(2)}) async-start(), calls=%async_computation.17 | async-start | bytes 18800640 | tf_op jit(solution)/shard_map/reduce_scatter | solution.py:74
  1097.1 209.6 %all-gather.17.cloned.1.call-start = ((), (), s32[]{:S(2)}) async-start(), calls=%async_computation.20 | async-start | bytes 3538944 | tf_op jit(solution)/shard_map/all_gather | solution.py:244
  1279.4 98.1 %reduce-scatter.27.cloned.1.call-start = ((), (), s32[]{:S(2)}) async-start(), calls=%async_computation.26 | async-start | bytes 884736
  1319.4 77.1 %reduce-scatter.25.cloned.1.call-start = ((), (), s32[]{:S(2)}) async-start(), calls=%async_computation.25 | async-start | bytes 1327104
  1347.7 102.0 %reduce-scatter.23.cloned.1.call-start = ((), (), s32[]{:S(2)}) async-start(), calls=%async_computation.24 | async-start | bytes 4423680 | tf_op jit(solution)/shard_map/reduce_scatter | solution.py:319
  1360.2 178.8 %reduce-scatter.21.cloned.1.call-start = ((), (), s32[]{:S(2)}) async-start(), calls=%async_computation.23 | async-start | bytes 8847360 | tf_op jit(solution)/shard_map/reduce_scatter | solution.py:316
  1374.8 196.7 %all-reduce.4.cloned.1.call-start = ((), (), s32[]{:S(2)}) async-start(), calls=%async_computation.22 | async-start | bytes 491520 | tf_op jit(solution)/shard_map/psum | solution.py:327
  1377.5 226.4 %all-reduce.6.cloned.1.call-start = ((), (), s32[]{:S(2)}) async-start(), calls=%async_computation.27 | async-start | bytes 524288 | tf_op jit(solution)/shard_map/psum | solution.py:324
  1398.3 214.5 %reduce-scatter.19.cloned.1.call-start = ((), (), s32[]{:S(2)}) async-start(), calls=%async_computation.21 | async-start | bytes 3538944 | tf_op jit(solution)/shard_map/reduce_scatter | solution.py:299
  1403.0 136.0 %copy-start.9 = (f32[5,192,2,256]{3,2,1,0:T(2,128)S(1)}, f32[5,192,2,256]{3,2,1,0:T(2,128)}, u32[]{:S(2)}) copy-start(f32[5,192,2,256]{3,2,1,0:T(2,128)} %param.42) | copy-start | bytes 5898244
  1551.4 127.4 %copy-start.51 = (f32[2,1536]{1,0:T(2,128)S(1)}, f32[2,1536]{1,0:T(2,128)}, u32[]{:S(2)}) copy-start(f32[2,1536]{1,0:T(2,128)} %param.30) | copy-start | bytes 36868
  1551.4 128.8 %copy-start.23 = (bf16[128,1536]{1,0:T(8,128)(2,1)S(1)}, bf16[128,1536]{1,0:T(8,128)(2,1)}, u32[]{:S(2)}) copy-start(bf16[128,1536]{1,0:T(8,128)(2,1)} %param.27) | copy-start | bytes 1179652
  1551.4 128.8 %copy-start.24 = (f32[128,1536]{1,0:T(8,128)S(1)}, f32[128,1536]{1,0:T(8,128)}, u32[]{:S(2)}) copy-start(f32[128,1536]{1,0:T(8,128)} %get-tuple-element.455) | copy-start | bytes 2359300
  1551.4 128.8 %copy-start.58 = (f32[128]{0:T(128)S(1)}, f32[128]{0:T(128)}, u32[]{:S(2)}) copy-start(f32[128]{0:T(128)} %copy-done.56) | copy-start | bytes 1540
  1551.5 128.8 %copy-start.64 = (f32[128]{0:T(128)S(1)}, f32[128]{0:T(128)}, u32[]{:S(2)}) copy-start(f32[128]{0:T(128)} %copy-done.63) | copy-start | bytes 1540
  (59 other events, 914.0 us)
Sparse Core Ops, SparseCore 0:
  12.7 29.7 all-gather.6
  99.2 43.3 reduce-scatter.12
  1279.5 27.1 all-gather.16
  1381.3 190.0 all-reduce.3
  1574.5 29.3 all-reduce.5
Sparse Core Ops, SparseCore 1:
  101.8 85.8 all-gather.10
  257.3 154.9 all-gather.8
  414.4 47.8 all-gather.12
  463.9 156.2 all-gather.14
  867.4 145.7 reduce-scatter.16
  1097.2 145.6 reduce-scatter.14
  1319.5 35.6 reduce-scatter.26
  1358.1 38.3 reduce-scatter.24
  1399.0 50.6 reduce-scatter.22
  1452.2 86.8 reduce-scatter.20
  1541.5 37.3 reduce-scatter.18
where the time goes:
time: 1700 us; the launch traced here: 1690 us
  waiting for transfers between devices  595 us (35%)
  blocking collectives  582 us (34%)
  local copies, waits for them, and re-layouts  301 us (18%)
  matrix products  123 us (7%)
  other arithmetic  69.4 us (4%)
    all_to_all x2, blocking collectives, from_experts(): lax.all_to_all(shaped.astype(jnp.bfloat16), 'col', split_axis=2, concat_a...  289 us
    all_gather x2, waiting for transfers between devices, to_experts(): return lax.all_gather(spread, 'row', axis=1, tiled=True)  194 us
    all_to_all x2, blocking collectives, to_experts(): lax.all_to_all(outgoing, 'col', split_axis=0, concat_axis=1, tiled=True)  167 us
    reduce_scatter x2, waiting for transfers between devices, from_experts(): lax.psum_scatter(exchanged.astype(jnp.bfloat16), 'row', scatter_dimension...  116 us
    convert_element_type x2, local copies, waits for them, and re-layouts, from_experts(): shaped.astype(jnp.bfloat16)  114 us
    reduce_scatter x1, waiting for transfers between devices, per_device(): lax.psum_scatter(grad_gate_up.astype(jnp.bfloat16), 'dp', scatter_dimensi...  85.4 us
    psum x1, blocking collectives, per_device(): lax.psum((jnp.stack([grad_gain_one, grad_gain_two]), grad_router), ('dp',...  64.6 us
    reduce_scatter x1, waiting for transfers between devices, per_device(): lax.psum_scatter(grad_down.astype(jnp.bfloat16), 'dp', scatter_dimension=...  40.9 us
  transfers between devices with their start and end apart: 16, of which 11 were waited for; matrix products, arithmetic and copies ran while one was open for 17% of the time, Pallas kernels for 0%

commit v1 on v0

v1 whole, which is shorter than its diff:
```python
import functools

import jax
import jax.numpy as jnp
from jax import lax
from jax.experimental import pallas as pl
from jax.experimental.pallas import tpu as pltpu
from jax.sharding import PartitionSpec as P

HEAD_SIZE = 64
STEP = 10
QUERY_PER_KEY = 3
SPAN = QUERY_PER_KEY * HEAD_SIZE
QKV = SPAN + 2 * HEAD_SIZE
MODEL = 1536
ROWS = 128
STORED = 192
GROUP = 1024
PLANE = 2048
FF_DEV = 256
EXPERTS = 40
EXPERTS_DEV = 5
SLOTS = 112
TILE = 512
PAIR = 256
QUERY_TILE = 256
EXTRA = 128
CHUNKS = ((0, 1), (1, 2), (3, 2))

EXACT_MATH = lax.Precision.HIGHEST
NORM_EPS = 1e-05
NEG_FILL = -1e30
BETA_ONE = 0.9
BETA_TWO = 0.95
ADAM_EPS = 1e-08
DECAY_RATE = 0.1
RATE_GAIN = 0.5
RATE_ROUTER = 0.03
RATE_NARROW = 0.05
RATE_WIDE = 0.4
SCALE = HEAD_SIZE ** (-0.5)
F32 = jnp.float32
BF16 = jnp.bfloat16
VMEM_LIMIT = 60 * 1024 * 1024


def inv_rms(values):
    return lax.rsqrt(jnp.mean(values * values, axis=-1, keepdims=True) + NORM_EPS)


def adamw(weight, gradient, moment_one, moment_two, step_rate, weight_decay):
    first_new = BETA_ONE * moment_one + (1.0 - BETA_ONE) * gradient
    second_new = BETA_TWO * moment_two + (1.0 - BETA_TWO) * gradient * gradient
    boost_one = 1.0 / (1.0 - BETA_ONE**STEP)
    boost_two = 1.0 / (1.0 - BETA_TWO**STEP)
    direction = first_new * boost_one / (jnp.sqrt(second_new * boost_two) + ADAM_EPS)
    return (weight - step_rate * (direction + weight_decay * weight), first_new, second_new)


def norm_back(values, inverse, gain_row, upstream):
    normalized = values * inverse
    scaled = upstream * gain_row
    grad_gain = jnp.sum(upstream * normalized, axis=0)
    grad_values = inverse * (
        scaled - normalized * jnp.mean(scaled * normalized, axis=-1, keepdims=True)
    )
    return (grad_values, grad_gain)


def dot(a, b):
    return jnp.dot(a, b, preferred_element_type=F32)


def dot_nt(a, b):
    return lax.dot_general(a, b, (((1,), (1,)), ((), ())), preferred_element_type=F32)


def dot_tn(a, b):
    return lax.dot_general(a, b, (((0,), (0,)), ((), ())), preferred_element_type=F32)


def row_blocks(refs):
    blocks = []
    for ref in refs:
        for start in range(0, ref.shape[0], ROWS):
            blocks.append((ref, start))
    return blocks


def place(order_ref, block):
    return pl.ds(pl.multiple_of(order_ref[block] * ROWS, ROWS), ROWS)


def stored_rows(spread_ref, block):
    return pl.ds(pl.multiple_of(spread_ref[block] * STORED, STORED), STORED)


def visible(doc_row_ref, doc_col_ref, tile):
    keys = (tile + 1) * QUERY_TILE
    key_at = lax.broadcasted_iota(jnp.int32, (keys, QUERY_TILE), 0)
    query_at = lax.broadcasted_iota(jnp.int32, (keys, QUERY_TILE), 1) + tile * QUERY_TILE
    same = doc_col_ref[:keys, :] == doc_row_ref[:, tile * QUERY_TILE : keys]
    return same & (key_at <= query_at)


def attend_kernel(order_ref, spread_ref, doc_row_ref, doc_col_ref, *refs):
    normed_ref, w_ref, qkv_ref, att_ref, lse_ref, near_ref, far_ref = refs[-7:]
    pieces, weights = refs[:8], refs[8:-7]
    for block, (ref, start) in enumerate(row_blocks(pieces)):
        normed_ref[place(order_ref, block), :] = ref[start : start + ROWS, :]
    for block, ref in enumerate(weights):
        for other in range(2):
            w_ref[stored_rows(spread_ref, 2 * block + other), :] = ref[other]
    for tile in range(GROUP // QUERY_TILE):
        rows = slice(tile * QUERY_TILE, (tile + 1) * QUERY_TILE)
        qkv_ref[rows, :] = dot(normed_ref[rows, :], w_ref[...])[:, :QKV].astype(BF16)
    keys_all = qkv_ref[:, SPAN : SPAN + HEAD_SIZE]
    values_t = qkv_ref[:, SPAN + HEAD_SIZE : QKV].astype(F32).T.astype(BF16)
    lse_ref[...] = jnp.zeros_like(lse_ref)
    for tile in range(GROUP // QUERY_TILE):
        keys = (tile + 1) * QUERY_TILE
        rows = slice(tile * QUERY_TILE, keys)
        allowed = visible(doc_row_ref, doc_col_ref, tile)
        outs = [jnp.zeros((HEAD_SIZE, QUERY_TILE), F32)]
        for head in range(QUERY_PER_KEY):
            query = qkv_ref[rows, head * HEAD_SIZE : (head + 1) * HEAD_SIZE]
            scores = jnp.where(allowed, dot_nt(keys_all[:keys], query) * SCALE, NEG_FILL)
            peak = jnp.max(scores, axis=0, keepdims=True)
            weights = jnp.exp(scores - peak)
            total = jnp.sum(weights, axis=0, keepdims=True)
            probs = (weights * (1.0 / total)).astype(BF16)
            outs.append(dot(values_t[:, :keys], probs))
            lse_ref[head : head + 1, rows] = peak + jnp.log(total)
        att_ref[rows, :] = jnp.concatenate(outs, axis=0).T.astype(BF16)
    proj = w_ref[:, SPAN + HEAD_SIZE :]
    for block in range(GROUP // ROWS):
        part_ref = near_ref if block < 4 else far_ref
        part_ref[block % 4 * ROWS : (block % 4 + 1) * ROWS, :] = dot_nt(
            att_ref[place(order_ref, block), :], proj
        ).astype(BF16)


def attend_back_kernel(
    order_ref,
    spread_ref,
    doc_row_ref,
    doc_col_ref,
    gain_ref,
    w_ref,
    normed_ref,
    qkv_ref,
    att_ref,
    lse_ref,
    *refs,
):
    pieces, refs = refs[:8], refs[8:]
    near_ref, far_ref, *grads_refs, dgain_ref = refs[:7]
    dattn_ref, datt_ref, dqkv_ref, dkv_ref, whole_ref = refs[7:]
    for block, (ref, start) in enumerate(row_blocks(pieces)):
        dattn_ref[place(order_ref, block), :] = ref[start : start + ROWS, :]
    proj = w_ref[:, SPAN + HEAD_SIZE :]
    for tile in range(GROUP // QUERY_TILE):
        rows = slice(tile * QUERY_TILE, (tile + 1) * QUERY_TILE)
        datt_ref[rows, :] = dot(dattn_ref[rows, :], proj).astype(BF16)
    keys_all = qkv_ref[:, SPAN : SPAN + HEAD_SIZE]
    values_all = qkv_ref[:, SPAN + HEAD_SIZE : QKV]
    keys_t = keys_all.astype(F32).T.astype(BF16)
    dkv_ref[...] = jnp.zeros_like(dkv_ref)
    for tile in range(GROUP // QUERY_TILE):
        keys = (tile + 1) * QUERY_TILE
        rows = slice(tile * QUERY_TILE, keys)
        allowed = visible(doc_row_ref, doc_col_ref, tile)
        outs = []
        for head in range(QUERY_PER_KEY):
            query = qkv_ref[rows, head * HEAD_SIZE : (head + 1) * HEAD_SIZE]
            dout = datt_ref[rows, (head + 1) * HEAD_SIZE : (head + 2) * HEAD_SIZE]
            scores = jnp.where(allowed, dot_nt(keys_all[:keys], query) * SCALE, NEG_FILL)
            probs = jnp.exp(scores - lse_ref[head : head + 1, rows])
            dprobs = dot_nt(values_all[:keys], dout)
            shift = jnp.sum(probs * dprobs, axis=0, keepdims=True)
            dscores = (probs * (dprobs - shift)).astype(BF16)
            dkv_ref[:keys, :HEAD_SIZE] += dot(dscores, query)
            dkv_ref[:keys, HEAD_SIZE:] += dot(probs.astype(BF16), dout)
            outs.append(dot(keys_t[:, :keys], dscores))
        dqkv_ref[rows, :SPAN] = (jnp.concatenate(outs, axis=0).T * SCALE).astype(BF16)
    dqkv_ref[:, SPAN : SPAN + HEAD_SIZE] = (dkv_ref[:, :HEAD_SIZE] * SCALE).astype(BF16)
    dqkv_ref[:, SPAN + HEAD_SIZE :] = dkv_ref[:, HEAD_SIZE:].astype(BF16)
    qkv_mat = w_ref[:, :QKV]
    dgain = jnp.zeros((1, MODEL), F32)
    for block in range(GROUP // ROWS):
        at = place(order_ref, block)
        part = dot_nt(dqkv_ref[at, :], qkv_mat)
        dgain = dgain + jnp.sum(part * normed_ref[at, :].astype(F32), axis=0, keepdims=True)
        part_ref = near_ref if block < 4 else far_ref
        part_ref[block % 4 * ROWS : (block % 4 + 1) * ROWS, :] = part.astype(BF16)
    dgain_ref[...] = dgain / gain_ref[...]
    for start in range(0, MODEL, PAIR):
        cols = slice(start, start + PAIR)
        qkv_part = dot_tn(dqkv_ref[...], normed_ref[:, cols])
        proj_part = dot_tn(att_ref[...], dattn_ref[:, cols])[HEAD_SIZE:]
        whole_ref[cols, :] = jnp.concatenate([qkv_part, proj_part], axis=0).T.astype(BF16)
    for block in range(8):
        grads_refs[block // 2][block % 2] = whole_ref[stored_rows(spread_ref, block), :]


def vmem_spec():
    return pl.BlockSpec(memory_space=pltpu.VMEM)


def smem_spec():
    return pl.BlockSpec(memory_space=pltpu.SMEM)


def attend(order, spread, doc_row, doc_col, pieces, weights):
    return pl.pallas_call(
        attend_kernel,
        in_specs=[smem_spec()] * 2 + [vmem_spec()] * (2 + len(pieces) + len(weights)),
        out_specs=[vmem_spec()] * 7,
        out_shape=[
            jax.ShapeDtypeStruct((GROUP, MODEL), BF16),
            jax.ShapeDtypeStruct((MODEL, 2 * PAIR), BF16),
            jax.ShapeDtypeStruct((GROUP, QKV), BF16),
            jax.ShapeDtypeStruct((GROUP, PAIR), BF16),
            jax.ShapeDtypeStruct((8, GROUP), F32),
            jax.ShapeDtypeStruct((GROUP // 2, MODEL), BF16),
            jax.ShapeDtypeStruct((GROUP // 2, MODEL), BF16),
        ],
        compiler_params=pltpu.CompilerParams(vmem_limit_bytes=VMEM_LIMIT),
        cost_estimate=pl.CostEstimate(
            flops=4 * 10**9, bytes_accessed=12 * 10**6, transcendentals=2 * 10**6
        ),
        name="attend",
    )(order, spread, doc_row, doc_col, *pieces, *weights)


def attend_back(order, spread, doc_row, doc_col, gain, weights, normed, qkv, att, lse, pieces):
    return pl.pallas_call(
        attend_back_kernel,
        in_specs=[smem_spec()] * 2 + [vmem_spec()] * (8 + len(pieces)),
        out_specs=[vmem_spec()] * 7,
        out_shape=[
            jax.ShapeDtypeStruct((GROUP // 2, MODEL), BF16),
            jax.ShapeDtypeStruct((GROUP // 2, MODEL), BF16),
        ]
        + [jax.ShapeDtypeStruct((2, STORED, 2 * PAIR), BF16)] * 4
        + [
            jax.ShapeDtypeStruct((1, MODEL), F32),
        ],
        scratch_shapes=[
            pltpu.VMEM((GROUP, MODEL), BF16),
            pltpu.VMEM((GROUP, PAIR), BF16),
            pltpu.VMEM((GROUP, QKV), BF16),
            pltpu.VMEM((GROUP, 2 * HEAD_SIZE), F32),
            pltpu.VMEM((MODEL, 2 * PAIR), BF16),
        ],
        compiler_params=pltpu.CompilerParams(vmem_limit_bytes=VMEM_LIMIT),
        cost_estimate=pl.CostEstimate(
            flops=8 * 10**9, bytes_accessed=16 * 10**6, transcendentals=2 * 10**6
        ),
        name="attend_back",
    )(order, spread, doc_row, doc_col, gain, weights, normed, qkv, att, lse, *pieces)


def moe_kernel(first_ref, rank_ref, bias_ref, router_ref, w_ref, *refs, begin, count, more):
    sources, refs = (refs[:4], refs[4:8]), refs[8:]
    if more:
        prev_out_ref, prev_dn_ref = refs[:2]
        refs = refs[2:]
    out_ref, dn_ref, g_ref, in_all, dout_all, hid_all, dgu_all, held, sems = refs
    step = pl.program_id(0)
    last = PLANE // TILE - 1

    def copies(tile):
        return [
            pltpu.make_async_copy(
                sources[kind][tile], held.at[kind, tile % 2], sems.at[kind, tile % 2]
            )
            for kind in range(2)
        ]

    for tile in range(last + 1):

        @pl.when(step == max(tile - 1, 0))
        def _():
            for copy in copies(tile):
                copy.start()

    for tile in range(last + 1):

        @pl.when(step == tile)
        def _():
            for copy in copies(tile):
                copy.wait()

    t_ref, c_ref = held.at[0, lax.rem(step, 2)], held.at[1, lax.rem(step, 2)]
    pairs = TILE // PAIR
    height = pairs * SLOTS
    spot = pl.ds(pl.multiple_of(step * height, 16), height)
    logits = dot_nt(router_ref[...], t_ref[...]) + bias_ref[...]
    logits = jnp.exp(logits - jnp.max(logits, axis=0, keepdims=True))
    gates = logits / jnp.sum(logits, axis=0, keepdims=True)
    slot_at = lax.broadcasted_iota(jnp.int32, (SLOTS, PAIR), 0)
    picks, slot_gates, ins, cots = [], [], [], []
    for pair in range(pairs):
        cols = slice(pair * PAIR, (pair + 1) * PAIR)
        hits = [slot_at == rank_ref[pair, begin + e : begin + e + 1, :] for e in range(count)]
        slot_gates.append(
            [
                jnp.sum(
                    jnp.where(hits[e], gates[begin + e : begin + e + 1, cols], 0.0),
                    axis=1,
                    keepdims=True,
                )
                for e in range(count)
            ]
        )
        pick = jnp.concatenate([jnp.where(h, 1.0, 0.0).astype(BF16) for h in hits], axis=0)
        picks.append(pick)
        ins.append(dot(pick, t_ref[cols, :]).astype(BF16))
        cots.append(dot(pick, c_ref[cols, :]).astype(BF16))
    mixed = [[] for _ in range(pairs)]
    dins = [[] for _ in range(pairs)]
    lane = lax.broadcasted_iota(jnp.int32, (height, EXTRA), 1)
    for e in range(count):
        part = slice(e * SLOTS, (e + 1) * SLOTS)
        rows_in = jnp.concatenate([v[part] for v in ins], axis=0)
        rows_cot = jnp.concatenate([v[part] for v in cots], axis=0)
        gate = jnp.concatenate([v[e] for v in slot_gates], axis=0)
        gate_up_w = w_ref[:, e, :, : 2 * FF_DEV].reshape(MODEL, 2 * FF_DEV)
        down_w = w_ref[:, e, :, 2 * FF_DEV :].reshape(MODEL, FF_DEV)
        gate_up = dot(rows_in, gate_up_w)
        pre, up = gate_up[:, :FF_DEV], gate_up[:, FF_DEV:]
        sig = 1.0 / (1.0 + jnp.exp(-pre))
        silu = pre * sig
        hidden = (silu * up).astype(BF16)
        plain = dot(rows_cot, down_w)
        dgate = jnp.sum(hidden.astype(F32) * plain, axis=1, keepdims=True)
        dhidden = plain * gate
        dpre = dhidden * up * sig * (1.0 + pre * (1.0 - sig))
        dgu = jnp.concatenate([dpre, dhidden * silu], axis=1).astype(BF16)
        in_all[e, spot, :] = rows_in
        dout_all[e, spot, :] = (rows_cot.astype(F32) * gate).astype(BF16)
        hid_all[e, spot, :] = hidden
        dgu_all[e, spot, :] = dgu
        mix = (dot_nt(hidden, down_w) * gate).astype(BF16)
        din = dot_nt(dgu, gate_up_w).astype(BF16)
        high = dgate.astype(BF16).astype(F32)
        tail = jnp.where(lane == first_ref[0] + (begin + e), high, 0.0) + jnp.where(
            lane == first_ref[0] + (begin + e + EXPERTS), dgate - high, 0.0
        )
        din = jnp.concatenate([din, tail.astype(BF16)], axis=1)
        for pair in range(pairs):
            rows = slice(pair * SLOTS, (pair + 1) * SLOTS)
            mixed[pair].append(mix[rows])
            dins[pair].append(din[rows])
    for pair in range(pairs):
        cols = slice(pair * PAIR, (pair + 1) * PAIR)
        out = dot_tn(picks[pair], jnp.concatenate(mixed[pair], axis=0))
        dn = dot_tn(picks[pair], jnp.concatenate(dins[pair], axis=0))
        if more:
            out = out + prev_out_ref[cols, :].astype(F32)
            dn = dn + prev_dn_ref[cols, :].astype(F32)
        out_ref[cols, :] = out.astype(BF16)
        dn_ref[cols, :] = dn.astype(BF16)

    @pl.when(step == last)
    def _():
        for e in range(count):
            for start in range(0, MODEL, 2 * 192):
                cols = slice(start, start + 384)
                gate_up_g = dot_tn(in_all[e, :, cols], dgu_all[e])
                down_g = dot_tn(dout_all[e, :, cols], hid_all[e])
                both = jnp.concatenate([gate_up_g, down_g], axis=1).astype(BF16)
                for half in range(2):
                    g_ref[start // 192 + half, e, :, :] = both[half * 192 : (half + 1) * 192, :]


def moe(chunk, first, rank, bias, router_t, weights, rows, cots, previous):
    begin, count = chunk
    height = PLANE // PAIR * SLOTS
    wide = pl.BlockSpec((TILE, MODEL), lambda i: (i, 0))
    wider = pl.BlockSpec((TILE, MODEL + EXTRA), lambda i: (i, 0))
    whole = pl.BlockSpec((8, count, 192, 3 * FF_DEV), lambda i: (0, 0, 0, 0), pipeline_mode=pl.Buffered(1))
    flops = 2 * count * height * MODEL * (9 * FF_DEV + 5 * PAIR)
    return pl.pallas_call(
        functools.partial(moe_kernel, begin=begin, count=count, more=previous is not None),
        grid=(PLANE // TILE,),
        in_specs=[
            smem_spec(),
            pl.BlockSpec((TILE // PAIR, 8, PAIR), lambda i: (i, 0, 0)),
            pl.BlockSpec((EXPERTS, TILE), lambda i: (0, i)),
            pl.BlockSpec((EXPERTS, MODEL), lambda i: (0, 0)),
            whole,
        ]
        + [pl.BlockSpec(memory_space=pl.ANY)] * 8
        + ([wide, wider] if previous is not None else []),
        out_specs=[wide, wider, pl.BlockSpec((8, count, 192, 3 * FF_DEV), lambda i: (0, 0, 0, 0))],
        out_shape=[
            jax.ShapeDtypeStruct((PLANE, MODEL), BF16),
            jax.ShapeDtypeStruct((PLANE, MODEL + EXTRA), BF16),
            jax.ShapeDtypeStruct((8, count, 192, 3 * FF_DEV), BF16),
        ],
        scratch_shapes=[
            pltpu.VMEM((count, height, MODEL), BF16),
            pltpu.VMEM((count, height, MODEL), BF16),
            pltpu.VMEM((count, height, FF_DEV), BF16),
            pltpu.VMEM((count, height, 2 * FF_DEV), BF16),
            pltpu.VMEM((2, 2, TILE, MODEL), BF16),
            pltpu.SemaphoreType.DMA((2, 2)),
        ],
        compiler_params=pltpu.CompilerParams(vmem_limit_bytes=VMEM_LIMIT),
        cost_estimate=pl.CostEstimate(
            flops=flops, bytes_accessed=50 * 10**6, transcendentals=count * height * FF_DEV
        ),
        name="moe",
    )(first, rank, bias, router_t, weights, *rows, *cots, *(previous or ()))


def slot_tables(routes_all, col):
    ids = jnp.remainder(routes_all - EXPERTS_DEV * col, EXPERTS)
    hits = jnp.any(ids[None] == jnp.arange(EXPERTS, dtype=jnp.int32)[:, None, None], axis=-1)
    bias = jnp.where(hits, 0.0, NEG_FILL).astype(F32)
    local = hits[:EXPERTS_DEV].reshape(EXPERTS_DEV, PLANE // PAIR, PAIR)
    upto = jnp.arange(PAIR)[:, None] <= jnp.arange(PAIR)[None, :]
    counts = jnp.einsum(
        "epi,ij->pej", local.astype(BF16), upto.astype(BF16), preferred_element_type=F32
    ).astype(jnp.int32)
    rank = jnp.where(local.transpose(1, 0, 2), counts - 1, -1)
    rank = jnp.pad(rank, ((0, 0), (0, 8 - EXPERTS_DEV), (0, 0)), constant_values=-1)
    return bias, rank


def across_col(value, distance):
    pairs = [(2 * x + c, 2 * ((x + distance) % 4) + c) for x in range(4) for c in range(2)]
    return lax.ppermute(value, "col", pairs)


def other_core(value):
    return lax.ppermute(value, "col", [(s, s ^ 1) for s in range(8)])


def other_row(value):
    return lax.ppermute(value, "row", [(0, 1), (1, 0)])


def along_z(value, distance):
    pairs = [(4 * y + z, 4 * y + (z + distance) % 4) for y in range(2) for z in range(4)]
    return lax.ppermute(value, "dp", pairs)


def other_y(value):
    return lax.ppermute(value, "dp", [(s, s ^ 4) for s in range(8)])


def total(values):
    result = values[0].astype(F32)
    for value in values[1:]:
        result = result + value.astype(F32)
    return result


def gather_col(value):
    near = [value] + [across_col(value, d) for d in (1, 2, 3)]
    return near + [other_core(v) for v in near]


def gather_plane(value):
    near = []
    for mine in (value, other_row(value)):
        near.append(jnp.concatenate([mine] + [across_col(mine, d) for d in (1, 2, 3)], axis=0))
    return near + [other_core(v) for v in near]


def scatter_blocks(near, far):
    blocks = [
        total([near[d * ROWS : (d + 1) * ROWS], far[d * ROWS : (d + 1) * ROWS]]) for d in range(4)
    ]
    return [blocks[0]] + [across_col(blocks[d].astype(BF16), -d) for d in (1, 2, 3)]


def scatter_col(near, far):
    return total(scatter_blocks(near, other_core(far)))


def scatter_plane(value):
    half = value.shape[0] // 2
    quarter = half // 2
    far = other_core(value[half:])
    theirs = total(scatter_blocks(value[quarter:half], far[quarter:]))
    mine = total(scatter_blocks(value[:quarter], far[:quarter]))
    return mine + other_row(theirs.astype(BF16)).astype(F32)


def gather_dp(value):
    both = jnp.stack([value, other_y(value)])
    return [both] + [along_z(both, d) for d in (1, 2, 3)]


def scatter_dp(values):
    both = total([values[0]] + [along_z(values[d], -d) for d in (1, 2, 3)])
    mine = (both[0] + other_y(both[1].astype(BF16)).astype(F32)).astype(BF16)
    return total([mine, other_row(mine)])


def sum_all(value):
    value = value + other_core(value)
    value = value + across_col(value, 2)
    value = value + lax.ppermute(value, "col", [(s, s ^ 2) for s in range(8)])
    value = value + other_row(value)
    value = value + other_y(value)
    value = value + along_z(value, 2)
    return value + lax.ppermute(value, "dp", [(s, s ^ 1) for s in range(8)])


def per_device(
    tokens,
    cotangent,
    lengths,
    routes,
    norm_gains,
    gain_first,
    gain_second,
    router_w,
    router_first,
    router_second,
    projection_weight,
    projection_first_moment,
    projection_second_moment,
    w_proj,
    proj_first,
    proj_second,
    w_gate_up,
    gate_up_first,
    gate_up_second,
    w_down,
    down_first,
    down_second,
):
    col, row, dp = lax.axis_index("col"), lax.axis_index("row"), lax.axis_index("dp")
    across, core = col // 2, col % 2
    attn_w = jnp.concatenate([projection_weight[:, 0, :], w_proj.T], axis=1).astype(BF16)
    attn_pieces = gather_dp(attn_w)
    expert_w = jnp.concatenate(
        [w_gate_up.reshape(EXPERTS_DEV, 192, 2 * FF_DEV), w_down.transpose(0, 2, 1)], axis=2
    ).astype(BF16)
    expert_ws = [
        lax.all_gather(expert_w[b : b + n], "dp", axis=0, tiled=False) for b, n in CHUNKS
    ]

    residual_in = tokens.astype(F32)
    inverse_one = inv_rms(residual_in)
    normed_one = (residual_in * inverse_one * norm_gains[0]).astype(BF16)
    normed_pieces = gather_col(normed_one)
    steps = jnp.arange(4, dtype=jnp.int32)
    away = 2 * jnp.remainder(across - steps, 4)
    order = jnp.concatenate([away + core, away + 1 - core])
    spread = (
        jnp.remainder(dp % 4 - steps, 4)[:, None]
        + 4 * jnp.stack([dp // 4, 1 - dp // 4]).astype(jnp.int32)[None, :]
    ).reshape(-1)
    token_places = jnp.arange(GROUP, dtype=jnp.int32)
    doc_ends = jnp.cumsum(lengths[0])
    documents = jnp.sum((token_places[:, None] >= doc_ends[None, :]).astype(jnp.int32), axis=1)
    doc_row, doc_col = documents[None, :], documents[:, None]
    normed_full, attn_full, qkv, att, lse, *attn_parts = attend(
        order, spread, doc_row, doc_col, normed_pieces, attn_pieces
    )
    attn_out = scatter_col(*attn_parts)

    cot_ready, _ = lax.optimization_barrier((cotangent, normed_pieces))
    cots = gather_plane(cot_ready)
    routes_all = lax.all_gather(routes, ("row", "col"), axis=0, tiled=False)
    plane = jnp.stack([row * 8, (1 - row) * 8])[None, :, None] + order.reshape(2, 1, 4)
    routes_all = routes_all[plane.reshape(-1)].reshape(PLANE, -1)

    residual = residual_in + attn_out
    inverse_two = inv_rms(residual)
    normed_two = (residual * inverse_two * norm_gains[1]).astype(BF16)
    rows_all = gather_plane(normed_two)
    router_low = router_w.astype(BF16)
    bias, rank = slot_tables(routes_all, col)
    router_t = jnp.roll(router_low.T, -EXPERTS_DEV * col, axis=0)
    first = (EXPERTS_DEV * col).astype(jnp.int32).reshape(1)
    previous = None
    expert_grads = []
    for chunk, weights in zip(CHUNKS, expert_ws):
        *previous, grads = moe(chunk, first, rank, bias, router_t, weights, rows_all, cots, previous)
        expert_grads.append(grads)
    mix_part, dn_part = previous
    dn = scatter_plane(dn_part)
    mix_part, _ = lax.optimization_barrier((mix_part, dn))
    mixture = scatter_plane(mix_part)
    expert_sums = [
        lax.psum_scatter(g, "dp", scatter_dimension=0, tiled=False) for g in expert_grads
    ]
    output = (residual + mixture).astype(BF16)

    logits = jnp.dot(normed_two, router_low, preferred_element_type=F32)
    route_hits = jnp.any(
        routes[:, None, :] == jnp.arange(EXPERTS, dtype=jnp.int32)[None, :, None], axis=-1
    )
    gates = jax.nn.softmax(jnp.where(route_hits, logits, NEG_FILL), axis=-1)
    dgate = dn[:, MODEL : MODEL + EXPERTS] + dn[:, MODEL + EXPERTS : MODEL + 2 * EXPERTS]
    dlogits = gates * (dgate - jnp.sum(gates * dgate, axis=-1, keepdims=True))
    dnormed_two = dn[:, :MODEL] + jnp.dot(dlogits, router_low.astype(F32).T, precision=EXACT_MATH)
    grad_router = lax.dot_general(
        dlogits, normed_two.astype(F32), (((0,), (0,)), ((), ())), precision=EXACT_MATH
    )
    upstream = cotangent.astype(F32)
    dresid_norm, grad_gain_two = norm_back(residual, inverse_two, norm_gains[1], dnormed_two)
    dresidual = upstream + dresid_norm
    dattn_pieces = gather_col(dresidual.astype(BF16))
    near, far, *attn_grads, grad_gain_one = attend_back(
        order,
        spread,
        doc_row,
        doc_col,
        norm_gains[:1],
        attn_full,
        normed_full,
        qkv,
        att,
        lse,
        dattn_pieces,
    )
    dnormed = scatter_col(near, far)
    dtokens_norm, _ = norm_back(residual_in, inverse_one, norm_gains[0], dnormed)
    dtokens = dresidual + dtokens_norm
    attn_sums = scatter_dp(attn_grads)
    early = sum_all(jnp.concatenate([grad_router, grad_gain_two[None]], axis=0))
    sum_router = early[:EXPERTS].T
    sum_gains = jnp.concatenate([sum_all(grad_gain_one), early[EXPERTS:]], axis=0)
    sum_qkv = attn_sums[:, None, :QKV]
    sum_proj = attn_sums[:, QKV:].T
    expert_sum = jnp.concatenate(expert_sums, axis=0).astype(F32)
    sum_gate_up = expert_sum[:, :, : 2 * FF_DEV].reshape(EXPERTS_DEV, 192, 2, FF_DEV)
    sum_down = expert_sum[:, :, 2 * FF_DEV :].transpose(0, 2, 1)
    return (
        output,
        dtokens,
        *adamw(norm_gains, sum_gains, gain_first, gain_second, RATE_GAIN, 0.0),
        *adamw(router_w, sum_router, router_first, router_second, RATE_ROUTER, DECAY_RATE),
        *adamw(
            projection_weight,
            sum_qkv,
            projection_first_moment,
            projection_second_moment,
            RATE_NARROW,
            DECAY_RATE,
        ),
        *adamw(w_proj, sum_proj, proj_first, proj_second, RATE_WIDE, DECAY_RATE),
        *adamw(w_gate_up, sum_gate_up, gate_up_first, gate_up_second, RATE_NARROW, DECAY_RATE),
        *adamw(w_down, sum_down, down_first, down_second, RATE_WIDE, DECAY_RATE),
    )


def solution(mesh):
    by_token = P(("dp", "row", "col"), None)
    qkv_at, proj_at = P("dp", "col", None), P("col", "dp")
    gate_up_at, down_at = P("col", "dp", None, "row"), P("col", "row", "dp")
    return jax.shard_map(
        per_device,
        mesh=mesh,
        in_specs=(by_token, by_token, P(("dp", "row"), None), by_token)
        + (P(),) * 6
        + (qkv_at,) * 3
        + (proj_at,) * 3
        + (gate_up_at,) * 3
        + (down_at,) * 3,
        out_specs=(by_token, by_token)
        + (P(),) * 6
        + (qkv_at,) * 3
        + (proj_at,) * 3
        + (gate_up_at,) * 3
        + (down_at,) * 3,
        check_vma=False,
    )
```

time: 1700 us -> 607 us (0.36)
  blocking collectives: 582 us -> 21 us
  waiting for transfers between devices: 595 us -> 241 us
  local copies, waits for them, and re-layouts: 301 us -> 40.1 us
  Pallas kernels: 0 us -> 126 us
  matrix products: 123 us -> 1.71 us
  starting transfers between devices: 2.73 us -> 105 us
  other arithmetic: 69.4 us -> 49.5 us
    all_to_all x4 -> x0, blocking collectives: 455 us -> none  [the longest x2 289 us: from_experts(): lax.all_to_all(shaped.astype(jnp.bfloat16), 'col', split_axis=2, concat_a...]
    reduce_scatter x6 -> x3, waiting for transfers between devices: 270 us -> 0.01 us  [per_device(): lax.psum_scatter(g, 'dp', scatter_dimension=0, tiled=False)]
    all_gather x6 -> x3, waiting for transfers between devices: 257 us -> 0.04 us  [per_device(): lax.all_gather(expert_w[b:b + n], 'dp', axis=0, tiled=False)]
    ppermute x0 -> x79, waiting for transfers between devices: none -> 241 us  [the longest x38 142 us: across_col(): return lax.ppermute(value, 'col', pairs)]
    convert_element_type x4 -> x1, local copies, waits for them, and re-layouts: 130 us -> 0.7 us  [scatter_dp(): mine = (both[0] + other_y(both[1].astype(BF16)).astype(F32)).astype(BF16)]
    pallas_call x0 -> x5, Pallas kernels: none -> 126 us  [the longest x3 90.5 us: moe(): pl.pallas_call(functools.partial(moe_kernel, begin=begin, count=count, mo...]
    dot_general x29 -> x4, matrix products: 123 us -> 1.71 us  [the longest x1 0.79 us: per_device(): jnp.dot(dlogits, router_low.astype(F32).T, precision=EXACT_MATH)]
    ppermute x0 -> x79, starting transfers between devices: none -> 104 us  [the longest x38 50 us: across_col(): return lax.ppermute(value, 'col', pairs)]
  transfers between devices with their start and end apart: 16 -> 85, of which waited for: 11 -> 40; matrix products, arithmetic and copies ran while one was open for 17% -> 13% of each run, Pallas kernels for 0% -> 21%
where the time goes in v1:
time: 607 us; the launch traced here: 599 us
  waiting for transfers between devices  241 us (40%)
  Pallas kernels  126 us (21%)
  starting transfers between devices  105 us (17%)
  other arithmetic  49.5 us (8%)
  local copies, waits for them, and re-layouts  40.1 us (7%)
  blocking collectives  21 us (3%)
  between operations  15.5 us (3%)
    ppermute x38, waiting for transfers between devices, across_col(): return lax.ppermute(value, 'col', pairs)  142 us
    pallas_call x3, Pallas kernels, moe(): pl.pallas_call(functools.partial(moe_kernel, begin=begin, count=count, mo...  90.5 us
    ppermute x38, starting transfers between devices, across_col(): return lax.ppermute(value, 'col', pairs)  50 us
    ppermute x8, waiting for transfers between devices, along_z(): return lax.ppermute(value, 'dp', pairs)  45.6 us
    ppermute x8, starting transfers between devices, along_z(): return lax.ppermute(value, 'dp', pairs)  35.1 us
    ppermute x7, waiting for transfers between devices, other_row(): return lax.ppermute(value, 'row', [(0, 1), (1, 0)])  26 us
    unnamed x145, local copies, waits for them, and re-layouts  23.2 us
    all_gather x1, blocking collectives, per_device(): routes_all = lax.all_gather(routes, ('row', 'col'), axis=0, tiled=False)  21 us
  transfers between devices with their start and end apart: 85, of which 40 were waited for; matrix products, arithmetic and copies ran while one was open for 13% of the time, Pallas kernels for 21%

profile of v1, /device:TPU:32, one launch (start us, length us, event | category | flops | bytes accessed | tf_op | source)
XLA Modules:
  0.0 599.3 jit_solution(1575891081258316681)
XLA Ops:
  38.7 8.5 %collective-permute-done.10.refs_11_ = bf16[2,192,512]{2,1,0:T(8,128)(2,1)} collective-permute-done((bf16[2,192,512]{2,1,0:T(8,128)(2,1)S(1)}, bf16[2,192,512]{2,1,0:T(8,128)(2,1)}, u32[]{:S(2)}, u32[]{:S(2)}) %collective-permute-start.10) | collective-permute-done | bytes 393248 | tf_op jit(solution)/shard_map/ppermute | solution.py:448
  54.1 12.6 %collective-permute-done.9.refs_10_ = bf16[2,192,512]{2,1,0:T(8,128)(2,1)S(1)} collective-permute-done((bf16[2,192,512]{2,1,0:T(8,128)(2,1)S(1)}, bf16[2,192,512]{2,1,0:T(8,128)(2,1)S(1)}, u32[]{:S(2)}, u32[]{:S(2)}) %collective-permute-start.9) | collective-permute-done | bytes 393248 | tf_op jit(solution)/shard_map/ppermute | solution.py:448
  68.3 15.3 %attend.1 = (bf16[1024,1536]{1,0:T(8,128)(2,1)}, bf16[1536,512]{1,0:T(8,128)(2,1)}, bf16[1024,320]{1,0:T(8,128)(2,1)}, bf16[1024,256]{1,0:T(8,128)(2,1)}, f32[8,...) custom-call(s32[8]{0:T(128)} %pad_add_fusion.order_ref, s32[8]{0:T(128)} %add.471.spread_ref, ...), custom_call_target="tpu_custom_call" | custom-call | flops 4000000000 | bytes 12000000 | tf_op jit(solution)/shard_map/attend/pallas_call | solution.py:215
  83.8 21.0 %all-gather = s32[2048,8]{0,1:T(8,128)S(1)} all-gather(s32[128,8]{0,1:T(8,128)S(1)} %copy-done.32), channel_id=2, replica_groups=mesh['dp'=8,'row'=2,'col'=8] {'row','col'}, dimensions={0}, use_global_device_ids=true | all-gather | bytes 69632 | tf_op jit(solution)/shard_map/all_gather | solution.py:572
  120.6 9.7 %collective-permute-done.24 = bf16[128,1536]{1,0:T(8,128)(2,1)S(1)} collective-permute-done((bf16[128,1536]{1,0:T(8,128)(2,1)S(1)}, bf16[128,1536]{1,0:T(8,128)(2,1)S(1)}, u32[]{:S(2)}, u32[]{:S(2)}) %collective-permute-start.24) | collective-permute-done | bytes 393248 | tf_op jit(solution)/shard_map/ppermute | solution.py:435
  138.2 17.4 %collective-permute-done.28 = bf16[128,1536]{1,0:T(8,128)(2,1)S(1)} collective-permute-done((bf16[128,1536]{1,0:T(8,128)(2,1)}, bf16[128,1536]{1,0:T(8,128)(2,1)S(1)}, u32[]{:S(2)}, u32[]{:S(2)}) %collective-permute-start.28) | collective-permute-done | bytes 393248 | tf_op jit(solution)/shard_map/ppermute | solution.py:435
  156.4 6.8 %collective-permute-done.14 = bf16[128,1536]{1,0:T(8,128)(2,1)S(1)} collective-permute-done((bf16[128,1536]{1,0:T(8,128)(2,1)S(1)}, bf16[128,1536]{1,0:T(8,128)(2,1)S(1)}, u32[]{:S(2)}, u32[]{:S(2)}) %collective-permute-start.14) | collective-permute-done | bytes 393248 | tf_op jit(solution)/shard_map/ppermute | solution.py:435
  175.5 10.6 %collective-permute-done.15 = bf16[128,1536]{1,0:T(8,128)(2,1)S(1)} collective-permute-done((bf16[128,1536]{1,0:T(8,128)(2,1)S(1)}, bf16[128,1536]{1,0:T(8,128)(2,1)S(1)}, u32[]{:S(2)}, u32[]{:S(2)}) %collective-permute-start.15) | collective-permute-done | bytes 393248 | tf_op jit(solution)/shard_map/ppermute | solution.py:435
  189.3 14.2 %collective-permute-done.19 = bf16[128,1536]{1,0:T(8,128)(2,1)S(1)} collective-permute-done((bf16[128,1536]{1,0:T(8,128)(2,1)S(1)}, bf16[128,1536]{1,0:T(8,128)(2,1)S(1)}, u32[]{:S(2)}, u32[]{:S(2)}) %collective-permute-start.19) | collective-permute-done | bytes 393248 | tf_op jit(solution)/shard_map/ppermute | solution.py:435
  205.0 6.2 %collective-permute-done.21 = bf16[128,1536]{1,0:T(8,128)(2,1)S(1)} collective-permute-done((bf16[128,1536]{1,0:T(8,128)(2,1)S(1)}, bf16[128,1536]{1,0:T(8,128)(2,1)S(1)}, u32[]{:S(2)}, u32[]{:S(2)}) %collective-permute-start.21) | collective-permute-done | bytes 393248 | tf_op jit(solution)/shard_map/ppermute | solution.py:435
  215.8 22.3 %moe.3 = (bf16[2048,1536]{1,0:T(8,128)(2,1)}, bf16[2048,1664]{1,0:T(8,128)(2,1)}, bf16[8,1,192,768]{3,2,1,0:T(8,128)(2,1)}) custom-call(s32[1]{0:T(128)} %bitcast.11.first_ref, s32[8,8,256]{2,1,0:T(8,128)} %pad.4.rank_ref, f32[40,2048]{1,0:T(8,128)} %broadcast_select_fusion.bias_ref, bf16[40,1536]{1,0:T(8,128)(2,1)} %fusion.26.router_ref, ...), custom_call_target="tpu_custom_call" | custom-call | flops 9865003008 | bytes 50000000 | tf_op jit(solution)/shard_map/moe/pallas_call | solution.py:385
  238.4 33.8 %moe.4 = (bf16[2048,1536]{1,0:T(8,128)(2,1)}, bf16[2048,1664]{1,0:T(8,128)(2,1)}, bf16[8,2,192,768]{3,2,1,0:T(8,128)(2,1)}) custom-call(s32[1]{0:T(128)} %bitcast.11.first_ref, s32[8,8,256]{2,1,0:T(8,128)} %pad.4.rank_ref, f32[40,2048]{1,0:T(8,128)} %broadcast_select_fusion.bias_ref, bf16[40,1536]{1,0:T(8,128)(2,1)} %fusion.26.router_ref, ...), custom_call_target="tpu_custom_call" | custom-call | flops 19730006016 | bytes 50000000 | tf_op jit(solution)/shard_map/moe/pallas_call | solution.py:385
  272.3 34.4 %moe.5 = (bf16[2048,1536]{1,0:T(8,128)(2,1)}, bf16[2048,1664]{1,0:T(8,128)(2,1)}, bf16[8,2,192,768]{3,2,1,0:T(8,128)(2,1)}) custom-call(s32[1]{0:T(128)} %bitcast.11.first_ref, s32[8,8,256]{2,1,0:T(8,128)} %pad.4.rank_ref, f32[40,2048]{1,0:T(8,128)} %broadcast_select_fusion.bias_ref, bf16[40,1536]{1,0:T(8,128)(2,1)} %fusion.26.router_ref, ...), custom_call_target="tpu_custom_call" | custom-call | flops 19730006016 | bytes 50000000 | tf_op jit(solution)/shard_map/moe/pallas_call | solution.py:385
  326.3 12.9 %collective-permute-done.37 = bf16[128,1664]{1,0:T(8,128)(2,1)S(1)} collective-permute-done((bf16[128,1664]{1,0:T(8,128)(2,1)S(1)}, bf16[128,1664]{1,0:T(8,128)(2,1)S(1)}, u32[]{:S(2)}, u32[]{:S(2)}) %collective-permute-start.37) | collective-permute-done | bytes 426016 | tf_op jit(solution)/shard_map/ppermute | solution.py:435
  353.3 8.0 %collective-permute-done.36 = bf16[128,1664]{1,0:T(8,128)(2,1)} collective-permute-done((bf16[128,1664]{1,0:T(8,128)(2,1)}, bf16[128,1664]{1,0:T(8,128)(2,1)}, u32[]{:S(2)}, u32[]{:S(2)}) %collective-permute-start.36) | collective-permute-done | bytes 426016 | tf_op jit(solution)/shard_map/ppermute | solution.py:435
  377.5 6.6 %collective-permute-done.45 = bf16[128,1536]{1,0:T(8,128)(2,1)S(1)} collective-permute-done((bf16[128,1536]{1,0:T(8,128)(2,1)S(1)}, bf16[128,1536]{1,0:T(8,128)(2,1)S(1)}, u32[]{:S(2)}, u32[]{:S(2)}) %collective-permute-start.45) | collective-permute-done | bytes 393248 | tf_op jit(solution)/shard_map/ppermute | solution.py:435
  386.4 6.0 %collective-permute-start.44 = (bf16[128,1536]{1,0:T(8,128)(2,1)S(1)}, bf16[128,1536]{1,0:T(8,128)(2,1)S(1)}, u32[]{:S(2)}, u32[]{:S(2)}) collective-permute-start(bf16[128,1536]{1,0:T(8,128)(2,1)S(1)} %get-tuple-element.204), channel_id=1, source_target_pairs={{0,2},{1,3},{2,4},{3,5},{4,6},{5,7},{6,0},{7,1},{8,10},{9,11},{10,... | collective-permute-start | bytes 1179656 | tf_op jit(solution)/shard_map/ppermute | solution.py:435
  398.0 18.9 %collective-permute-done.68 = f32[41,1536]{1,0:T(8,128)S(1)} collective-permute-done((f32[41,1536]{1,0:T(8,128)S(1)}, f32[41,1536]{1,0:T(8,128)S(1)}, u32[]{:S(2)}, u32[]{:S(2)}) %collective-permute-start.68) | collective-permute-done | bytes 251936 | tf_op jit(solution)/shard_map/ppermute | solution.py:435
  428.0 8.1 %collective-permute-done.70 = f32[41,1536]{1,0:T(8,128)S(1)} collective-permute-done((f32[41,1536]{1,0:T(8,128)S(1)}, f32[41,1536]{1,0:T(8,128)S(1)}, u32[]{:S(2)}, u32[]{:S(2)}) %collective-permute-start.70) | collective-permute-done | bytes 251936 | tf_op jit(solution)/shard_map/ppermute | solution.py:443
  442.9 21.8 %collective-permute-start.72 = (f32[41,1536]{1,0:T(8,128)S(1)}, f32[41,1536]{1,0:T(8,128)S(1)}, u32[]{:S(2)}, u32[]{:S(2)}) collective-permute-start(f32[41,1536]{1,0:T(8,128)S(1)} %add.548), channel_id=1, source_target_pairs={{0,32},{16,48},{32,0},{48,16},{64,96},{80,112},{96,64},{112,80},{1... | collective-permute-start | bytes 755720 | tf_op jit(solution)/shard_map/ppermute | solution.py:448
  464.8 7.3 %collective-permute-done.72 = f32[41,1536]{1,0:T(8,128)S(1)} collective-permute-done((f32[41,1536]{1,0:T(8,128)S(1)}, f32[41,1536]{1,0:T(8,128)S(1)}, u32[]{:S(2)}, u32[]{:S(2)}) %collective-permute-start.72) | collective-permute-done | bytes 251936 | tf_op jit(solution)/shard_map/ppermute | solution.py:448
  474.4 20.0 %attend_back.1 = (bf16[512,1536]{1,0:T(8,128)(2,1)}, bf16[512,1536]{1,0:T(8,128)(2,1)}, bf16[2,192,512]{2,1,0:T(8,128)(2,1)}, bf16[2,192,512]{2,1,0:T(8,128)(2,1...) custom-call(s32[8]{0:T(128)} %pad_add_fusion.order_ref, s32[8]{0:T(128)} %add.471.spread_ref, ...), custom_call_target="tpu_custom_call" | custom-call | flops 8000000000 | bytes 16000000 | tf_op jit(solution)/shard_map/attend_back/pallas_call | solution.py:237
  529.4 9.5 %collective-permute-done.74 = bf16[2,192,512]{2,1,0:T(8,128)(2,1)S(1)} collective-permute-done((bf16[2,192,512]{2,1,0:T(8,128)(2,1)S(1)}, bf16[2,192,512]{2,1,0:T(8,128)(2,1)S(1)}, u32[]{:S(2)}, u32[]{:S(2)}) %collective-permute-start.74) | collective-permute-done | bytes 393248 | tf_op jit(solution)/shard_map/ppermute | solution.py:448
  549.8 9.8 %multiply_subtract_fusion = (f32[5,192,2,256]{3,2,1,0:T(2,128)}, f32[5,192,2,256]{3,2,1,0:T(2,128)}, f32[5,192,2,256]{3,2,1,0:T(2,128)}) fusion(f32[5,192,2,256]{3,2,1,0:T(2,128)S(1)} %copy-done.1, f32[5,192,2,256]{3,2,1,0:T(2,128)} %reshape.286, f32[5,192,2,256]{3,2,1,0:T(2,128)} %param.39, f32[5,192,2,256]{3,2,1,0:T(2,128)} %param.40), kind=kLoop, calls=%fused_computation.5 | loop fusion | flops 7372800 | bytes 13762560 | tf_op jit(solution)/shard_map/sub | solution.py:57
  (400 shorter events, 242.2 us)
Async XLA Ops:
  7.2 207.2 %all-gather.12.cloned.1.call-start = ((), (), s32[]{:S(2)}) async-start(), calls=%async_computation.8 | async-start | bytes 2654208 | tf_op jit(solution)/shard_map/all_gather | solution.py:547
  11.5 226.9 %all-gather.10.cloned.1.call-start = ((), (), s32[]{:S(2)}) async-start(), calls=%async_computation.7 | async-start | bytes 5308416 | tf_op jit(solution)/shard_map/all_gather | solution.py:547
  12.7 259.6 %all-gather.8.cloned.1.call-start = ((), (), s32[]{:S(2)}) async-start(), calls=%async_computation.6 | async-start | bytes 5308416 | tf_op jit(solution)/shard_map/all_gather | solution.py:547
  21.4 521.7 %reduce-scatter.4.cloned.1.call-start = ((), (), s32[]{:S(2)}) async-start(), calls=%async_computation.3 | async-start | bytes 2654208 | tf_op jit(solution)/shard_map/reduce_scatter | solution.py:594
  35.2 31.4 %collective-permute-start.9 = (bf16[2,192,512]{2,1,0:T(8,128)(2,1)S(1)}, bf16[2,192,512]{2,1,0:T(8,128)(2,1)S(1)}, u32[]{:S(2)}, u32[]{:S(2)}) collective-permute-start(bf16[2,192,512]{2,1,0:T(8,128)(2,1)S(1)} %pad_maximum_fusion.2.refs_8_), channel_id=1, source_target_pairs={{0,32},{16,48},{32,0},{48,16},{64,96},{80,112},{96,64},{112,80},{1... | collective-permute-start | bytes 1179656 | tf_op jit(solution)/shard_map/ppermute | solution.py:448
  83.7 48.4 %collective-permute-start.11 = (bf16[512,1536]{1,0:T(8,128)(2,1)}, bf16[512,1536]{1,0:T(8,128)(2,1)S(1)}, u32[]{:S(2)}, u32[]{:S(2)}) collective-permute-start(bf16[512,1536]{1,0:T(8,128)(2,1)} %get-tuple-element.46), channel_id=1, source_target_pairs={{0,1},{1,0},{2,3},{3,2},{4,5},{5,4},{6,7},{7,6},{8,9},{9,8},{10,11... | collective-permute-start | bytes 4718600 | tf_op jit(solution)/shard_map/ppermute | solution.py:439
  118.4 37.2 %collective-permute-start.28 = (bf16[128,1536]{1,0:T(8,128)(2,1)}, bf16[128,1536]{1,0:T(8,128)(2,1)S(1)}, u32[]{:S(2)}, u32[]{:S(2)}) collective-permute-start(bf16[128,1536]{1,0:T(8,128)(2,1)} %collective-permute-done.27), channel_id=1, source_target_pairs={{0,2},{1,3},{2,4},{3,5},{4,6},{5,7},{6,0},{7,1},{8,10},{9,11},{10,... | collective-permute-start | bytes 1179656 | tf_op jit(solution)/shard_map/ppermute | solution.py:435
  130.3 35.9 %collective-permute-start.29 = (bf16[128,1536]{1,0:T(8,128)(2,1)}, bf16[128,1536]{1,0:T(8,128)(2,1)S(1)}, u32[]{:S(2)}, u32[]{:S(2)}) collective-permute-start(bf16[128,1536]{1,0:T(8,128)(2,1)} %collective-permute-done.27), channel_id=1, source_target_pairs={{0,4},{1,5},{2,6},{3,7},{4,0},{5,1},{6,2},{7,3},{8,12},{9,13},{10,... | collective-permute-start | bytes 1179656 | tf_op jit(solution)/shard_map/ppermute | solution.py:435
  169.3 45.1 %collective-permute-start.31 = (bf16[512,1536]{1,0:T(8,128)(2,1)}, bf16[512,1536]{1,0:T(8,128)(2,1)}, u32[]{:S(2)}, u32[]{:S(2)}) collective-permute-start(bf16[512,1536]{1,0:T(8,128)(2,1)} %constant_dynamic-update-slice_fusion.4.refs_4_), channel_id=1, source_target_pairs={{0,1},{1,0},{2,3},{3,2},{4,5},{5,4},{6,7},{7,6},{8,9},{9,8},{10,11... | collective-permute-start | bytes 4718600 | tf_op jit(solution)/shard_map/ppermute | solution.py:439
  175.5 38.9 %collective-permute-start.32 = (bf16[512,1536]{1,0:T(8,128)(2,1)}, bf16[512,1536]{1,0:T(8,128)(2,1)}, u32[]{:S(2)}, u32[]{:S(2)}) collective-permute-start(bf16[512,1536]{1,0:T(8,128)(2,1)} %constant_dynamic-update-slice_fusion.8.refs_5_), channel_id=1, source_target_pairs={{0,1},{1,0},{2,3},{3,2},{4,5},{5,4},{6,7},{7,6},{8,9},{9,8},{10,11... | collective-permute-start | bytes 4718600 | tf_op jit(solution)/shard_map/ppermute | solution.py:439
  238.1 305.0 %reduce-scatter.8.cloned.1.call-start = ((), (), s32[]{:S(2)}) async-start(), calls=%async_computation.5 | async-start | bytes 5308416 | tf_op jit(solution)/shard_map/reduce_scatter | solution.py:594
  306.7 236.4 %reduce-scatter.6.cloned.1.call-start = ((), (), s32[]{:S(2)}) async-start(), calls=%async_computation.4 | async-start | bytes 5308416 | tf_op jit(solution)/shard_map/reduce_scatter | solution.py:594
  321.6 29.0 %collective-permute-start.34 = (bf16[128,1664]{1,0:T(8,128)(2,1)}, bf16[128,1664]{1,0:T(8,128)(2,1)}, u32[]{:S(2)}, u32[]{:S(2)}) collective-permute-start(bf16[128,1664]{1,0:T(8,128)(2,1)} %get-tuple-element.194), channel_id=1, source_target_pairs={{0,6},{1,7},{2,0},{3,1},{4,2},{5,3},{6,4},{7,5},{8,14},{9,15},{10,... | collective-permute-start | bytes 1277960 | tf_op jit(solution)/shard_map/ppermute | solution.py:435
  324.3 29.0 %collective-permute-start.35 = (bf16[128,1664]{1,0:T(8,128)(2,1)}, bf16[128,1664]{1,0:T(8,128)(2,1)}, u32[]{:S(2)}, u32[]{:S(2)}) collective-permute-start(bf16[128,1664]{1,0:T(8,128)(2,1)} %get-tuple-element.199), channel_id=1, source_target_pairs={{0,4},{1,5},{2,6},{3,7},{4,0},{5,1},{6,2},{7,3},{8,12},{9,13},{10,... | collective-permute-start | bytes 1277960 | tf_op jit(solution)/shard_map/ppermute | solution.py:435
  374.8 42.3 %collective-permute-start.42 = (bf16[128,1536]{1,0:T(8,128)(2,1)S(1)}, bf16[128,1536]{1,0:T(8,128)(2,1)S(1)}, u32[]{:S(2)}, u32[]{:S(2)}) collective-permute-start(bf16[128,1536]{1,0:T(8,128)(2,1)S(1)} %get-tuple-element.200), channel_id=1, source_target_pairs={{0,6},{1,7},{2,0},{3,1},{4,2},{5,3},{6,4},{7,5},{8,14},{9,15},{10,... | collective-permute-start | bytes 1179656 | tf_op jit(solution)/shard_map/ppermute | solution.py:435
  384.1 32.9 %collective-permute-start.43 = (bf16[128,1536]{1,0:T(8,128)(2,1)S(1)}, bf16[128,1536]{1,0:T(8,128)(2,1)S(1)}, u32[]{:S(2)}, u32[]{:S(2)}) collective-permute-start(bf16[128,1536]{1,0:T(8,128)(2,1)S(1)} %get-tuple-element.205), channel_id=1, source_target_pairs={{0,4},{1,5},{2,6},{3,7},{4,0},{5,1},{6,2},{7,3},{8,12},{9,13},{10,... | collective-permute-start | bytes 1179656 | tf_op jit(solution)/shard_map/ppermute | solution.py:435
  386.4 30.7 %collective-permute-start.44 = (bf16[128,1536]{1,0:T(8,128)(2,1)S(1)}, bf16[128,1536]{1,0:T(8,128)(2,1)S(1)}, u32[]{:S(2)}, u32[]{:S(2)}) collective-permute-start(bf16[128,1536]{1,0:T(8,128)(2,1)S(1)} %get-tuple-element.204), channel_id=1, source_target_pairs={{0,2},{1,3},{2,4},{3,5},{4,6},{5,7},{6,0},{7,1},{8,10},{9,11},{10,... | collective-permute-start | bytes 1179656 | tf_op jit(solution)/shard_map/ppermute | solution.py:435
  437.0 36.3 %collective-permute-start.52 = (bf16[128,1536]{1,0:T(8,128)(2,1)S(1)}, bf16[128,1536]{1,0:T(8,128)(2,1)S(1)}, u32[]{:S(2)}, u32[]{:S(2)}) collective-permute-start(bf16[128,1536]{1,0:T(8,128)(2,1)S(1)} %get-tuple-element.214.refs_0_), channel_id=1, source_target_pairs={{0,1},{1,0},{2,3},{3,2},{4,5},{5,4},{6,7},{7,6},{8,9},{9,8},{10,11... | collective-permute-start | bytes 1179656 | tf_op jit(solution)/shard_map/ppermute | solution.py:439
  437.0 36.3 %collective-permute-start.53 = (bf16[128,1536]{1,0:T(8,128)(2,1)S(1)}, bf16[128,1536]{1,0:T(8,128)(2,1)S(1)}, u32[]{:S(2)}, u32[]{:S(2)}) collective-permute-start(bf16[128,1536]{1,0:T(8,128)(2,1)S(1)} %collective-permute-done.49.refs_1_), channel_id=1, source_target_pairs={{0,1},{1,0},{2,3},{3,2},{4,5},{5,4},{6,7},{7,6},{8,9},{9,8},{10,11... | collective-permute-start | bytes 1179656 | tf_op jit(solution)/shard_map/ppermute | solution.py:439
  442.3 31.0 %collective-permute-start.54 = (bf16[128,1536]{1,0:T(8,128)(2,1)S(1)}, bf16[128,1536]{1,0:T(8,128)(2,1)S(1)}, u32[]{:S(2)}, u32[]{:S(2)}) collective-permute-start(bf16[128,1536]{1,0:T(8,128)(2,1)S(1)} %collective-permute-done.50.refs_2_), channel_id=1, source_target_pairs={{0,1},{1,0},{2,3},{3,2},{4,5},{5,4},{6,7},{7,6},{8,9},{9,8},{10,11... | collective-permute-start | bytes 1179656 | tf_op jit(solution)/shard_map/ppermute | solution.py:439
  442.3 31.0 %collective-permute-start.55 = (bf16[128,1536]{1,0:T(8,128)(2,1)S(1)}, bf16[128,1536]{1,0:T(8,128)(2,1)S(1)}, u32[]{:S(2)}, u32[]{:S(2)}) collective-permute-start(bf16[128,1536]{1,0:T(8,128)(2,1)S(1)} %collective-permute-done.51.refs_3_), channel_id=1, source_target_pairs={{0,1},{1,0},{2,3},{3,2},{4,5},{5,4},{6,7},{7,6},{8,9},{9,8},{10,11... | collective-permute-start | bytes 1179656 | tf_op jit(solution)/shard_map/ppermute | solution.py:439
  442.9 29.1 %collective-permute-start.72 = (f32[41,1536]{1,0:T(8,128)S(1)}, f32[41,1536]{1,0:T(8,128)S(1)}, u32[]{:S(2)}, u32[]{:S(2)}) collective-permute-start(f32[41,1536]{1,0:T(8,128)S(1)} %add.548), channel_id=1, source_target_pairs={{0,32},{16,48},{32,0},{48,16},{64,96},{80,112},{96,64},{112,80},{1... | collective-permute-start | bytes 755720 | tf_op jit(solution)/shard_map/ppermute | solution.py:448
  472.1 47.3 %collective-permute-start.73 = (f32[41,1536]{1,0:T(8,128)S(1)}, f32[41,1536]{1,0:T(8,128)S(1)}, u32[]{:S(2)}, u32[]{:S(2)}) collective-permute-start(f32[41,1536]{1,0:T(8,128)S(1)} %add.549), channel_id=1, source_target_pairs={{0,16},{16,0},{32,48},{48,32},{64,80},{80,64},{96,112},{112,96},{1... | collective-permute-start | bytes 755720 | tf_op jit(solution)/shard_map/ppermute | solution.py:512
  528.7 39.3 %collective-permute-start.56 = (bf16[512,1536]{1,0:T(8,128)(2,1)}, bf16[512,1536]{1,0:T(8,128)(2,1)}, u32[]{:S(2)}, u32[]{:S(2)}) collective-permute-start(bf16[512,1536]{1,0:T(8,128)(2,1)} %get-tuple-element.61), channel_id=1, source_target_pairs={{0,1},{1,0},{2,3},{3,2},{4,5},{5,4},{6,7},{7,6},{8,9},{9,8},{10,11... | collective-permute-start | bytes 4718600 | tf_op jit(solution)/shard_map/ppermute | solution.py:439
  (124 other events, 2143.8 us)
Sparse Core Ops, SparseCore 0:
  11.6 56.1 all-gather.11
  70.0 58.3 all-gather.9
  130.7 67.9 all-gather.7
  238.2 49.7 reduce-scatter.3
  306.8 68.2 reduce-scatter.7
  377.4 70.1 reduce-scatter.5

commit v2 on v1

--- a/solution.py
+++ b/solution.py
@@ -20,12 +20,14 @@
 FF_DEV = 256
 EXPERTS = 40
 EXPERTS_DEV = 5
+TOP = 8
 SLOTS = 112
 TILE = 512
 PAIR = 256
 QUERY_TILE = 256
 EXTRA = 128
-CHUNKS = ((0, 1), (1, 2), (3, 2))
+SMALL = 48
+CHUNKS = ((0, 3), (3, 2))
 
 EXACT_MATH = lax.Precision.HIGHEST
 NORM_EPS = 1e-05
@@ -44,6 +46,54 @@
 VMEM_LIMIT = 60 * 1024 * 1024
 
 
+def row_pairs(stored):
+    parts = stored.reshape(EXPERTS_DEV, STORED, 2, FF_DEV // 128, 128)
+    return parts.transpose(0, 1, 3, 2, 4).reshape(-1, 128)
+
+
+def paired_rows(rows):
+    parts = rows.reshape(EXPERTS_DEV, STORED, FF_DEV // 128, 2, 128)
+    return parts.transpose(0, 1, 3, 2, 4).reshape(EXPERTS_DEV, STORED, 2, FF_DEV)
+
+
+def adamw_kernel(g_ref, *refs):
+    olds, news = refs[:6], refs[6:]
+    for half in range(FF_DEV // 128):
+        for kind in range(2):
+            at = pl.ds(2 * half + kind, STORED, stride=4)
+            start = kind * FF_DEV + half * 128
+            gradient = g_ref[0, :, start : start + 128].astype(F32)
+            weight, first, second = (ref[at, :] for ref in olds[:3])
+            results = adamw(weight, gradient, first, second, RATE_NARROW, DECAY_RATE)
+            for ref, result in zip(news[:3], results):
+                ref[at, :] = result
+    gradient = g_ref[0, :, 2 * FF_DEV :].astype(F32)
+    weight, first, second = (ref[0] for ref in olds[3:])
+    results = adamw(weight, gradient, first, second, RATE_WIDE, DECAY_RATE)
+    for ref, result in zip(news[3:], results):
+        ref[0] = result
+
+
+def update_experts(gradient, gate_up, down):
+    pair_rows = pl.BlockSpec((4 * STORED, 128), lambda i: (i, 0))
+    down_rows = pl.BlockSpec((1, STORED, FF_DEV), lambda i: (i, 0, 0))
+    specs = [pair_rows] * 3 + [down_rows] * 3
+    pair_shape = jax.ShapeDtypeStruct((EXPERTS_DEV * 4 * STORED, 128), F32)
+    down_shape = jax.ShapeDtypeStruct((EXPERTS_DEV, STORED, FF_DEV), F32)
+    new = pl.pallas_call(
+        adamw_kernel,
+        grid=(EXPERTS_DEV,),
+        in_specs=[pl.BlockSpec((1, STORED, 3 * FF_DEV), lambda i: (i, 0, 0))] + specs,
+        out_specs=specs,
+        out_shape=[pair_shape] * 3 + [down_shape] * 3,
+        cost_estimate=pl.CostEstimate(
+            flops=20 * 10**6, bytes_accessed=20 * 10**6, transcendentals=10**6
+        ),
+        name="update_experts",
+    )(gradient, *[row_pairs(v) for v in gate_up], *[v.transpose(0, 2, 1) for v in down])
+    return [paired_rows(v) for v in new[:3]] + [v.transpose(0, 2, 1) for v in new[3:]]
+
+
 def inv_rms(values):
     return lax.rsqrt(jnp.mean(values * values, axis=-1, keepdims=True) + NORM_EPS)
 
@@ -103,14 +153,11 @@
     return same & (key_at <= query_at)
 
 
-def attend_kernel(order_ref, spread_ref, doc_row_ref, doc_col_ref, *refs):
-    normed_ref, w_ref, qkv_ref, att_ref, lse_ref, near_ref, far_ref = refs[-7:]
-    pieces, weights = refs[:8], refs[8:-7]
+def attend_kernel(order_ref, doc_row_ref, doc_col_ref, *refs):
+    normed_ref, qkv_ref, att_ref, lse_ref, near_ref, far_ref = refs[-6:]
+    pieces, w_ref = refs[:8], refs[8]
     for block, (ref, start) in enumerate(row_blocks(pieces)):
         normed_ref[place(order_ref, block), :] = ref[start : start + ROWS, :]
-    for block, ref in enumerate(weights):
-        for other in range(2):
-            w_ref[stored_rows(spread_ref, 2 * block + other), :] = ref[other]
     for tile in range(GROUP // QUERY_TILE):
         rows = slice(tile * QUERY_TILE, (tile + 1) * QUERY_TILE)
         qkv_ref[rows, :] = dot(normed_ref[rows, :], w_ref[...])[:, :QKV].astype(BF16)
@@ -146,6 +193,7 @@
     doc_row_ref,
     doc_col_ref,
     gain_ref,
+    small_ref,
     w_ref,
     normed_ref,
     qkv_ref,
@@ -154,8 +202,8 @@
     *refs,
 ):
     pieces, refs = refs[:8], refs[8:]
-    near_ref, far_ref, *grads_refs, dgain_ref = refs[:7]
-    dattn_ref, datt_ref, dqkv_ref, dkv_ref, whole_ref = refs[7:]
+    near_ref, far_ref, *grads_refs = refs[:4]
+    dattn_ref, datt_ref, dqkv_ref, dkv_ref, whole_ref = refs[4:]
     for block, (ref, start) in enumerate(row_blocks(pieces)):
         dattn_ref[place(order_ref, block), :] = ref[start : start + ROWS, :]
     proj = w_ref[:, SPAN + HEAD_SIZE :]
@@ -193,14 +241,17 @@
         dgain = dgain + jnp.sum(part * normed_ref[at, :].astype(F32), axis=0, keepdims=True)
         part_ref = near_ref if block < 4 else far_ref
         part_ref[block % 4 * ROWS : (block % 4 + 1) * ROWS, :] = part.astype(BF16)
-    dgain_ref[...] = dgain / gain_ref[...]
+    small_at = lax.broadcasted_iota(jnp.int32, (SMALL, MODEL), 0)
+    small = jnp.where(small_at == EXPERTS + 1, dgain / gain_ref[...], small_ref[...])
+    far_ref[GROUP // 2 :, :] = small.astype(BF16)
     for start in range(0, MODEL, PAIR):
         cols = slice(start, start + PAIR)
         qkv_part = dot_tn(dqkv_ref[...], normed_ref[:, cols])
         proj_part = dot_tn(att_ref[...], dattn_ref[:, cols])[HEAD_SIZE:]
-        whole_ref[cols, :] = jnp.concatenate([qkv_part, proj_part], axis=0).T.astype(BF16)
+        both = jnp.concatenate([qkv_part, proj_part], axis=0)
+        whole_ref[cols, :] = both.T.astype(BF16)
     for block in range(8):
-        grads_refs[block // 2][block % 2] = whole_ref[stored_rows(spread_ref, block), :]
+        grads_refs[block // 4][block % 4] = whole_ref[stored_rows(spread_ref, block), :]
 
 
 def vmem_spec():
@@ -211,14 +262,13 @@
     return pl.BlockSpec(memory_space=pltpu.SMEM)
 
 
-def attend(order, spread, doc_row, doc_col, pieces, weights):
+def attend(order, doc_row, doc_col, pieces, weights):
     return pl.pallas_call(
         attend_kernel,
-        in_specs=[smem_spec()] * 2 + [vmem_spec()] * (2 + len(pieces) + len(weights)),
-        out_specs=[vmem_spec()] * 7,
+        in_specs=[smem_spec()] + [vmem_spec()] * (3 + len(pieces)),
+        out_specs=[vmem_spec()] * 6,
         out_shape=[
             jax.ShapeDtypeStruct((GROUP, MODEL), BF16),
-            jax.ShapeDtypeStruct((MODEL, 2 * PAIR), BF16),
             jax.ShapeDtypeStruct((GROUP, QKV), BF16),
             jax.ShapeDtypeStruct((GROUP, PAIR), BF16),
             jax.ShapeDtypeStruct((8, GROUP), F32),
@@ -227,25 +277,22 @@
         ],
         compiler_params=pltpu.CompilerParams(vmem_limit_bytes=VMEM_LIMIT),
         cost_estimate=pl.CostEstimate(
-            flops=4 * 10**9, bytes_accessed=12 * 10**6, transcendentals=2 * 10**6
+            flops=10**6, bytes_accessed=10**5, transcendentals=0
         ),
         name="attend",
-    )(order, spread, doc_row, doc_col, *pieces, *weights)
-
-
-def attend_back(order, spread, doc_row, doc_col, gain, weights, normed, qkv, att, lse, pieces):
+    )(order, doc_row, doc_col, *pieces, weights)
+
+
+def attend_back(order, spread, doc_row, doc_col, gain, small, weights, normed, qkv, att, lse, pieces):
     return pl.pallas_call(
         attend_back_kernel,
-        in_specs=[smem_spec()] * 2 + [vmem_spec()] * (8 + len(pieces)),
-        out_specs=[vmem_spec()] * 7,
+        in_specs=[smem_spec()] * 2 + [vmem_spec()] * (9 + len(pieces)),
+        out_specs=[vmem_spec()] * 4,
         out_shape=[
             jax.ShapeDtypeStruct((GROUP // 2, MODEL), BF16),
-            jax.ShapeDtypeStruct((GROUP // 2, MODEL), BF16),
+            jax.ShapeDtypeStruct((GROUP // 2 + SMALL, MODEL), BF16),
         ]
-        + [jax.ShapeDtypeStruct((2, STORED, 2 * PAIR), BF16)] * 4
-        + [
-            jax.ShapeDtypeStruct((1, MODEL), F32),
-        ],
+        + [jax.ShapeDtypeStruct((4, STORED, 2 * PAIR), BF16)] * 2,
         scratch_shapes=[
             pltpu.VMEM((GROUP, MODEL), BF16),
             pltpu.VMEM((GROUP, PAIR), BF16),
@@ -255,27 +302,33 @@
         ],
         compiler_params=pltpu.CompilerParams(vmem_limit_bytes=VMEM_LIMIT),
         cost_estimate=pl.CostEstimate(
-            flops=8 * 10**9, bytes_accessed=16 * 10**6, transcendentals=2 * 10**6
+            flops=10**6, bytes_accessed=10**5, transcendentals=0
         ),
         name="attend_back",
-    )(order, spread, doc_row, doc_col, gain, weights, normed, qkv, att, lse, *pieces)
-
-
-def moe_kernel(first_ref, rank_ref, bias_ref, router_ref, w_ref, *refs, begin, count, more):
+    )(order, spread, doc_row, doc_col, gain, small, weights, normed, qkv, att, lse, *pieces)
+
+
+def moe_kernel(first_ref, router_ref, w_ref, *refs, begin, count, more):
     sources, refs = (refs[:4], refs[4:8]), refs[8:]
     if more:
         prev_out_ref, prev_dn_ref = refs[:2]
+        refs = refs[3:]
+        outs, refs = (refs[:2], refs[2:4]), refs[4:]
+    else:
+        out_ref, dn_ref = refs[:2]
         refs = refs[2:]
-    out_ref, dn_ref, g_ref, in_all, dout_all, hid_all, dgu_all, held, sems = refs
+    g_ref, in_all, dout_all, hid_all, dgu_all, held_t, held_c, sems, done, done_sems = refs
     step = pl.program_id(0)
+    pairs = TILE // PAIR
+    height = pairs * SLOTS
     last = PLANE // TILE - 1
 
     def copies(tile):
         return [
             pltpu.make_async_copy(
-                sources[kind][tile], held.at[kind, tile % 2], sems.at[kind, tile % 2]
+                sources[kind][tile], held.at[tile % 2], sems.at[kind, tile % 2]
             )
-            for kind in range(2)
+            for kind, held in enumerate((held_t, held_c))
         ]
 
     for tile in range(last + 1):
@@ -292,32 +345,45 @@
             for copy in copies(tile):
                 copy.wait()
 
-    t_ref, c_ref = held.at[0, lax.rem(step, 2)], held.at[1, lax.rem(step, 2)]
-    pairs = TILE // PAIR
-    height = pairs * SLOTS
+    t_ref, c_ref = held_t.at[lax.rem(step, 2)], held_c.at[lax.rem(step, 2)]
+    ids = c_ref[:, MODEL:].astype(F32).T.astype(jnp.int32)
+    expert_at = lax.broadcasted_iota(jnp.int32, (EXPERTS, TILE), 0) + first_ref[0]
+    expert_at = jnp.where(expert_at >= EXPERTS, expert_at - EXPERTS, expert_at)
+    hits = ids[:1] == expert_at
+    for choice in range(1, TOP):
+        hits = hits | (ids[choice : choice + 1] == expert_at)
+    mine = jnp.where(hits[:8], 1.0, 0.0)
+    upto = lax.broadcasted_iota(jnp.int32, (PAIR, PAIR), 0) <= lax.broadcasted_iota(
+        jnp.int32, (PAIR, PAIR), 1
+    )
+    upto = jnp.where(upto, 1.0, 0.0).astype(BF16)
+    ranks = []
+    for pair in range(pairs):
+        here = mine[:, pair * PAIR : (pair + 1) * PAIR]
+        ranks.append(jnp.where(here > 0.5, dot(here.astype(BF16), upto) - 1.0, -1.0).astype(jnp.int32))
     spot = pl.ds(pl.multiple_of(step * height, 16), height)
-    logits = dot_nt(router_ref[...], t_ref[...]) + bias_ref[...]
+    logits = jnp.where(hits, dot_nt(router_ref[...], t_ref[...]), NEG_FILL)
     logits = jnp.exp(logits - jnp.max(logits, axis=0, keepdims=True))
     gates = logits / jnp.sum(logits, axis=0, keepdims=True)
     slot_at = lax.broadcasted_iota(jnp.int32, (SLOTS, PAIR), 0)
     picks, slot_gates, ins, cots = [], [], [], []
     for pair in range(pairs):
         cols = slice(pair * PAIR, (pair + 1) * PAIR)
-        hits = [slot_at == rank_ref[pair, begin + e : begin + e + 1, :] for e in range(count)]
+        taken = [slot_at == ranks[pair][begin + e : begin + e + 1, :] for e in range(count)]
         slot_gates.append(
             [
                 jnp.sum(
-                    jnp.where(hits[e], gates[begin + e : begin + e + 1, cols], 0.0),
+                    jnp.where(taken[e], gates[begin + e : begin + e + 1, cols], 0.0),
                     axis=1,
                     keepdims=True,
                 )
                 for e in range(count)
             ]
         )
-        pick = jnp.concatenate([jnp.where(h, 1.0, 0.0).astype(BF16) for h in hits], axis=0)
+        pick = jnp.concatenate([jnp.where(h, 1.0, 0.0).astype(BF16) for h in taken], axis=0)
         picks.append(pick)
         ins.append(dot(pick, t_ref[cols, :]).astype(BF16))
-        cots.append(dot(pick, c_ref[cols, :]).astype(BF16))
+        cots.append(dot(pick, c_ref[cols, :MODEL]).astype(BF16))
     mixed = [[] for _ in range(pairs)]
     dins = [[] for _ in range(pairs)]
     lane = lax.broadcasted_iota(jnp.int32, (height, EXTRA), 1)
@@ -360,26 +426,52 @@
         if more:
             out = out + prev_out_ref[cols, :].astype(F32)
             dn = dn + prev_dn_ref[cols, :].astype(F32)
-        out_ref[cols, :] = out.astype(BF16)
-        dn_ref[cols, :] = dn.astype(BF16)
+        if not more:
+            out_ref[cols, :] = out.astype(BF16)
+            dn_ref[cols, :] = dn.astype(BF16)
+            continue
+
+        for side in range(2):
+
+            @pl.when(step // 2 == side)
+            def _():
+                outs[side][0][cols, :] = out.astype(BF16)
+                outs[side][1][cols, :] = dn.astype(BF16)
 
     @pl.when(step == last)
     def _():
+        sent = []
         for e in range(count):
-            for start in range(0, MODEL, 2 * 192):
-                cols = slice(start, start + 384)
+            if e >= 2:
+                sent[e - 2].wait()
+            for start in range(0, MODEL, 2 * STORED):
+                cols = slice(start, start + 2 * STORED)
                 gate_up_g = dot_tn(in_all[e, :, cols], dgu_all[e])
                 down_g = dot_tn(dout_all[e, :, cols], hid_all[e])
                 both = jnp.concatenate([gate_up_g, down_g], axis=1).astype(BF16)
                 for half in range(2):
-                    g_ref[start // 192 + half, e, :, :] = both[half * 192 : (half + 1) * 192, :]
-
-
-def moe(chunk, first, rank, bias, router_t, weights, rows, cots, previous):
+                    at = slice(half * STORED, (half + 1) * STORED)
+                    done[e % 2, start // STORED + half, :, :] = both[at, :]
+            sent.append(
+                pltpu.make_async_copy(done.at[e % 2], g_ref.at[:, begin + e], done_sems.at[e % 2])
+            )
+            sent[e].start()
+        for copy in sent[-2:]:
+            copy.wait()
+
+
+def moe(chunk, first, router_t, weights, rows, cots, previous):
     begin, count = chunk
     height = PLANE // PAIR * SLOTS
     wide = pl.BlockSpec((TILE, MODEL), lambda i: (i, 0))
     wider = pl.BlockSpec((TILE, MODEL + EXTRA), lambda i: (i, 0))
+    if previous is None:
+        sums = [wide, wider]
+        shapes = [(PLANE, MODEL), (PLANE, MODEL + EXTRA)]
+    else:
+        sides = (lambda i: (jnp.minimum(i, 1), 0)), (lambda i: (jnp.maximum(i - 2, 0), 0))
+        sums = [pl.BlockSpec((TILE, w), side) for side in sides for w in (MODEL, MODEL + EXTRA)]
+        shapes = [(PLANE // 2, MODEL), (PLANE // 2, MODEL + EXTRA)] * 2
     whole = pl.BlockSpec((8, count, 192, 3 * FF_DEV), lambda i: (0, 0, 0, 0), pipeline_mode=pl.Buffered(1))
     flops = 2 * count * height * MODEL * (9 * FF_DEV + 5 * PAIR)
     return pl.pallas_call(
@@ -387,47 +479,34 @@
         grid=(PLANE // TILE,),
         in_specs=[
             smem_spec(),
-            pl.BlockSpec((TILE // PAIR, 8, PAIR), lambda i: (i, 0, 0)),
-            pl.BlockSpec((EXPERTS, TILE), lambda i: (0, i)),
             pl.BlockSpec((EXPERTS, MODEL), lambda i: (0, 0)),
             whole,
         ]
         + [pl.BlockSpec(memory_space=pl.ANY)] * 8
-        + ([wide, wider] if previous is not None else []),
-        out_specs=[wide, wider, pl.BlockSpec((8, count, 192, 3 * FF_DEV), lambda i: (0, 0, 0, 0))],
-        out_shape=[
-            jax.ShapeDtypeStruct((PLANE, MODEL), BF16),
-            jax.ShapeDtypeStruct((PLANE, MODEL + EXTRA), BF16),
-            jax.ShapeDtypeStruct((8, count, 192, 3 * FF_DEV), BF16),
+        + ([wide, wider, pl.BlockSpec(memory_space=pl.ANY)] if previous is not None else []),
+        out_specs=sums + [pl.BlockSpec(memory_space=pl.ANY)],
+        out_shape=[jax.ShapeDtypeStruct(shape, BF16) for shape in shapes]
+        + [
+            jax.ShapeDtypeStruct((8, EXPERTS_DEV, STORED, 3 * FF_DEV), BF16),
         ],
+        input_output_aliases={} if previous is None else {13: 4},
         scratch_shapes=[
             pltpu.VMEM((count, height, MODEL), BF16),
             pltpu.VMEM((count, height, MODEL), BF16),
             pltpu.VMEM((count, height, FF_DEV), BF16),
             pltpu.VMEM((count, height, 2 * FF_DEV), BF16),
-            pltpu.VMEM((2, 2, TILE, MODEL), BF16),
+            pltpu.VMEM((2, TILE, MODEL), BF16),
+            pltpu.VMEM((2, TILE, MODEL + EXTRA), BF16),
             pltpu.SemaphoreType.DMA((2, 2)),
+            pltpu.VMEM((2, 8, STORED, 3 * FF_DEV), BF16),
+            pltpu.SemaphoreType.DMA((2,)),
         ],
         compiler_params=pltpu.CompilerParams(vmem_limit_bytes=VMEM_LIMIT),
         cost_estimate=pl.CostEstimate(
-            flops=flops, bytes_accessed=50 * 10**6, transcendentals=count * height * FF_DEV
+            flops=10**6, bytes_accessed=10**5, transcendentals=0
         ),
         name="moe",
-    )(first, rank, bias, router_t, weights, *rows, *cots, *(previous or ()))
-
-
-def slot_tables(routes_all, col):
-    ids = jnp.remainder(routes_all - EXPERTS_DEV * col, EXPERTS)
-    hits = jnp.any(ids[None] == jnp.arange(EXPERTS, dtype=jnp.int32)[:, None, None], axis=-1)
-    bias = jnp.where(hits, 0.0, NEG_FILL).astype(F32)
-    local = hits[:EXPERTS_DEV].reshape(EXPERTS_DEV, PLANE // PAIR, PAIR)
-    upto = jnp.arange(PAIR)[:, None] <= jnp.arange(PAIR)[None, :]
-    counts = jnp.einsum(
-        "epi,ij->pej", local.astype(BF16), upto.astype(BF16), preferred_element_type=F32
-    ).astype(jnp.int32)
-    rank = jnp.where(local.transpose(1, 0, 2), counts - 1, -1)
-    rank = jnp.pad(rank, ((0, 0), (0, 8 - EXPERTS_DEV), (0, 0)), constant_values=-1)
-    return bias, rank
+    )(first, router_t, weights, *rows, *cots, *(previous or ()))
 
 
 def across_col(value, distance):
@@ -459,57 +538,40 @@
     return result
 
 
+def after(value, *before):
+    return lax.optimization_barrier((value, before))[0]
+
+
+def spread_col(value):
+    return [value] + [across_col(value, d) for d in (1, 2, 3)]
+
+
 def gather_col(value):
-    near = [value] + [across_col(value, d) for d in (1, 2, 3)]
+    near = spread_col(value)
     return near + [other_core(v) for v in near]
 
 
-def gather_plane(value):
-    near = []
-    for mine in (value, other_row(value)):
-        near.append(jnp.concatenate([mine] + [across_col(mine, d) for d in (1, 2, 3)], axis=0))
-    return near + [other_core(v) for v in near]
-
-
 def scatter_blocks(near, far):
-    blocks = [
+    sums = [
         total([near[d * ROWS : (d + 1) * ROWS], far[d * ROWS : (d + 1) * ROWS]]) for d in range(4)
     ]
-    return [blocks[0]] + [across_col(blocks[d].astype(BF16), -d) for d in (1, 2, 3)]
-
-
-def scatter_col(near, far):
-    return total(scatter_blocks(near, other_core(far)))
-
-
-def scatter_plane(value):
-    half = value.shape[0] // 2
-    quarter = half // 2
-    far = other_core(value[half:])
-    theirs = total(scatter_blocks(value[quarter:half], far[quarter:]))
-    mine = total(scatter_blocks(value[:quarter], far[:quarter]))
-    return mine + other_row(theirs.astype(BF16)).astype(F32)
-
-
-def gather_dp(value):
-    both = jnp.stack([value, other_y(value)])
-    return [both] + [along_z(both, d) for d in (1, 2, 3)]
-
-
-def scatter_dp(values):
-    both = total([values[0]] + [along_z(values[d], -d) for d in (1, 2, 3)])
-    mine = (both[0] + other_y(both[1].astype(BF16)).astype(F32)).astype(BF16)
-    return total([mine, other_row(mine)])
-
-
-def sum_all(value):
-    value = value + other_core(value)
-    value = value + across_col(value, 2)
-    value = value + lax.ppermute(value, "col", [(s, s ^ 2) for s in range(8)])
-    value = value + other_row(value)
-    value = value + other_y(value)
-    value = value + along_z(value, 2)
-    return value + lax.ppermute(value, "dp", [(s, s ^ 1) for s in range(8)])
+    return sums[:1] + [v.astype(BF16) for v in sums[1:]]
+
+
+def collect_col(blocks):
+    return [blocks[0]] + [across_col(blocks[d], -d) for d in (1, 2, 3)]
+
+
+def flip_x(value):
+    return lax.ppermute(value, "col", [(s, s ^ 2) for s in range(8)])
+
+
+def flip_z(value):
+    return lax.ppermute(value, "dp", [(s, s ^ 1) for s in range(8)])
+
+
+def add_both(value, move):
+    return (value.astype(F32) + move(value).astype(F32)).astype(value.dtype)
 
 
 def per_device(
@@ -538,84 +600,101 @@
 ):
     col, row, dp = lax.axis_index("col"), lax.axis_index("row"), lax.axis_index("dp")
     across, core = col // 2, col % 2
-    attn_w = jnp.concatenate([projection_weight[:, 0, :], w_proj.T], axis=1).astype(BF16)
-    attn_pieces = gather_dp(attn_w)
-    expert_w = jnp.concatenate(
-        [w_gate_up.reshape(EXPERTS_DEV, 192, 2 * FF_DEV), w_down.transpose(0, 2, 1)], axis=2
-    ).astype(BF16)
-    expert_ws = [
-        lax.all_gather(expert_w[b : b + n], "dp", axis=0, tiled=False) for b, n in CHUNKS
-    ]
-
-    residual_in = tokens.astype(F32)
-    inverse_one = inv_rms(residual_in)
-    normed_one = (residual_in * inverse_one * norm_gains[0]).astype(BF16)
-    normed_pieces = gather_col(normed_one)
     steps = jnp.arange(4, dtype=jnp.int32)
     away = 2 * jnp.remainder(across - steps, 4)
     order = jnp.concatenate([away + core, away + 1 - core])
-    spread = (
-        jnp.remainder(dp % 4 - steps, 4)[:, None]
-        + 4 * jnp.stack([dp // 4, 1 - dp // 4]).astype(jnp.int32)[None, :]
-    ).reshape(-1)
+    spread = jnp.bitwise_xor(dp, jnp.arange(8, dtype=jnp.int32))
     token_places = jnp.arange(GROUP, dtype=jnp.int32)
     doc_ends = jnp.cumsum(lengths[0])
     documents = jnp.sum((token_places[:, None] >= doc_ends[None, :]).astype(jnp.int32), axis=1)
     doc_row, doc_col = documents[None, :], documents[:, None]
-    normed_full, attn_full, qkv, att, lse, *attn_parts = attend(
-        order, spread, doc_row, doc_col, normed_pieces, attn_pieces
-    )
-    attn_out = scatter_col(*attn_parts)
-
-    cot_ready, _ = lax.optimization_barrier((cotangent, normed_pieces))
-    cots = gather_plane(cot_ready)
-    routes_all = lax.all_gather(routes, ("row", "col"), axis=0, tiled=False)
-    plane = jnp.stack([row * 8, (1 - row) * 8])[None, :, None] + order.reshape(2, 1, 4)
-    routes_all = routes_all[plane.reshape(-1)].reshape(PLANE, -1)
+
+    residual_in = tokens.astype(F32)
+    inverse_one = inv_rms(residual_in)
+    normed_one = (residual_in * inverse_one * norm_gains[0]).astype(BF16)
+    attn_w = jnp.concatenate([projection_weight[:, 0, :], w_proj.T], axis=1).astype(BF16)
+    normed_near = spread_col(normed_one)
+    normed_pieces = normed_near + [other_core(v) for v in normed_near]
+    attn_full = lax.all_gather(attn_w, "dp", axis=0, tiled=True)
+
+    gate_up_w, down_w = after((w_gate_up, w_down), attn_w, normed_one)
+    expert_w = jnp.concatenate(
+        [gate_up_w.reshape(EXPERTS_DEV, 192, 2 * FF_DEV), down_w.transpose(0, 2, 1)], axis=2
+    ).astype(BF16)
+    expert_ws = []
+    for b, n in CHUNKS:
+        expert_ws.append(lax.all_gather(expert_w[b : b + n], "dp", axis=0, tiled=False))
+
+    tagged = jnp.concatenate(
+        [cotangent, routes.astype(BF16), jnp.zeros((ROWS, EXTRA - routes.shape[1]), BF16)], axis=1
+    )
+    cots = [jnp.concatenate(spread_col(tagged), axis=0)]
+    theirs = other_row(tagged)
+    cots.append(jnp.concatenate(spread_col(theirs), axis=0))
+    attn_full = after(attn_full, normed_pieces, cots)
+    normed_full, qkv, att, lse, near, far = attend(
+        order, doc_row, doc_col, normed_pieces, attn_full
+    )
+    attn_out = total(collect_col(scatter_blocks(near, other_core(far))))
+    cots = cots + [other_core(v) for v in cots]
+    router_low = router_w.astype(BF16)
+    router_t = jnp.roll(router_low.T, -EXPERTS_DEV * col, axis=0)
+    first = (EXPERTS_DEV * col).astype(jnp.int32).reshape(1)
 
     residual = residual_in + attn_out
     inverse_two = inv_rms(residual)
     normed_two = (residual * inverse_two * norm_gains[1]).astype(BF16)
-    rows_all = gather_plane(normed_two)
-    router_low = router_w.astype(BF16)
-    bias, rank = slot_tables(routes_all, col)
-    router_t = jnp.roll(router_low.T, -EXPERTS_DEV * col, axis=0)
-    first = (EXPERTS_DEV * col).astype(jnp.int32).reshape(1)
-    previous = None
-    expert_grads = []
-    for chunk, weights in zip(CHUNKS, expert_ws):
-        *previous, grads = moe(chunk, first, rank, bias, router_t, weights, rows_all, cots, previous)
-        expert_grads.append(grads)
-    mix_part, dn_part = previous
-    dn = scatter_plane(dn_part)
-    mix_part, _ = lax.optimization_barrier((mix_part, dn))
-    mixture = scatter_plane(mix_part)
-    expert_sums = [
-        lax.psum_scatter(g, "dp", scatter_dimension=0, tiled=False) for g in expert_grads
+    normed_two = after(normed_two, cots)
+    rows_all = [
+        jnp.concatenate(spread_col(v), axis=0) for v in (normed_two, other_row(normed_two))
     ]
-    output = (residual + mixture).astype(BF16)
-
+    rows_all = rows_all + [other_core(v) for v in rows_all]
     logits = jnp.dot(normed_two, router_low, preferred_element_type=F32)
     route_hits = jnp.any(
         routes[:, None, :] == jnp.arange(EXPERTS, dtype=jnp.int32)[None, :, None], axis=-1
     )
     gates = jax.nn.softmax(jnp.where(route_hits, logits, NEG_FILL), axis=-1)
+
+    previous = None
+    for chunk, weights in zip(CHUNKS, expert_ws):
+        previous = moe(chunk, first, router_t, weights, rows_all, cots, previous)
+    mix_near, dn_near, mix_far, dn_far, expert_grads = previous
+    expert_sum = lax.psum_scatter(expert_grads, "dp", scatter_dimension=0, tiled=False)
+
+    far = other_core(dn_far)
+    theirs = collect_col(scatter_blocks(dn_near[TILE:], far[TILE:]))
+    mine = collect_col(scatter_blocks(dn_near[:TILE], far[:TILE]))
+    mix_far = other_core(after(mix_far, far))
+    mix_blocks = []
+    for d in range(4):
+        parts = [slice(start + d * ROWS, start + (d + 1) * ROWS) for start in (0, TILE)]
+        parts = [total([mix_near[part], mix_far[part]]) for part in parts]
+        mix_blocks.append(jnp.concatenate(parts, axis=0).astype(BF16))
+    mine = after(mine, mix_blocks)
+    dn = total(mine) + other_row(total(theirs).astype(BF16)).astype(F32)
     dgate = dn[:, MODEL : MODEL + EXPERTS] + dn[:, MODEL + EXPERTS : MODEL + 2 * EXPERTS]
     dlogits = gates * (dgate - jnp.sum(gates * dgate, axis=-1, keepdims=True))
     dnormed_two = dn[:, :MODEL] + jnp.dot(dlogits, router_low.astype(F32).T, precision=EXACT_MATH)
-    grad_router = lax.dot_general(
-        dlogits, normed_two.astype(F32), (((0,), (0,)), ((), ())), precision=EXACT_MATH
-    )
     upstream = cotangent.astype(F32)
     dresid_norm, grad_gain_two = norm_back(residual, inverse_two, norm_gains[1], dnormed_two)
     dresidual = upstream + dresid_norm
-    dattn_pieces = gather_col(dresidual.astype(BF16))
-    near, far, *attn_grads, grad_gain_one = attend_back(
+    dattn_near = spread_col(dresidual.astype(BF16))
+    dattn_far = [other_core(v) for v in dattn_near]
+
+    grad_router = lax.dot_general(
+        dlogits, normed_two.astype(F32), (((0,), (0,)), ((), ())), precision=EXACT_MATH
+    )
+    small = jnp.concatenate(
+        [grad_router, grad_gain_two[None], jnp.zeros((SMALL - EXPERTS - 1, MODEL), F32)], axis=0
+    )
+    dattn_pieces = after(dattn_near + dattn_far, small)
+    near, far, *attn_grads = attend_back(
         order,
         spread,
         doc_row,
         doc_col,
         norm_gains[:1],
+        small,
         attn_full,
         normed_full,
         qkv,
@@ -623,18 +702,40 @@
         lse,
         dattn_pieces,
     )
-    dnormed = scatter_col(near, far)
+    theirs = other_core(far)
+    blocks = scatter_blocks(near, theirs)
+    small = total([far[GROUP // 2 :], theirs[GROUP // 2 :]]).astype(BF16)
+    moved = [across_col(jnp.concatenate([blocks[d], small], axis=0), -d) for d in (1, 2, 3)]
+    attn_moved = other_y(after(attn_grads[1], blocks))
+    moved, attn_moved = lax.optimization_barrier((moved, attn_moved))
+    mix_moved = collect_col(after(mix_blocks, moved))
+    smalls = jnp.stack([small] + [v[ROWS:] for v in moved])[jnp.remainder(steps - across, 4)]
+    small = total([smalls[d] for d in range(4)]).astype(BF16).reshape(-1, 2 * PAIR)
+    dnormed = total([blocks[0]] + [v[:ROWS] for v in moved])
     dtokens_norm, _ = norm_back(residual_in, inverse_one, norm_gains[0], dnormed)
     dtokens = dresidual + dtokens_norm
-    attn_sums = scatter_dp(attn_grads)
-    early = sum_all(jnp.concatenate([grad_router, grad_gain_two[None]], axis=0))
-    sum_router = early[:EXPERTS].T
-    sum_gains = jnp.concatenate([sum_all(grad_gain_one), early[EXPERTS:]], axis=0)
+    halves = total([attn_grads[0], attn_moved]).astype(BF16)
+    sent = jnp.concatenate([halves[2:].reshape(-1, 2 * PAIR), small], axis=0)
+    kept = jnp.concatenate([halves[:2].reshape(-1, 2 * PAIR), small], axis=0)
+    kept = total([kept, along_z(sent, 2)]).astype(BF16)
+    sent = kept[STORED:]
+    kept = jnp.concatenate([kept[:STORED], kept[2 * STORED :]], axis=0)
+    kept = total([kept, flip_z(sent)]).astype(BF16)
+    kept = add_both(kept, other_row)
+    attn_sums = kept[:STORED].astype(F32)
+    small = add_both(kept[STORED:], other_y)
+    experts_new = update_experts(
+        expert_sum, (w_gate_up, gate_up_first, gate_up_second), (w_down, down_first, down_second)
+    )
+    mix_moved = after(mix_moved, experts_new, dtokens, attn_sums)
+    mixed = total(mix_moved)
+    mixture = mixed[:ROWS] + other_row(mixed[ROWS:].astype(BF16)).astype(F32)
+    output = (residual + mixture).astype(BF16)
+    small = small.reshape(-1, MODEL).astype(F32)
+    sum_router = small[:EXPERTS].T
+    sum_gains = jnp.stack([small[EXPERTS + 1], small[EXPERTS]])
     sum_qkv = attn_sums[:, None, :QKV]
-    sum_proj = attn_sums[:, QKV:].T
-    expert_sum = jnp.concatenate(expert_sums, axis=0).astype(F32)
-    sum_gate_up = expert_sum[:, :, : 2 * FF_DEV].reshape(EXPERTS_DEV, 192, 2, FF_DEV)
-    sum_down = expert_sum[:, :, 2 * FF_DEV :].transpose(0, 2, 1)
+    sum_proj = attn_sums[:, QKV : 2 * PAIR].T
     return (
         output,
         dtokens,
@@ -649,8 +750,7 @@
             DECAY_RATE,
         ),
         *adamw(w_proj, sum_proj, proj_first, proj_second, RATE_WIDE, DECAY_RATE),
-        *adamw(w_gate_up, sum_gate_up, gate_up_first, gate_up_second, RATE_NARROW, DECAY_RATE),
-        *adamw(w_down, sum_down, down_first, down_second, RATE_WIDE, DECAY_RATE),
+        *experts_new,
     )
 
 

time: 607 us -> 502 us (0.83)
  waiting for transfers between devices: 241 us -> 198 us
  starting transfers between devices: 105 us -> 74.8 us
  blocking collectives: 21 us -> 0 us
  local copies, waits for them, and re-layouts: 40.1 us -> 31.7 us
  other arithmetic: 49.5 us -> 42 us
    ppermute x8 -> x1, waiting for transfers between devices: 45.6 us -> 5.19 us  [along_z(): return lax.ppermute(value, 'dp', pairs)]
    all_gather x1 -> x0, blocking collectives: 21 us -> none  [per_device(): routes_all = lax.all_gather(routes, ('row', 'col'), axis=0, tiled=False)]
    ppermute x8 -> x1, starting transfers between devices: 35.1 us -> 14.9 us  [along_z(): return lax.ppermute(value, 'dp', pairs)]
    sub x6 -> x4, other arithmetic: 16.8 us -> 2.1 us  [adamw(): weight - step_rate * (direction + weight_decay * weight)]
    pallas_call x1 -> x2, Pallas kernels: 15.3 us -> 25.1 us  [the longest x1 15.2 us: attend(): pl.pallas_call(attend_kernel, in_specs=[smem_spec()] + [vmem_spec()] * (3...]
    ppermute x4 -> x2, waiting for transfers between devices: 7.27 us -> 0.01 us  [other_y(): return lax.ppermute(value, 'dp', [(s, s ^ 4) for s in range(8)])]
    pallas_call x3 -> x2, Pallas kernels: 90.5 us -> 84.6 us  [moe(): pl.pallas_call(functools.partial(moe_kernel, begin=begin, count=count, mo...]
    ppermute x18 -> x16, waiting for transfers between devices: 12.6 us -> 18.3 us  [other_core(): return lax.ppermute(value, 'col', [(s, s ^ 1) for s in range(8)])]
  transfers between devices with their start and end apart: 85 -> 62, of which waited for: 40 -> 29; matrix products, arithmetic and copies ran while one was open for 13% -> 13% of each run, Pallas kernels for 21% -> 19%
where the time goes in v2:
time: 502 us; the launch traced here: 494 us
  waiting for transfers between devices  198 us (39%)
  Pallas kernels  130 us (26%)
  starting transfers between devices  74.8 us (15%)
  other arithmetic  42 us (8%)
  local copies, waits for them, and re-layouts  31.7 us (6%)
  between operations  15 us (3%)
    ppermute x33, waiting for transfers between devices, across_col(): return lax.ppermute(value, 'col', pairs)  143 us
    pallas_call x2, Pallas kernels, moe(): pl.pallas_call(functools.partial(moe_kernel, begin=begin, count=count, mo...  84.6 us
    ppermute x33, starting transfers between devices, across_col(): return lax.ppermute(value, 'col', pairs)  44.7 us
    ppermute x5, waiting for transfers between devices, other_row(): return lax.ppermute(value, 'row', [(0, 1), (1, 0)])  23.6 us
    unnamed x134, local copies, waits for them, and re-layouts  21 us
    pallas_call x1, Pallas kernels, attend_back(): pl.pallas_call(attend_back_kernel, in_specs=[smem_spec()] * 2 + [vmem_spe...  20.3 us
    ppermute x16, waiting for transfers between devices, other_core(): return lax.ppermute(value, 'col', [(s, s ^ 1) for s in range(8)])  18.3 us
    pallas_call x1, Pallas kernels, attend(): pl.pallas_call(attend_kernel, in_specs=[smem_spec()] + [vmem_spec()] * (3...  15.2 us
  transfers between devices with their start and end apart: 62, of which 29 were waited for; matrix products, arithmetic and copies ran while one was open for 13% of the time, Pallas kernels for 19%

profile of v2, /device:TPU:32, one launch (start us, length us, event | category | flops | bytes accessed | tf_op | source)
XLA Modules:
  0.0 493.9 jit_solution(18169950048816754697)
XLA Ops:
  34.3 9.0 %collective-permute-done.7 = bf16[128,1664]{1,0:T(8,128)(2,1)S(1)} collective-permute-done((bf16[128,1664]{1,0:T(8,128)(2,1)S(1)}, bf16[128,1664]{1,0:T(8,128)(2,1)S(1)}, u32[]{:S(2)}, u32[]{:S(2)}) %collective-permute-start.7) | collective-permute-done | bytes 426016 | tf_op jit(solution)/shard_map/ppermute | solution.py:514
  52.0 17.3 %collective-permute-done.11 = bf16[128,1664]{1,0:T(8,128)(2,1)S(1)} collective-permute-done((bf16[128,1664]{1,0:T(8,128)(2,1)}, bf16[128,1664]{1,0:T(8,128)(2,1)S(1)}, u32[]{:S(2)}, u32[]{:S(2)}) %collective-permute-start.11) | collective-permute-done | bytes 426016 | tf_op jit(solution)/shard_map/ppermute | solution.py:514
  73.4 5.7 %collective-permute-done.12 = bf16[128,1664]{1,0:T(8,128)(2,1)S(1)} collective-permute-done((bf16[128,1664]{1,0:T(8,128)(2,1)}, bf16[128,1664]{1,0:T(8,128)(2,1)S(1)}, u32[]{:S(2)}, u32[]{:S(2)}) %collective-permute-start.12) | collective-permute-done | bytes 426016 | tf_op jit(solution)/shard_map/ppermute | solution.py:514
  82.4 15.2 %attend.1 = (bf16[1024,1536]{1,0:T(8,128)(2,1)}, bf16[1024,320]{1,0:T(8,128)(2,1)}, bf16[1024,256]{1,0:T(8,128)(2,1)}, f32[8,1024]{1,0:T(8,128)}, bf16[512,1536]{1,0:T(8,128)(2,1)}, /*index=5*/bf16[512,1536]{1,0:T(8,128)(2,1)}) custom-call(s32[8]{0:T(128)} %pad_add_fusion.order_ref, s32[1,1024]{1,0:T(1,128)} %bitcast.111, s32[1024,1]{1,0:T(8,128)} %copy.122.doc_col_ref, ...), custom_call_target="tpu_custom_call" | custom-call | flops 1000000 | bytes 100000 | tf_op jit(solution)/shard_map/attend/pallas_call | solution.py:266
  98.7 4.0 collective-permute-done.14
  107.5 16.2 %collective-permute-done.15 = bf16[128,1536]{1,0:T(8,128)(2,1)S(1)} collective-permute-done((bf16[128,1536]{1,0:T(8,128)(2,1)S(1)}, bf16[128,1536]{1,0:T(8,128)(2,1)S(1)}, u32[]{:S(2)}, u32[]{:S(2)}) %collective-permute-start.15) | collective-permute-done | bytes 393248 | tf_op jit(solution)/shard_map/ppermute | solution.py:514
  132.9 8.8 %collective-permute-done.23 = bf16[128,1536]{1,0:T(8,128)(2,1)S(1)} collective-permute-done((bf16[128,1536]{1,0:T(8,128)(2,1)S(1)}, bf16[128,1536]{1,0:T(8,128)(2,1)S(1)}, u32[]{:S(2)}, u32[]{:S(2)}) %collective-permute-start.23) | collective-permute-done | bytes 393248 | tf_op jit(solution)/shard_map/ppermute | solution.py:522
  141.6 9.4 %collective-permute-done.20 = bf16[128,1536]{1,0:T(8,128)(2,1)S(1)} collective-permute-done((bf16[128,1536]{1,0:T(8,128)(2,1)S(1)}, bf16[128,1536]{1,0:T(8,128)(2,1)S(1)}, u32[]{:S(2)}, u32[]{:S(2)}) %collective-permute-start.20) | collective-permute-done | bytes 393248 | tf_op jit(solution)/shard_map/ppermute | solution.py:514
  154.4 12.3 %collective-permute-done.24 = bf16[128,1536]{1,0:T(8,128)(2,1)S(1)} collective-permute-done((bf16[128,1536]{1,0:T(8,128)(2,1)S(1)}, bf16[128,1536]{1,0:T(8,128)(2,1)S(1)}, u32[]{:S(2)}, u32[]{:S(2)}) %collective-permute-start.24) | collective-permute-done | bytes 393248 | tf_op jit(solution)/shard_map/ppermute | solution.py:514
  176.3 47.2 %moe.2 = (bf16[2048,1536]{1,0:T(8,128)(2,1)}, bf16[2048,1664]{1,0:T(8,128)(2,1)}, bf16[8,5,192,768]{3,2,1,0:T(8,128)(2,1)}) custom-call(s32[1]{0:T(128)} %bitcast.6.first_ref, bf16[40,1536]{1,0:T(8,128)(2,1)} %fusion.19.router_ref, bf16[8,3,192,768]{3,2,1,0:T(8,128)(2,1)} %bitcast.98, bf16[512,1536]{1,0:T(8,128)(2,1)} %copy-done.2, ...), custom_call_target="tpu_custom_call" | custom-call | flops 1000000 | bytes 100000 | tf_op jit(solution)/shard_map/moe/pallas_call | solution.py:477
  223.6 37.4 %moe.3 = (bf16[1024,1536]{1,0:T(8,128)(2,1)}, bf16[1024,1664]{1,0:T(8,128)(2,1)}, bf16[1024,1536]{1,0:T(8,128)(2,1)}, bf16[1024,1664]{1,0:T(8,128)(2,1)}, bf16[8,5,192,768]{3,2,1,0:T(8,128)(2,1)}) custom-call(s32[1]{0:T(128)} %bitcast.6.first_ref, bf16[40,1536]{1,0:T(8,128)(2,1)} %fusion.19.router_ref, ...), custom_call_target="tpu_custom_call", output_to_operand_aliasing={{4}: (13, {})} | custom-call | flops 1000000 | bytes 100000 | tf_op jit(solution)/shard_map/moe/pallas_call | solution.py:477
  261.3 6.1 %collective-permute-done.29 = bf16[1024,1664]{1,0:T(8,128)(2,1)S(1)} collective-permute-done((bf16[1024,1664]{1,0:T(8,128)(2,1)}, bf16[1024,1664]{1,0:T(8,128)(2,1)S(1)}, u32[]{:S(2)}, u32[]{:S(2)}) %collective-permute-start.29) | collective-permute-done | bytes 3407904 | tf_op jit(solution)/shard_map/ppermute | solution.py:518
  276.8 15.1 %collective-permute-done.34 = bf16[128,1664]{1,0:T(8,128)(2,1)S(1)} collective-permute-done((bf16[128,1664]{1,0:T(8,128)(2,1)S(1)}, bf16[128,1664]{1,0:T(8,128)(2,1)S(1)}, u32[]{:S(2)}, u32[]{:S(2)}) %collective-permute-start.34) | collective-permute-done | bytes 426016 | tf_op jit(solution)/shard_map/ppermute | solution.py:514
  291.9 4.7 collective-permute-start.33
  306.0 3.8 collective-permute-done.31
  320.5 15.5 %collective-permute-done.38.refs_1_ = bf16[128,1536]{1,0:T(8,128)(2,1)} collective-permute-done((bf16[128,1536]{1,0:T(8,128)(2,1)S(1)}, bf16[128,1536]{1,0:T(8,128)(2,1)}, u32[]{:S(2)}, u32[]{:S(2)}) %collective-permute-start.38) | collective-permute-done | bytes 393248 | tf_op jit(solution)/shard_map/ppermute | solution.py:514
  339.2 20.3 %attend_back.1 = (bf16[512,1536]{1,0:T(8,128)(2,1)}, bf16[560,1536]{1,0:T(8,128)(2,1)}, bf16[4,192,512]{2,1,0:T(8,128)(2,1)}, bf16[4,192,512]{2,1,0:T(8,128)(2,1)}) custom-call(s32[8]{0:T(128)} %pad_add_fusion.order_ref, s32[8]{0:T(128)} %iota_xor_fusion.spread_ref, s32[1,1024]{1,0:T(1,128)} %bitcast.112, s32[1024,1]{1,0:T(8,128)} %copy.122.doc_col_ref, ...), custom_call_target="tpu_custom_call" | custom-call | flops 1000000 | bytes 100000 | tf_op jit(solution)/shard_map/attend_back/pallas_call | solution.py:287
  371.6 22.2 %collective-permute-done.46 = bf16[176,1536]{1,0:T(8,128)(2,1)S(1)} collective-permute-done((bf16[176,1536]{1,0:T(8,128)(2,1)S(1)}, bf16[176,1536]{1,0:T(8,128)(2,1)S(1)}, u32[]{:S(2)}, u32[]{:S(2)}) %collective-permute-start.46) | collective-permute-done | bytes 540704 | tf_op jit(solution)/shard_map/ppermute | solution.py:514
  406.8 14.9 %collective-permute-start.53 = (bf16[528,512]{1,0:T(8,128)(2,1)}, bf16[528,512]{1,0:T(8,128)(2,1)}, u32[]{:S(2)}, u32[]{:S(2)}) collective-permute-start(bf16[528,512]{1,0:T(8,128)(2,1)} %pad_maximum_fusion.9), channel_id=1, source_target_pairs={{0,32},{16,48},{32,0},{48,16},{64,96},{80,112},{96,64},{112,80},{1... | collective-permute-start | bytes 1622024 | tf_op jit(solution)/shard_map/ppermute | solution.py:527
  429.2 5.2 %collective-permute-done.53 = bf16[528,512]{1,0:T(8,128)(2,1)} collective-permute-done((bf16[528,512]{1,0:T(8,128)(2,1)}, bf16[528,512]{1,0:T(8,128)(2,1)}, u32[]{:S(2)}, u32[]{:S(2)}) %collective-permute-start.53) | collective-permute-done | bytes 540704 | tf_op jit(solution)/shard_map/ppermute | solution.py:527
  437.6 7.7 %collective-permute-done.54 = bf16[336,512]{1,0:T(8,128)(2,1)S(1)} collective-permute-done((bf16[336,512]{1,0:T(8,128)(2,1)S(1)}, bf16[336,512]{1,0:T(8,128)(2,1)S(1)}, u32[]{:S(2)}, u32[]{:S(2)}) %collective-permute-start.54) | collective-permute-done | bytes 344096 | tf_op jit(solution)/shard_map/ppermute | solution.py:570
  449.2 6.3 %collective-permute-done.55 = bf16[336,512]{1,0:T(8,128)(2,1)S(1)} collective-permute-done((bf16[336,512]{1,0:T(8,128)(2,1)S(1)}, bf16[336,512]{1,0:T(8,128)(2,1)S(1)}, u32[]{:S(2)}, u32[]{:S(2)}) %collective-permute-start.55) | collective-permute-done | bytes 344096 | tf_op jit(solution)/shard_map/ppermute | solution.py:522
  464.2 9.9 %update_experts.1 = (f32[3840,128]{1,0:T(8,128)}, f32[3840,128]{1,0:T(8,128)}, f32[3840,128]{1,0:T(8,128)}, f32[5,192,256]{2,1,0:T(8,128)}, f32[5,192,256]{2,1,0:T(8,128)}, /*index=5*/f32[5,192,256]{2,1,0:T(8,128)}) custom-call(bf16[5,192,768]{2,1,0:T(8,128)(2,1)} %bitcast.105, f32[3840,128]{1,0:T(8,128)} %bitcast.97, f32[3840,128]{1,0:T(8,128)} %bitcast.101, ...), custom_call_target="tpu_custom_call" | custom-call | flops 20000000 | bytes 20000000 | tf_op jit(solution)/shard_map/update_experts/pallas_call | solution.py:83
  478.6 7.7 %collective-permute-done.56 = bf16[128,1536]{1,0:T(8,128)(2,1)S(1)} collective-permute-done((bf16[128,1536]{1,0:T(8,128)(2,1)S(1)}, bf16[128,1536]{1,0:T(8,128)(2,1)S(1)}, u32[]{:S(2)}, u32[]{:S(2)}) %collective-permute-start.56) | collective-permute-done | bytes 393248 | tf_op jit(solution)/shard_map/ppermute | solution.py:522
  (331 shorter events, 156.9 us)
Async XLA Ops:
  7.2 75.2 %all-gather.6.cloned.1.call-start = ((), (), s32[]{:S(2)}) async-start(), calls=%async_computation.1 | async-start | bytes 1769472 | tf_op jit(solution)/shard_map/all_gather | solution.py:618
  10.3 166.0 %all-gather.10.cloned.1.call-start = ((), (), s32[]{:S(2)}) async-start(), calls=%async_computation.4 | async-start | bytes 7962624 | tf_op jit(solution)/shard_map/all_gather | solution.py:626
  17.7 205.9 %all-gather.8.cloned.1.call-start = ((), (), s32[]{:S(2)}) async-start(), calls=%async_computation.3 | async-start | bytes 5308416 | tf_op jit(solution)/shard_map/all_gather | solution.py:626
  22.8 22.6 %collective-permute-start.8 = (bf16[128,1664]{1,0:T(8,128)(2,1)S(1)}, bf16[128,1664]{1,0:T(8,128)(2,1)S(1)}, u32[]{:S(2)}, u32[]{:S(2)}) collective-permute-start(bf16[128,1664]{1,0:T(8,128)(2,1)S(1)} %concatenate.69), channel_id=1, source_target_pairs={{0,4},{1,5},{2,6},{3,7},{4,0},{5,1},{6,2},{7,3},{8,12},{9,13},{10,... | collective-permute-start | bytes 1277960 | tf_op jit(solution)/shard_map/ppermute | solution.py:514
  27.0 45.8 %collective-permute-start = (bf16[128,1536]{1,0:T(8,128)(2,1)}, bf16[128,1536]{1,0:T(8,128)(2,1)}, u32[]{:S(2)}, u32[]{:S(2)}) collective-permute-start(bf16[128,1536]{1,0:T(8,128)(2,1)} %fusion.3.refs_0_), channel_id=1, source_target_pairs={{0,2},{1,3},{2,4},{3,5},{4,6},{5,7},{6,0},{7,1},{8,10},{9,11},{10,... | collective-permute-start | bytes 1179656 | tf_op jit(solution)/shard_map/ppermute | solution.py:514
  28.4 435.8 %reduce-scatter.2.cloned.1.call-start = ((), (), s32[]{:S(2)}) async-start(), calls=%async_computation.2 | async-start | bytes 13271040 | tf_op jit(solution)/shard_map/reduce_scatter | solution.py:662
  31.3 41.5 %collective-permute-start.1 = (bf16[128,1536]{1,0:T(8,128)(2,1)}, bf16[128,1536]{1,0:T(8,128)(2,1)S(1)}, u32[]{:S(2)}, u32[]{:S(2)}) collective-permute-start(bf16[128,1536]{1,0:T(8,128)(2,1)} %fusion.3.refs_0_), channel_id=1, source_target_pairs={{0,4},{1,5},{2,6},{3,7},{4,0},{5,1},{6,2},{7,3},{8,12},{9,13},{10,... | collective-permute-start | bytes 1179656 | tf_op jit(solution)/shard_map/ppermute | solution.py:514
  43.4 30.0 %collective-permute-start.2 = (bf16[128,1536]{1,0:T(8,128)(2,1)}, bf16[128,1536]{1,0:T(8,128)(2,1)S(1)}, u32[]{:S(2)}, u32[]{:S(2)}) collective-permute-start(bf16[128,1536]{1,0:T(8,128)(2,1)} %fusion.3.refs_0_), channel_id=1, source_target_pairs={{0,6},{1,7},{2,0},{3,1},{4,2},{5,3},{6,4},{7,5},{8,14},{9,15},{10,... | collective-permute-start | bytes 1179656 | tf_op jit(solution)/shard_map/ppermute | solution.py:514
  45.4 23.9 %collective-permute-start.11 = (bf16[128,1664]{1,0:T(8,128)(2,1)}, bf16[128,1664]{1,0:T(8,128)(2,1)S(1)}, u32[]{:S(2)}, u32[]{:S(2)}) collective-permute-start(bf16[128,1664]{1,0:T(8,128)(2,1)} %collective-permute-done.10), channel_id=1, source_target_pairs={{0,2},{1,3},{2,4},{3,5},{4,6},{5,7},{6,0},{7,1},{8,10},{9,11},{10,... | collective-permute-start | bytes 1277960 | tf_op jit(solution)/shard_map/ppermute | solution.py:514
  46.2 32.9 %collective-permute-start.12 = (bf16[128,1664]{1,0:T(8,128)(2,1)}, bf16[128,1664]{1,0:T(8,128)(2,1)S(1)}, u32[]{:S(2)}, u32[]{:S(2)}) collective-permute-start(bf16[128,1664]{1,0:T(8,128)(2,1)} %collective-permute-done.10), channel_id=1, source_target_pairs={{0,4},{1,5},{2,6},{3,7},{4,0},{5,1},{6,2},{7,3},{8,12},{9,13},{10,... | collective-permute-start | bytes 1277960 | tf_op jit(solution)/shard_map/ppermute | solution.py:514
  98.1 30.8 %collective-permute-start.18 = (bf16[512,1664]{1,0:T(8,128)(2,1)S(1)}, bf16[512,1664]{1,0:T(8,128)(2,1)S(1)}, u32[]{:S(2)}, u32[]{:S(2)}) collective-permute-start(bf16[512,1664]{1,0:T(8,128)(2,1)S(1)} %pad_maximum_fusion.refs_4_), channel_id=1, source_target_pairs={{0,1},{1,0},{2,3},{3,2},{4,5},{5,4},{6,7},{7,6},{8,9},{9,8},{10,11... | collective-permute-start | bytes 5111816 | tf_op jit(solution)/shard_map/ppermute | solution.py:518
  98.2 30.7 %collective-permute-start.19 = (bf16[512,1664]{1,0:T(8,128)(2,1)}, bf16[512,1664]{1,0:T(8,128)(2,1)S(1)}, u32[]{:S(2)}, u32[]{:S(2)}) collective-permute-start(bf16[512,1664]{1,0:T(8,128)(2,1)} %constant_dynamic-update-slice_fusion.refs_5_), channel_id=1, source_target_pairs={{0,1},{1,0},{2,3},{3,2},{4,5},{5,4},{6,7},{7,6},{8,9},{9,8},{10,11... | collective-permute-start | bytes 5111816 | tf_op jit(solution)/shard_map/ppermute | solution.py:518
  141.6 25.1 %collective-permute-start.24 = (bf16[128,1536]{1,0:T(8,128)(2,1)S(1)}, bf16[128,1536]{1,0:T(8,128)(2,1)S(1)}, u32[]{:S(2)}, u32[]{:S(2)}) collective-permute-start(bf16[128,1536]{1,0:T(8,128)(2,1)S(1)} %collective-permute-done.23), channel_id=1, source_target_pairs={{0,2},{1,3},{2,4},{3,5},{4,6},{5,7},{6,0},{7,1},{8,10},{9,11},{10,... | collective-permute-start | bytes 1179656 | tf_op jit(solution)/shard_map/ppermute | solution.py:514
  267.4 33.8 %collective-permute-start.30 = (bf16[1024,1536]{1,0:T(8,128)(2,1)}, bf16[1024,1536]{1,0:T(8,128)(2,1)S(1)}, u32[]{:S(2)}, u32[]{:S(2)}) collective-permute-start(bf16[1024,1536]{1,0:T(8,128)(2,1)} %get-tuple-element.86), channel_id=1, source_target_pairs={{0,1},{1,0},{2,3},{3,2},{4,5},{5,4},{6,7},{7,6},{8,9},{9,8},{10,11... | collective-permute-start | bytes 9437192 | tf_op jit(solution)/shard_map/ppermute | solution.py:518
  272.8 23.8 %collective-permute-start.36 = (bf16[128,1664]{1,0:T(8,128)(2,1)S(1)}, bf16[128,1664]{1,0:T(8,128)(2,1)S(1)}, u32[]{:S(2)}, u32[]{:S(2)}) collective-permute-start(bf16[128,1664]{1,0:T(8,128)(2,1)S(1)} %get-tuple-element.227), channel_id=1, source_target_pairs={{0,2},{1,3},{2,4},{3,5},{4,6},{5,7},{6,0},{7,1},{8,10},{9,11},{10,... | collective-permute-start | bytes 1277960 | tf_op jit(solution)/shard_map/ppermute | solution.py:514
  274.4 35.4 %collective-permute-start.31 = (bf16[128,1664]{1,0:T(8,128)(2,1)S(1)}, bf16[128,1664]{1,0:T(8,128)(2,1)S(1)}, u32[]{:S(2)}, u32[]{:S(2)}) collective-permute-start(bf16[128,1664]{1,0:T(8,128)(2,1)S(1)} %get-tuple-element.231), channel_id=1, source_target_pairs={{0,6},{1,7},{2,0},{3,1},{4,2},{5,3},{6,4},{7,5},{8,14},{9,15},{10,... | collective-permute-start | bytes 1277960 | tf_op jit(solution)/shard_map/ppermute | solution.py:514
  365.6 31.6 %collective-permute-start.49 = (bf16[4,192,512]{2,1,0:T(8,128)(2,1)S(1)}, bf16[4,192,512]{2,1,0:T(8,128)(2,1)S(1)}, u32[]{:S(2)}, u32[]{:S(2)}) collective-permute-start(bf16[4,192,512]{2,1,0:T(8,128)(2,1)S(1)} %copy-done.54), channel_id=1, source_target_pairs={{0,64},{16,80},{32,96},{48,112},{64,0},{80,16},{96,32},{112,48},{1... | collective-permute-start | bytes 2359304 | tf_op jit(solution)/shard_map/ppermute | solution.py:531
  368.2 25.5 %collective-permute-start.46 = (bf16[176,1536]{1,0:T(8,128)(2,1)S(1)}, bf16[176,1536]{1,0:T(8,128)(2,1)S(1)}, u32[]{:S(2)}, u32[]{:S(2)}) collective-permute-start(bf16[176,1536]{1,0:T(8,128)(2,1)S(1)} %get-tuple-element.253), channel_id=1, source_target_pairs={{0,6},{1,7},{2,0},{3,1},{4,2},{5,3},{6,4},{7,5},{8,14},{9,15},{10,... | collective-permute-start | bytes 1622024 | tf_op jit(solution)/shard_map/ppermute | solution.py:514
  370.6 23.2 %collective-permute-start.47 = (bf16[176,1536]{1,0:T(8,128)(2,1)S(1)}, bf16[176,1536]{1,0:T(8,128)(2,1)S(1)}, u32[]{:S(2)}, u32[]{:S(2)}) collective-permute-start(bf16[176,1536]{1,0:T(8,128)(2,1)S(1)} %get-tuple-element.252), channel_id=1, source_target_pairs={{0,4},{1,5},{2,6},{3,7},{4,0},{5,1},{6,2},{7,3},{8,12},{9,13},{10,... | collective-permute-start | bytes 1622024 | tf_op jit(solution)/shard_map/ppermute | solution.py:514
  370.6 26.5 %collective-permute-start.48 = (bf16[176,1536]{1,0:T(8,128)(2,1)S(1)}, bf16[176,1536]{1,0:T(8,128)(2,1)S(1)}, u32[]{:S(2)}, u32[]{:S(2)}) collective-permute-start(bf16[176,1536]{1,0:T(8,128)(2,1)S(1)} %get-tuple-element.251), channel_id=1, source_target_pairs={{0,2},{1,3},{2,4},{3,5},{4,6},{5,7},{6,0},{7,1},{8,10},{9,11},{10,... | collective-permute-start | bytes 1622024 | tf_op jit(solution)/shard_map/ppermute | solution.py:514
  406.8 27.6 %collective-permute-start.53 = (bf16[528,512]{1,0:T(8,128)(2,1)}, bf16[528,512]{1,0:T(8,128)(2,1)}, u32[]{:S(2)}, u32[]{:S(2)}) collective-permute-start(bf16[528,512]{1,0:T(8,128)(2,1)} %pad_maximum_fusion.9), channel_id=1, source_target_pairs={{0,32},{16,48},{32,0},{48,16},{64,96},{80,112},{96,64},{112,80},{1... | collective-permute-start | bytes 1622024 | tf_op jit(solution)/shard_map/ppermute | solution.py:527
  425.1 49.0 %collective-permute-start.50 = (bf16[256,1536]{1,0:T(8,128)(2,1)}, bf16[256,1536]{1,0:T(8,128)(2,1)}, u32[]{:S(2)}, u32[]{:S(2)}) collective-permute-start(bf16[256,1536]{1,0:T(8,128)(2,1)} %pad_maximum_fusion.6), channel_id=1, source_target_pairs={{0,6},{1,7},{2,0},{3,1},{4,2},{5,3},{6,4},{7,5},{8,14},{9,15},{10,... | collective-permute-start | bytes 2359304 | tf_op jit(solution)/shard_map/ppermute | solution.py:514
  427.8 46.3 %collective-permute-start.51 = (bf16[256,1536]{1,0:T(8,128)(2,1)}, bf16[256,1536]{1,0:T(8,128)(2,1)}, u32[]{:S(2)}, u32[]{:S(2)}) collective-permute-start(bf16[256,1536]{1,0:T(8,128)(2,1)} %pad_maximum_fusion.7), channel_id=1, source_target_pairs={{0,4},{1,5},{2,6},{3,7},{4,0},{5,1},{6,2},{7,3},{8,12},{9,13},{10,... | collective-permute-start | bytes 2359304 | tf_op jit(solution)/shard_map/ppermute | solution.py:514
  428.7 45.5 %collective-permute-start.52 = (bf16[256,1536]{1,0:T(8,128)(2,1)}, bf16[256,1536]{1,0:T(8,128)(2,1)}, u32[]{:S(2)}, u32[]{:S(2)}) collective-permute-start(bf16[256,1536]{1,0:T(8,128)(2,1)} %pad_maximum_fusion.8), channel_id=1, source_target_pairs={{0,2},{1,3},{2,4},{3,5},{4,6},{5,7},{6,0},{7,1},{8,10},{9,11},{10,... | collective-permute-start | bytes 2359304 | tf_op jit(solution)/shard_map/ppermute | solution.py:514
  (94 other events, 1158.2 us)
Sparse Core Ops, SparseCore 0:
  10.5 42.9 all-gather.5
  55.7 77.8 all-gather.9
  135.8 59.7 all-gather.7
  261.2 125.7 reduce-scatter.1

commit v3 on v2

--- a/solution.py
+++ b/solution.py
@@ -94,6 +94,23 @@
     return [paired_rows(v) for v in new[:3]] + [v.transpose(0, 2, 1) for v in new[3:]]
 
 
+def proj_kernel(g_ref, *refs):
+    olds, news = refs[:3], refs[3:]
+    gradient = g_ref[:, PAIR : 2 * PAIR].astype(F32).T[HEAD_SIZE:]
+    weight, first, second = (ref[...] for ref in olds)
+    results = adamw(weight, gradient, first, second, RATE_WIDE, DECAY_RATE)
+    for ref, result in zip(news, results):
+        ref[...] = result
+
+
+def update_proj(sums, *states):
+    return pl.pallas_call(
+        proj_kernel,
+        out_shape=[jax.ShapeDtypeStruct((SPAN, STORED), F32)] * 3,
+        name="update_proj",
+    )(sums, *states)
+
+
 def inv_rms(values):
     return lax.rsqrt(jnp.mean(values * values, axis=-1, keepdims=True) + NORM_EPS)
 
@@ -155,7 +172,7 @@
 
 def attend_kernel(order_ref, doc_row_ref, doc_col_ref, *refs):
     normed_ref, qkv_ref, att_ref, lse_ref, near_ref, far_ref = refs[-6:]
-    pieces, w_ref = refs[:8], refs[8]
+    pieces, w_ref = refs[:2], refs[2]
     for block, (ref, start) in enumerate(row_blocks(pieces)):
         normed_ref[place(order_ref, block), :] = ref[start : start + ROWS, :]
     for tile in range(GROUP // QUERY_TILE):
@@ -308,7 +325,7 @@
     )(order, spread, doc_row, doc_col, gain, small, weights, normed, qkv, att, lse, *pieces)
 
 
-def moe_kernel(first_ref, router_ref, w_ref, *refs, begin, count, more):
+def moe_kernel(first_ref, router_ref, stored_ref, *refs, begin, count, more):
     sources, refs = (refs[:4], refs[4:8]), refs[8:]
     if more:
         prev_out_ref, prev_dn_ref = refs[:2]
@@ -317,7 +334,8 @@
     else:
         out_ref, dn_ref = refs[:2]
         refs = refs[2:]
-    g_ref, in_all, dout_all, hid_all, dgu_all, held_t, held_c, sems, done, done_sems = refs
+    g_ref, in_all, dout_all, hid_all, dgu_all, held_t, held_c, sems, done, done_sems = refs[:10]
+    w_ref, w_sems = refs[10:]
     step = pl.program_id(0)
     pairs = TILE // PAIR
     height = pairs * SLOTS
@@ -331,12 +349,18 @@
             for kind, held in enumerate((held_t, held_c))
         ]
 
+    def fetch(e):
+        return pltpu.make_async_copy(stored_ref.at[:, e], w_ref.at[:, e], w_sems.at[e])
+
     for tile in range(last + 1):
 
         @pl.when(step == max(tile - 1, 0))
         def _():
             for copy in copies(tile):
                 copy.start()
+            if tile == 0:
+                for e in range(count):
+                    fetch(e).start()
 
     for tile in range(last + 1):
 
@@ -389,6 +413,11 @@
     lane = lax.broadcasted_iota(jnp.int32, (height, EXTRA), 1)
     for e in range(count):
         part = slice(e * SLOTS, (e + 1) * SLOTS)
+
+        @pl.when(step == 0)
+        def _():
+            fetch(e).wait()
+
         rows_in = jnp.concatenate([v[part] for v in ins], axis=0)
         rows_cot = jnp.concatenate([v[part] for v in cots], axis=0)
         gate = jnp.concatenate([v[e] for v in slot_gates], axis=0)
@@ -472,7 +501,6 @@
         sides = (lambda i: (jnp.minimum(i, 1), 0)), (lambda i: (jnp.maximum(i - 2, 0), 0))
         sums = [pl.BlockSpec((TILE, w), side) for side in sides for w in (MODEL, MODEL + EXTRA)]
         shapes = [(PLANE // 2, MODEL), (PLANE // 2, MODEL + EXTRA)] * 2
-    whole = pl.BlockSpec((8, count, 192, 3 * FF_DEV), lambda i: (0, 0, 0, 0), pipeline_mode=pl.Buffered(1))
     flops = 2 * count * height * MODEL * (9 * FF_DEV + 5 * PAIR)
     return pl.pallas_call(
         functools.partial(moe_kernel, begin=begin, count=count, more=previous is not None),
@@ -480,7 +508,7 @@
         in_specs=[
             smem_spec(),
             pl.BlockSpec((EXPERTS, MODEL), lambda i: (0, 0)),
-            whole,
+            pl.BlockSpec(memory_space=pl.ANY),
         ]
         + [pl.BlockSpec(memory_space=pl.ANY)] * 8
         + ([wide, wider, pl.BlockSpec(memory_space=pl.ANY)] if previous is not None else []),
@@ -500,6 +528,8 @@
             pltpu.SemaphoreType.DMA((2, 2)),
             pltpu.VMEM((2, 8, STORED, 3 * FF_DEV), BF16),
             pltpu.SemaphoreType.DMA((2,)),
+            pltpu.VMEM((8, count, STORED, 3 * FF_DEV), BF16),
+            pltpu.SemaphoreType.DMA((count,)),
         ],
         compiler_params=pltpu.CompilerParams(vmem_limit_bytes=VMEM_LIMIT),
         cost_estimate=pl.CostEstimate(
@@ -544,6 +574,13 @@
 
 def spread_col(value):
     return [value] + [across_col(value, d) for d in (1, 2, 3)]
+
+
+def relay_col(value):
+    ahead, behind = across_col(value, 1), across_col(value, -1)
+    half = value.shape[0] // 2
+    opposite = [across_col(ahead[:half], 1), across_col(behind[half:], -1)]
+    return [value, ahead, jnp.concatenate(opposite, axis=0), behind]
 
 
 def gather_col(value):
@@ -613,8 +650,9 @@
     inverse_one = inv_rms(residual_in)
     normed_one = (residual_in * inverse_one * norm_gains[0]).astype(BF16)
     attn_w = jnp.concatenate([projection_weight[:, 0, :], w_proj.T], axis=1).astype(BF16)
-    normed_near = spread_col(normed_one)
-    normed_pieces = normed_near + [other_core(v) for v in normed_near]
+    normed_near = relay_col(normed_one)
+    normed_near = jnp.concatenate(normed_near, axis=0)
+    normed_pieces = [normed_near, other_core(normed_near)]
     attn_full = lax.all_gather(attn_w, "dp", axis=0, tiled=True)
 
     gate_up_w, down_w = after((w_gate_up, w_down), attn_w, normed_one)
@@ -628,9 +666,9 @@
     tagged = jnp.concatenate(
         [cotangent, routes.astype(BF16), jnp.zeros((ROWS, EXTRA - routes.shape[1]), BF16)], axis=1
     )
-    cots = [jnp.concatenate(spread_col(tagged), axis=0)]
+    cots = [jnp.concatenate(relay_col(tagged), axis=0)]
     theirs = other_row(tagged)
-    cots.append(jnp.concatenate(spread_col(theirs), axis=0))
+    cots.append(jnp.concatenate(relay_col(theirs), axis=0))
     attn_full = after(attn_full, normed_pieces, cots)
     normed_full, qkv, att, lse, near, far = attend(
         order, doc_row, doc_col, normed_pieces, attn_full
@@ -646,7 +684,7 @@
     normed_two = (residual * inverse_two * norm_gains[1]).astype(BF16)
     normed_two = after(normed_two, cots)
     rows_all = [
-        jnp.concatenate(spread_col(v), axis=0) for v in (normed_two, other_row(normed_two))
+        jnp.concatenate(relay_col(v), axis=0) for v in (normed_two, other_row(normed_two))
     ]
     rows_all = rows_all + [other_core(v) for v in rows_all]
     logits = jnp.dot(normed_two, router_low, preferred_element_type=F32)
@@ -707,35 +745,37 @@
     small = total([far[GROUP // 2 :], theirs[GROUP // 2 :]]).astype(BF16)
     moved = [across_col(jnp.concatenate([blocks[d], small], axis=0), -d) for d in (1, 2, 3)]
     attn_moved = other_y(after(attn_grads[1], blocks))
-    moved, attn_moved = lax.optimization_barrier((moved, attn_moved))
+    moved, = lax.optimization_barrier((moved,))
+    attn_moved = after(attn_moved, moved)
     mix_moved = collect_col(after(mix_blocks, moved))
-    smalls = jnp.stack([small] + [v[ROWS:] for v in moved])[jnp.remainder(steps - across, 4)]
-    small = total([smalls[d] for d in range(4)]).astype(BF16).reshape(-1, 2 * PAIR)
+    pairs = total([small, moved[1][ROWS:]]), total([moved[0][ROWS:], moved[2][ROWS:]])
+    small = (pairs[0] + pairs[1]).astype(BF16).reshape(-1, 2 * PAIR)
     dnormed = total([blocks[0]] + [v[:ROWS] for v in moved])
     dtokens_norm, _ = norm_back(residual_in, inverse_one, norm_gains[0], dnormed)
     dtokens = dresidual + dtokens_norm
     halves = total([attn_grads[0], attn_moved]).astype(BF16)
     sent = jnp.concatenate([halves[2:].reshape(-1, 2 * PAIR), small], axis=0)
     kept = jnp.concatenate([halves[:2].reshape(-1, 2 * PAIR), small], axis=0)
-    kept = total([kept, along_z(sent, 2)]).astype(BF16)
+    experts_new = update_experts(
+        expert_sum, (w_gate_up, gate_up_first, gate_up_second), (w_down, down_first, down_second)
+    )
+    kept = total([kept, after(along_z(sent, 2), experts_new)]).astype(BF16)
     sent = kept[STORED:]
     kept = jnp.concatenate([kept[:STORED], kept[2 * STORED :]], axis=0)
     kept = total([kept, flip_z(sent)]).astype(BF16)
     kept = add_both(kept, other_row)
-    attn_sums = kept[:STORED].astype(F32)
+    attn_sums = kept[:STORED]
     small = add_both(kept[STORED:], other_y)
-    experts_new = update_experts(
-        expert_sum, (w_gate_up, gate_up_first, gate_up_second), (w_down, down_first, down_second)
-    )
-    mix_moved = after(mix_moved, experts_new, dtokens, attn_sums)
+    sum_qkv = attn_sums[:, None, :QKV].astype(F32)
+    proj_new = update_proj(attn_sums, w_proj, proj_first, proj_second)
+    mix_moved = after(mix_moved, dtokens, attn_sums)
     mixed = total(mix_moved)
-    mixture = mixed[:ROWS] + other_row(mixed[ROWS:].astype(BF16)).astype(F32)
+    mix_theirs = after(other_row(mixed[ROWS:].astype(BF16)), proj_new, small)
+    mixture = mixed[:ROWS] + mix_theirs.astype(F32)
     output = (residual + mixture).astype(BF16)
     small = small.reshape(-1, MODEL).astype(F32)
     sum_router = small[:EXPERTS].T
     sum_gains = jnp.stack([small[EXPERTS + 1], small[EXPERTS]])
-    sum_qkv = attn_sums[:, None, :QKV]
-    sum_proj = attn_sums[:, QKV : 2 * PAIR].T
     return (
         output,
         dtokens,
@@ -749,7 +789,7 @@
             RATE_NARROW,
             DECAY_RATE,
         ),
-        *adamw(w_proj, sum_proj, proj_first, proj_second, RATE_WIDE, DECAY_RATE),
+        *proj_new,
         *experts_new,
     )
 

time: 502 us -> 469 us (0.934)
  waiting for transfers between devices: 198 us -> 145 us
  starting transfers between devices: 74.8 us -> 100 us
  local copies, waits for them, and re-layouts: 31.7 us -> 25.1 us
    ppermute x33 -> x38, waiting for transfers between devices: 143 us -> 113 us  [across_col(): return lax.ppermute(value, 'col', pairs)]
    ppermute x5, waiting for transfers between devices: 23.6 us -> 4.64 us  [other_row(): return lax.ppermute(value, 'row', [(0, 1), (1, 0)])]
    ppermute x33 -> x38, starting transfers between devices: 44.7 us -> 61.2 us  [across_col(): return lax.ppermute(value, 'col', pairs)]
    unnamed x134 -> x117, local copies, waits for them, and re-layouts: 21 us -> 13.8 us
    ppermute x1, starting transfers between devices: 14.9 us -> 20.3 us  [along_z(): return lax.ppermute(value, 'dp', pairs)]
    ppermute x1, waiting for transfers between devices: 5.19 us -> 0.01 us  [along_z(): return lax.ppermute(value, 'dp', pairs)]
    ppermute x5, starting transfers between devices: 9.84 us -> 15 us  [other_row(): return lax.ppermute(value, 'row', [(0, 1), (1, 0)])]
    ppermute x16 -> x13, waiting for transfers between devices: 18.3 us -> 17.1 us  [other_core(): return lax.ppermute(value, 'col', [(s, s ^ 1) for s in range(8)])]
  transfers between devices with their start and end apart: 62 -> 64, of which waited for: 29 -> 31; matrix products, arithmetic and copies ran while one was open for 13% -> 13% of each run, Pallas kernels for 19% -> 21%
where the time goes in v3:
time: 469 us; the launch traced here: 462 us
  waiting for transfers between devices  145 us (31%)
  Pallas kernels  134 us (29%)
  starting transfers between devices  100 us (21%)
  other arithmetic  40 us (9%)
  local copies, waits for them, and re-layouts  25.1 us (5%)
  between operations  15.1 us (3%)
    ppermute x38, waiting for transfers between devices, across_col(): return lax.ppermute(value, 'col', pairs)  113 us
    pallas_call x2, Pallas kernels, moe(): pl.pallas_call(functools.partial(moe_kernel, begin=begin, count=count, mo...  85.5 us
    ppermute x38, starting transfers between devices, across_col(): return lax.ppermute(value, 'col', pairs)  61.2 us
    pallas_call x1, Pallas kernels, attend_back(): pl.pallas_call(attend_back_kernel, in_specs=[smem_spec()] * 2 + [vmem_spe...  20.4 us
    ppermute x1, starting transfers between devices, along_z(): return lax.ppermute(value, 'dp', pairs)  20.3 us
    ppermute x13, waiting for transfers between devices, other_core(): return lax.ppermute(value, 'col', [(s, s ^ 1) for s in range(8)])  17.1 us
    pallas_call x1, Pallas kernels, attend(): pl.pallas_call(attend_kernel, in_specs=[smem_spec()] + [vmem_spec()] * (3...  15.7 us
    ppermute x5, starting transfers between devices, other_row(): return lax.ppermute(value, 'row', [(0, 1), (1, 0)])  15 us
  transfers between devices with their start and end apart: 64, of which 31 were waited for; matrix products, arithmetic and copies ran while one was open for 13% of the time, Pallas kernels for 21%

profile of v3, /device:TPU:32, one launch (start us, length us, event | category | flops | bytes accessed | tf_op | source)
XLA Modules:
  0.0 461.7 jit_solution(7899069142376098942)
XLA Ops:
  50.7 6.4 %collective-permute-done.10 = bf16[128,1664]{1,0:T(8,128)(2,1)S(1)} collective-permute-done((bf16[128,1664]{1,0:T(8,128)(2,1)}, bf16[128,1664]{1,0:T(8,128)(2,1)S(1)}, u32[]{:S(2)}, u32[]{:S(2)}) %collective-permute-start.10) | collective-permute-done | bytes 426016 | tf_op jit(solution)/shard_map/ppermute | solution.py:544
  64.5 15.7 %attend.1 = (bf16[1024,1536]{1,0:T(8,128)(2,1)}, bf16[1024,320]{1,0:T(8,128)(2,1)}, bf16[1024,256]{1,0:T(8,128)(2,1)}, f32[8,1024]{1,0:T(8,128)}, bf16[512,1536]{1,0:T(8,128)(2,1)}, /*index=5*/bf16[512,1536]{1,0:T(8,128)(2,1)}) custom-call(s32[8]{0:T(128)} %pad_add_fusion.order_ref, s32[1,1024]{1,0:T(1,128)} %bitcast.97, s32[1024,1]{1,0:T(8,128)} %copy.104.doc_col_ref, ...), custom_call_target="tpu_custom_call" | custom-call | flops 1000000 | bytes 100000 | tf_op jit(solution)/shard_map/attend/pallas_call | solution.py:283
  85.4 3.7 collective-permute-start.15
  90.1 16.1 %collective-permute-done.15 = bf16[128,1536]{1,0:T(8,128)(2,1)S(1)} collective-permute-done((bf16[128,1536]{1,0:T(8,128)(2,1)S(1)}, bf16[128,1536]{1,0:T(8,128)(2,1)S(1)}, u32[]{:S(2)}, u32[]{:S(2)}) %collective-permute-start.15) | collective-permute-done | bytes 393248 | tf_op jit(solution)/shard_map/ppermute | solution.py:544
  118.6 4.8 %collective-permute-done.20 = bf16[128,1536]{1,0:T(8,128)(2,1)S(1)} collective-permute-done((bf16[128,1536]{1,0:T(8,128)(2,1)S(1)}, bf16[128,1536]{1,0:T(8,128)(2,1)S(1)}, u32[]{:S(2)}, u32[]{:S(2)}) %collective-permute-start.20) | collective-permute-done | bytes 393248 | tf_op jit(solution)/shard_map/ppermute | solution.py:544
  134.0 4.7 %collective-permute-done.25 = bf16[128,1536]{1,0:T(8,128)(2,1)S(1)} collective-permute-done((bf16[128,1536]{1,0:T(8,128)(2,1)S(1)}, bf16[128,1536]{1,0:T(8,128)(2,1)S(1)}, u32[]{:S(2)}, u32[]{:S(2)}) %collective-permute-start.25) | collective-permute-done | bytes 393248 | tf_op jit(solution)/shard_map/ppermute | solution.py:544
  142.2 3.5 collective-permute-done.26
  149.4 47.5 %moe.2 = (bf16[2048,1536]{1,0:T(8,128)(2,1)}, bf16[2048,1664]{1,0:T(8,128)(2,1)}, bf16[8,5,192,768]{3,2,1,0:T(8,128)(2,1)}) custom-call(s32[1]{0:T(128)} %bitcast.6.first_ref, bf16[40,1536]{1,0:T(8,128)(2,1)} %fusion.19.router_ref, bf16[8,3,192,768]{3,2,1,0:T(8,128)(2,1)} %bitcast.84, bf16[512,1536]{1,0:T(8,128)(2,1)} %constant_dynamic-update-slice_fusion.15.refs_0_, ...), custom_call_target="tpu_custom_call" | custom-call | flops 1000000 | bytes 100000 | tf_op jit(solution)/shard_map/moe/pallas_call | solution.py:505
  196.9 3.6 all-gather.8.cloned.1.call-done
  200.6 38.0 %moe.3 = (bf16[1024,1536]{1,0:T(8,128)(2,1)}, bf16[1024,1664]{1,0:T(8,128)(2,1)}, bf16[1024,1536]{1,0:T(8,128)(2,1)}, bf16[1024,1664]{1,0:T(8,128)(2,1)}, bf16[8,5,192,768]{3,2,1,0:T(8,128)(2,1)}) custom-call(s32[1]{0:T(128)} %bitcast.6.first_ref, bf16[40,1536]{1,0:T(8,128)(2,1)} %fusion.19.router_ref, ...), custom_call_target="tpu_custom_call", output_to_operand_aliasing={{4}: (13, {})} | custom-call | flops 1000000 | bytes 100000 | tf_op jit(solution)/shard_map/moe/pallas_call | solution.py:505
  238.7 6.2 %collective-permute-done.31 = bf16[1024,1664]{1,0:T(8,128)(2,1)S(1)} collective-permute-done((bf16[1024,1664]{1,0:T(8,128)(2,1)}, bf16[1024,1664]{1,0:T(8,128)(2,1)S(1)}, u32[]{:S(2)}, u32[]{:S(2)}) %collective-permute-start.31) | collective-permute-done | bytes 3407904 | tf_op jit(solution)/shard_map/ppermute | solution.py:548
  255.2 14.3 %collective-permute-done.36 = bf16[128,1664]{1,0:T(8,128)(2,1)S(1)} collective-permute-done((bf16[128,1664]{1,0:T(8,128)(2,1)S(1)}, bf16[128,1664]{1,0:T(8,128)(2,1)S(1)}, u32[]{:S(2)}, u32[]{:S(2)}) %collective-permute-start.36) | collective-permute-done | bytes 426016 | tf_op jit(solution)/shard_map/ppermute | solution.py:544
  269.5 4.7 %collective-permute-start.35 = (bf16[128,1664]{1,0:T(8,128)(2,1)S(1)}, bf16[128,1664]{1,0:T(8,128)(2,1)S(1)}, u32[]{:S(2)}, u32[]{:S(2)}) collective-permute-start(bf16[128,1664]{1,0:T(8,128)(2,1)S(1)} %get-tuple-element.237), channel_id=1, source_target_pairs={{0,2},{1,3},{2,4},{3,5},{4,6},{5,7},{6,0},{7,1},{8,10},{9,11},{10,... | collective-permute-start | bytes 1277960 | tf_op jit(solution)/shard_map/ppermute | solution.py:544
  283.3 4.0 collective-permute-done.33
  287.4 3.7 collective-permute-done.35
  298.5 15.2 %collective-permute-done.40.refs_1_ = bf16[128,1536]{1,0:T(8,128)(2,1)} collective-permute-done((bf16[128,1536]{1,0:T(8,128)(2,1)S(1)}, bf16[128,1536]{1,0:T(8,128)(2,1)}, u32[]{:S(2)}, u32[]{:S(2)}) %collective-permute-start.40) | collective-permute-done | bytes 393248 | tf_op jit(solution)/shard_map/ppermute | solution.py:544
  316.9 20.4 %attend_back.1 = (bf16[512,1536]{1,0:T(8,128)(2,1)}, bf16[560,1536]{1,0:T(8,128)(2,1)}, bf16[4,192,512]{2,1,0:T(8,128)(2,1)}, bf16[4,192,512]{2,1,0:T(8,128)(2,1)}) custom-call(s32[8]{0:T(128)} %pad_add_fusion.order_ref, s32[8]{0:T(128)} %iota_xor_fusion.spread_ref, s32[1,1024]{1,0:T(1,128)} %bitcast.98, s32[1024,1]{1,0:T(8,128)} %copy.104.doc_col_ref, ...), custom_call_target="tpu_custom_call" | custom-call | flops 1000000 | bytes 100000 | tf_op jit(solution)/shard_map/attend_back/pallas_call | solution.py:304
  337.4 3.7 collective-permute-done.47
  348.6 21.0 %collective-permute-done.48 = bf16[176,1536]{1,0:T(8,128)(2,1)S(1)} collective-permute-done((bf16[176,1536]{1,0:T(8,128)(2,1)S(1)}, bf16[176,1536]{1,0:T(8,128)(2,1)S(1)}, u32[]{:S(2)}, u32[]{:S(2)}) %collective-permute-start.48) | collective-permute-done | bytes 540704 | tf_op jit(solution)/shard_map/ppermute | solution.py:544
  377.2 20.3 %collective-permute-start.55 = (bf16[528,512]{1,0:T(8,128)(2,1)}, bf16[528,512]{1,0:T(8,128)(2,1)}, u32[]{:S(2)}, u32[]{:S(2)}) collective-permute-start(bf16[528,512]{1,0:T(8,128)(2,1)} %pad_maximum_fusion.8), channel_id=1, source_target_pairs={{0,32},{16,48},{32,0},{48,16},{64,96},{80,112},{96,64},{112,80},{1... | collective-permute-start | bytes 1622024 | tf_op jit(solution)/shard_map/ppermute | solution.py:557
  401.9 9.9 %update_experts.1 = (f32[3840,128]{1,0:T(8,128)}, f32[3840,128]{1,0:T(8,128)}, f32[3840,128]{1,0:T(8,128)}, f32[5,192,256]{2,1,0:T(8,128)}, f32[5,192,256]{2,1,0:T(8,128)}, /*index=5*/f32[5,192,256]{2,1,0:T(8,128)}) custom-call(bf16[5,192,768]{2,1,0:T(8,128)(2,1)} %bitcast.91, f32[3840,128]{1,0:T(8,128)} %bitcast.83, f32[3840,128]{1,0:T(8,128)} %bitcast.87, ...), custom_call_target="tpu_custom_call" | custom-call | flops 20000000 | bytes 20000000 | tf_op jit(solution)/shard_map/update_experts/pallas_call | solution.py:83
  415.1 6.6 %collective-permute-done.56 = bf16[336,512]{1,0:T(8,128)(2,1)S(1)} collective-permute-done((bf16[336,512]{1,0:T(8,128)(2,1)S(1)}, bf16[336,512]{1,0:T(8,128)(2,1)S(1)}, u32[]{:S(2)}, u32[]{:S(2)}) %collective-permute-start.56) | collective-permute-done | bytes 344096 | tf_op jit(solution)/shard_map/ppermute | solution.py:607
  427.1 3.9 collective-permute-done.57
  433.7 3.7 collective-permute-done.53
  (321 shorter events, 164.9 us)
Async XLA Ops:
  7.2 57.3 %all-gather.6.cloned.1.call-start = ((), (), s32[]{:S(2)}) async-start(), calls=%async_computation.1 | async-start | bytes 1769472 | tf_op jit(solution)/shard_map/all_gather | solution.py:656
  10.2 139.2 %all-gather.10.cloned.1.call-start = ((), (), s32[]{:S(2)}) async-start(), calls=%async_computation.4 | async-start | bytes 7962624 | tf_op jit(solution)/shard_map/all_gather | solution.py:664
  17.7 182.8 %all-gather.8.cloned.1.call-start = ((), (), s32[]{:S(2)}) async-start(), calls=%async_computation.3 | async-start | bytes 5308416 | tf_op jit(solution)/shard_map/all_gather | solution.py:664
  21.3 22.5 %collective-permute-start.9 = (bf16[128,1664]{1,0:T(8,128)(2,1)S(1)}, bf16[128,1664]{1,0:T(8,128)(2,1)}, u32[]{:S(2)}, u32[]{:S(2)}) collective-permute-start(bf16[128,1664]{1,0:T(8,128)(2,1)S(1)} %concatenate.73), channel_id=1, source_target_pairs={{0,8},{8,0},{1,9},{9,1},{2,10},{10,2},{3,11},{11,3},{4,12},{12,4},... | collective-permute-start | bytes 1277960 | tf_op jit(solution)/shard_map/ppermute | solution.py:552
  28.7 373.2 %reduce-scatter.2.cloned.1.call-start = ((), (), s32[]{:S(2)}) async-start(), calls=%async_computation.2 | async-start | bytes 13271040 | tf_op jit(solution)/shard_map/reduce_scatter | solution.py:700
  80.3 31.0 %collective-permute-start.18 = (bf16[512,1664]{1,0:T(8,128)(2,1)}, bf16[512,1664]{1,0:T(8,128)(2,1)S(1)}, u32[]{:S(2)}, u32[]{:S(2)}) collective-permute-start(bf16[512,1664]{1,0:T(8,128)(2,1)} %copy-done.2), channel_id=1, source_target_pairs={{0,1},{1,0},{2,3},{3,2},{4,5},{5,4},{6,7},{7,6},{8,9},{9,8},{10,11... | collective-permute-start | bytes 5111816 | tf_op jit(solution)/shard_map/ppermute | solution.py:548
  80.8 30.5 %collective-permute-start.19 = (bf16[512,1664]{1,0:T(8,128)(2,1)S(1)}, bf16[512,1664]{1,0:T(8,128)(2,1)S(1)}, u32[]{:S(2)}, u32[]{:S(2)}) collective-permute-start(bf16[512,1664]{1,0:T(8,128)(2,1)S(1)} %constant_dynamic-update-slice_fusion.10.refs_5_), channel_id=1, source_target_pairs={{0,1},{1,0},{2,3},{3,2},{4,5},{5,4},{6,7},{7,6},{8,9},{9,8},{10,11... | collective-permute-start | bytes 5111816 | tf_op jit(solution)/shard_map/ppermute | solution.py:548
  85.4 20.8 %collective-permute-start.15 = (bf16[128,1536]{1,0:T(8,128)(2,1)S(1)}, bf16[128,1536]{1,0:T(8,128)(2,1)S(1)}, u32[]{:S(2)}, u32[]{:S(2)}) collective-permute-start(bf16[128,1536]{1,0:T(8,128)(2,1)S(1)} %get-tuple-element.255), channel_id=1, source_target_pairs={{0,6},{1,7},{2,0},{3,1},{4,2},{5,3},{6,4},{7,5},{8,14},{9,15},{10,... | collective-permute-start | bytes 1179656 | tf_op jit(solution)/shard_map/ppermute | solution.py:544
  89.2 20.5 %collective-permute-start.17 = (bf16[128,1536]{1,0:T(8,128)(2,1)S(1)}, bf16[128,1536]{1,0:T(8,128)(2,1)S(1)}, u32[]{:S(2)}, u32[]{:S(2)}) collective-permute-start(bf16[128,1536]{1,0:T(8,128)(2,1)S(1)} %get-tuple-element.256), channel_id=1, source_target_pairs={{0,2},{1,3},{2,4},{3,5},{4,6},{5,7},{6,0},{7,1},{8,10},{9,11},{10,... | collective-permute-start | bytes 1179656 | tf_op jit(solution)/shard_map/ppermute | solution.py:544
  244.9 33.7 %collective-permute-start.32 = (bf16[1024,1536]{1,0:T(8,128)(2,1)}, bf16[1024,1536]{1,0:T(8,128)(2,1)S(1)}, u32[]{:S(2)}, u32[]{:S(2)}) collective-permute-start(bf16[1024,1536]{1,0:T(8,128)(2,1)} %get-tuple-element.91), channel_id=1, source_target_pairs={{0,1},{1,0},{2,3},{3,2},{4,5},{5,4},{6,7},{7,6},{8,9},{9,8},{10,11... | collective-permute-start | bytes 9437192 | tf_op jit(solution)/shard_map/ppermute | solution.py:548
  247.6 21.9 %collective-permute-start.36 = (bf16[128,1664]{1,0:T(8,128)(2,1)S(1)}, bf16[128,1664]{1,0:T(8,128)(2,1)S(1)}, u32[]{:S(2)}, u32[]{:S(2)}) collective-permute-start(bf16[128,1664]{1,0:T(8,128)(2,1)S(1)} %get-tuple-element.240), channel_id=1, source_target_pairs={{0,6},{1,7},{2,0},{3,1},{4,2},{5,3},{6,4},{7,5},{8,14},{9,15},{10,... | collective-permute-start | bytes 1277960 | tf_op jit(solution)/shard_map/ppermute | solution.py:544
  251.2 23.0 %collective-permute-start.38 = (bf16[128,1664]{1,0:T(8,128)(2,1)S(1)}, bf16[128,1664]{1,0:T(8,128)(2,1)S(1)}, u32[]{:S(2)}, u32[]{:S(2)}) collective-permute-start(bf16[128,1664]{1,0:T(8,128)(2,1)S(1)} %get-tuple-element.238), channel_id=1, source_target_pairs={{0,2},{1,3},{2,4},{3,5},{4,6},{5,7},{6,0},{7,1},{8,10},{9,11},{10,... | collective-permute-start | bytes 1277960 | tf_op jit(solution)/shard_map/ppermute | solution.py:544
  252.8 34.6 %collective-permute-start.33 = (bf16[128,1664]{1,0:T(8,128)(2,1)S(1)}, bf16[128,1664]{1,0:T(8,128)(2,1)S(1)}, u32[]{:S(2)}, u32[]{:S(2)}) collective-permute-start(bf16[128,1664]{1,0:T(8,128)(2,1)S(1)} %get-tuple-element.242), channel_id=1, source_target_pairs={{0,6},{1,7},{2,0},{3,1},{4,2},{5,3},{6,4},{7,5},{8,14},{9,15},{10,... | collective-permute-start | bytes 1277960 | tf_op jit(solution)/shard_map/ppermute | solution.py:544
  269.5 21.5 %collective-permute-start.35 = (bf16[128,1664]{1,0:T(8,128)(2,1)S(1)}, bf16[128,1664]{1,0:T(8,128)(2,1)S(1)}, u32[]{:S(2)}, u32[]{:S(2)}) collective-permute-start(bf16[128,1664]{1,0:T(8,128)(2,1)S(1)} %get-tuple-element.237), channel_id=1, source_target_pairs={{0,2},{1,3},{2,4},{3,5},{4,6},{5,7},{6,0},{7,1},{8,10},{9,11},{10,... | collective-permute-start | bytes 1277960 | tf_op jit(solution)/shard_map/ppermute | solution.py:544
  292.9 20.8 %collective-permute-start.40 = (bf16[128,1536]{1,0:T(8,128)(2,1)S(1)}, bf16[128,1536]{1,0:T(8,128)(2,1)}, u32[]{:S(2)}, u32[]{:S(2)}) collective-permute-start(bf16[128,1536]{1,0:T(8,128)(2,1)S(1)} %fusion.30.refs_0_), channel_id=1, source_target_pairs={{0,2},{1,3},{2,4},{3,5},{4,6},{5,7},{6,0},{7,1},{8,10},{9,11},{10,... | collective-permute-start | bytes 1179656 | tf_op jit(solution)/shard_map/ppermute | solution.py:544
  293.0 20.7 %collective-permute-start.41 = (bf16[128,1536]{1,0:T(8,128)(2,1)S(1)}, bf16[128,1536]{1,0:T(8,128)(2,1)}, u32[]{:S(2)}, u32[]{:S(2)}) collective-permute-start(bf16[128,1536]{1,0:T(8,128)(2,1)S(1)} %fusion.30.refs_0_), channel_id=1, source_target_pairs={{0,4},{1,5},{2,6},{3,7},{4,0},{5,1},{6,2},{7,3},{8,12},{9,13},{10,... | collective-permute-start | bytes 1179656 | tf_op jit(solution)/shard_map/ppermute | solution.py:544
  343.9 25.7 %collective-permute-start.48 = (bf16[176,1536]{1,0:T(8,128)(2,1)S(1)}, bf16[176,1536]{1,0:T(8,128)(2,1)S(1)}, u32[]{:S(2)}, u32[]{:S(2)}) collective-permute-start(bf16[176,1536]{1,0:T(8,128)(2,1)S(1)} %get-tuple-element.264), channel_id=1, source_target_pairs={{0,6},{1,7},{2,0},{3,1},{4,2},{5,3},{6,4},{7,5},{8,14},{9,15},{10,... | collective-permute-start | bytes 1622024 | tf_op jit(solution)/shard_map/ppermute | solution.py:544
  346.2 23.4 %collective-permute-start.49 = (bf16[176,1536]{1,0:T(8,128)(2,1)S(1)}, bf16[176,1536]{1,0:T(8,128)(2,1)S(1)}, u32[]{:S(2)}, u32[]{:S(2)}) collective-permute-start(bf16[176,1536]{1,0:T(8,128)(2,1)S(1)} %get-tuple-element.263), channel_id=1, source_target_pairs={{0,4},{1,5},{2,6},{3,7},{4,0},{5,1},{6,2},{7,3},{8,12},{9,13},{10,... | collective-permute-start | bytes 1622024 | tf_op jit(solution)/shard_map/ppermute | solution.py:544
  346.2 26.8 %collective-permute-start.50 = (bf16[176,1536]{1,0:T(8,128)(2,1)S(1)}, bf16[176,1536]{1,0:T(8,128)(2,1)S(1)}, u32[]{:S(2)}, u32[]{:S(2)}) collective-permute-start(bf16[176,1536]{1,0:T(8,128)(2,1)S(1)} %get-tuple-element.262), channel_id=1, source_target_pairs={{0,2},{1,3},{2,4},{3,5},{4,6},{5,7},{6,0},{7,1},{8,10},{9,11},{10,... | collective-permute-start | bytes 1622024 | tf_op jit(solution)/shard_map/ppermute | solution.py:544
  347.1 27.5 %collective-permute-start.54 = (bf16[4,192,512]{2,1,0:T(8,128)(2,1)}, bf16[4,192,512]{2,1,0:T(8,128)(2,1)}, u32[]{:S(2)}, u32[]{:S(2)}) collective-permute-start(bf16[4,192,512]{2,1,0:T(8,128)(2,1)} %get-tuple-element.120), channel_id=1, source_target_pairs={{0,64},{16,80},{32,96},{48,112},{64,0},{80,16},{96,32},{112,48},{1... | collective-permute-start | bytes 2359304 | tf_op jit(solution)/shard_map/ppermute | solution.py:561
  377.2 34.6 %collective-permute-start.55 = (bf16[528,512]{1,0:T(8,128)(2,1)}, bf16[528,512]{1,0:T(8,128)(2,1)}, u32[]{:S(2)}, u32[]{:S(2)}) collective-permute-start(bf16[528,512]{1,0:T(8,128)(2,1)} %pad_maximum_fusion.8), channel_id=1, source_target_pairs={{0,32},{16,48},{32,0},{48,16},{64,96},{80,112},{96,64},{112,80},{1... | collective-permute-start | bytes 1622024 | tf_op jit(solution)/shard_map/ppermute | solution.py:557
  397.5 36.2 %collective-permute-start.51 = (bf16[256,1536]{1,0:T(8,128)(2,1)}, bf16[256,1536]{1,0:T(8,128)(2,1)}, u32[]{:S(2)}, u32[]{:S(2)}) collective-permute-start(bf16[256,1536]{1,0:T(8,128)(2,1)} %pad_maximum_fusion.5), channel_id=1, source_target_pairs={{0,6},{1,7},{2,0},{3,1},{4,2},{5,3},{6,4},{7,5},{8,14},{9,15},{10,... | collective-permute-start | bytes 2359304 | tf_op jit(solution)/shard_map/ppermute | solution.py:544
  400.2 33.5 %collective-permute-start.52 = (bf16[256,1536]{1,0:T(8,128)(2,1)}, bf16[256,1536]{1,0:T(8,128)(2,1)}, u32[]{:S(2)}, u32[]{:S(2)}) collective-permute-start(bf16[256,1536]{1,0:T(8,128)(2,1)} %pad_maximum_fusion.6), channel_id=1, source_target_pairs={{0,4},{1,5},{2,6},{3,7},{4,0},{5,1},{6,2},{7,3},{8,12},{9,13},{10,... | collective-permute-start | bytes 2359304 | tf_op jit(solution)/shard_map/ppermute | solution.py:544
  401.0 36.4 %collective-permute-start.53 = (bf16[256,1536]{1,0:T(8,128)(2,1)}, bf16[256,1536]{1,0:T(8,128)(2,1)}, u32[]{:S(2)}, u32[]{:S(2)}) collective-permute-start(bf16[256,1536]{1,0:T(8,128)(2,1)} %pad_maximum_fusion.7), channel_id=1, source_target_pairs={{0,2},{1,3},{2,4},{3,5},{4,6},{5,7},{6,0},{7,1},{8,10},{9,11},{10,... | collective-permute-start | bytes 2359304 | tf_op jit(solution)/shard_map/ppermute | solution.py:544
  (85 other events, 970.4 us)
Sparse Core Ops, SparseCore 0:
  10.4 42.7 all-gather.5
  55.4 79.1 all-gather.9
  136.8 63.6 all-gather.7
  238.7 130.7 reduce-scatter.1

commit v4 on v3

--- a/solution.py
+++ b/solution.py
@@ -24,7 +24,7 @@
 SLOTS = 112
 TILE = 512
 PAIR = 256
-QUERY_TILE = 256
+QUERY_TILE = 512
 EXTRA = 128
 SMALL = 48
 CHUNKS = ((0, 3), (3, 2))
@@ -60,7 +60,7 @@
     olds, news = refs[:6], refs[6:]
     for half in range(FF_DEV // 128):
         for kind in range(2):
-            at = pl.ds(2 * half + kind, STORED, stride=4)
+            at = pl.ds(2 * half + kind, STORED // 2, stride=4)
             start = kind * FF_DEV + half * 128
             gradient = g_ref[0, :, start : start + 128].astype(F32)
             weight, first, second = (ref[at, :] for ref in olds[:3])
@@ -75,15 +75,15 @@
 
 
 def update_experts(gradient, gate_up, down):
-    pair_rows = pl.BlockSpec((4 * STORED, 128), lambda i: (i, 0))
-    down_rows = pl.BlockSpec((1, STORED, FF_DEV), lambda i: (i, 0, 0))
+    pair_rows = pl.BlockSpec((2 * STORED, 128), lambda e, i: (2 * e + i, 0))
+    down_rows = pl.BlockSpec((1, STORED // 2, FF_DEV), lambda e, i: (e, i, 0))
     specs = [pair_rows] * 3 + [down_rows] * 3
     pair_shape = jax.ShapeDtypeStruct((EXPERTS_DEV * 4 * STORED, 128), F32)
     down_shape = jax.ShapeDtypeStruct((EXPERTS_DEV, STORED, FF_DEV), F32)
     new = pl.pallas_call(
         adamw_kernel,
-        grid=(EXPERTS_DEV,),
-        in_specs=[pl.BlockSpec((1, STORED, 3 * FF_DEV), lambda i: (i, 0, 0))] + specs,
+        grid=(EXPERTS_DEV, 2),
+        in_specs=[pl.BlockSpec((1, STORED // 2, 3 * FF_DEV), lambda e, i: (e, i, 0))] + specs,
         out_specs=specs,
         out_shape=[pair_shape] * 3 + [down_shape] * 3,
         cost_estimate=pl.CostEstimate(
@@ -197,11 +197,9 @@
             lse_ref[head : head + 1, rows] = peak + jnp.log(total)
         att_ref[rows, :] = jnp.concatenate(outs, axis=0).T.astype(BF16)
     proj = w_ref[:, SPAN + HEAD_SIZE :]
-    for block in range(GROUP // ROWS):
-        part_ref = near_ref if block < 4 else far_ref
-        part_ref[block % 4 * ROWS : (block % 4 + 1) * ROWS, :] = dot_nt(
-            att_ref[place(order_ref, block), :], proj
-        ).astype(BF16)
+    for side, part_ref in enumerate((near_ref, far_ref)):
+        rows = [att_ref[place(order_ref, 4 * side + block), :] for block in range(4)]
+        part_ref[...] = dot_nt(jnp.concatenate(rows, axis=0), proj).astype(BF16)
 
 
 def attend_back_kernel(
@@ -252,12 +250,14 @@
     dqkv_ref[:, SPAN + HEAD_SIZE :] = dkv_ref[:, HEAD_SIZE:].astype(BF16)
     qkv_mat = w_ref[:, :QKV]
     dgain = jnp.zeros((1, MODEL), F32)
-    for block in range(GROUP // ROWS):
-        at = place(order_ref, block)
-        part = dot_nt(dqkv_ref[at, :], qkv_mat)
-        dgain = dgain + jnp.sum(part * normed_ref[at, :].astype(F32), axis=0, keepdims=True)
-        part_ref = near_ref if block < 4 else far_ref
-        part_ref[block % 4 * ROWS : (block % 4 + 1) * ROWS, :] = part.astype(BF16)
+    for side, part_ref in enumerate((near_ref, far_ref)):
+        places = [place(order_ref, 4 * side + block) for block in range(4)]
+        rows = jnp.concatenate([dqkv_ref[at, :] for at in places], axis=0)
+        part = dot_nt(rows, qkv_mat)
+        for block, at in enumerate(places):
+            here = part[block * ROWS : (block + 1) * ROWS] * normed_ref[at, :].astype(F32)
+            dgain = dgain + jnp.sum(here, axis=0, keepdims=True)
+        part_ref[: GROUP // 2, :] = part.astype(BF16)
     small_at = lax.broadcasted_iota(jnp.int32, (SMALL, MODEL), 0)
     small = jnp.where(small_at == EXPERTS + 1, dgain / gain_ref[...], small_ref[...])
     far_ref[GROUP // 2 :, :] = small.astype(BF16)
@@ -425,7 +425,7 @@
         down_w = w_ref[:, e, :, 2 * FF_DEV :].reshape(MODEL, FF_DEV)
         gate_up = dot(rows_in, gate_up_w)
         pre, up = gate_up[:, :FF_DEV], gate_up[:, FF_DEV:]
-        sig = 1.0 / (1.0 + jnp.exp(-pre))
+        sig = 0.5 * jnp.tanh(0.5 * pre) + 0.5
         silu = pre * sig
         hidden = (silu * up).astype(BF16)
         plain = dot(rows_cot, down_w)
@@ -760,6 +760,7 @@
         expert_sum, (w_gate_up, gate_up_first, gate_up_second), (w_down, down_first, down_second)
     )
     kept = total([kept, after(along_z(sent, 2), experts_new)]).astype(BF16)
+    mix_moved = after(mix_moved, kept)
     sent = kept[STORED:]
     kept = jnp.concatenate([kept[:STORED], kept[2 * STORED :]], axis=0)
     kept = total([kept, flip_z(sent)]).astype(BF16)
@@ -768,7 +769,6 @@
     small = add_both(kept[STORED:], other_y)
     sum_qkv = attn_sums[:, None, :QKV].astype(F32)
     proj_new = update_proj(attn_sums, w_proj, proj_first, proj_second)
-    mix_moved = after(mix_moved, dtokens, attn_sums)
     mixed = total(mix_moved)
     mix_theirs = after(other_row(mixed[ROWS:].astype(BF16)), proj_new, small)
     mixture = mixed[:ROWS] + mix_theirs.astype(F32)

time: 469 us -> 479 us (1.021)
  waiting for transfers between devices: 145 us -> 160 us
  starting transfers between devices: 100 us -> 94.8 us
  local copies, waits for them, and re-layouts: 25.1 us -> 30.1 us
    ppermute x38, waiting for transfers between devices: 113 us -> 126 us  [across_col(): return lax.ppermute(value, 'col', pairs)]
    ppermute x1, waiting for transfers between devices: 6.6 us -> 0.01 us  [flip_z(): return lax.ppermute(value, 'dp', [(s, s ^ 1) for s in range(8)])]
    all_gather x2, waiting for transfers between devices: 3.63 us -> 8.57 us  [per_device(): lax.all_gather(expert_w[b:b + n], 'dp', axis=0, tiled=False)]
    unnamed x117 -> x127, local copies, waits for them, and re-layouts: 13.8 us -> 14.8 us
  transfers between devices with their start and end apart: 64 -> 64, of which waited for: 31 -> 30; matrix products, arithmetic and copies ran while one was open for 13% -> 12% of each run, Pallas kernels for 21% -> 20%
where the time goes in v4:
time: 479 us; the launch traced here: 471 us
  waiting for transfers between devices  160 us (33%)
  Pallas kernels  130 us (27%)
  starting transfers between devices  94.8 us (20%)
  other arithmetic  39.4 us (8%)
  local copies, waits for them, and re-layouts  30.1 us (6%)
  between operations  15.1 us (3%)
    ppermute x38, waiting for transfers between devices, across_col(): return lax.ppermute(value, 'col', pairs)  126 us
    pallas_call x2, Pallas kernels, moe(): pl.pallas_call(functools.partial(moe_kernel, begin=begin, count=count, mo...  84.4 us
    ppermute x38, starting transfers between devices, across_col(): return lax.ppermute(value, 'col', pairs)  59.6 us
    pallas_call x1, Pallas kernels, attend_back(): pl.pallas_call(attend_back_kernel, in_specs=[smem_spec()] * 2 + [vmem_spe...  19 us
    ppermute x1, starting transfers between devices, along_z(): return lax.ppermute(value, 'dp', pairs)  17.5 us
    ppermute x13, waiting for transfers between devices, other_core(): return lax.ppermute(value, 'col', [(s, s ^ 1) for s in range(8)])  16.9 us
    unnamed x127, local copies, waits for them, and re-layouts  14.8 us
    ppermute x5, starting transfers between devices, other_row(): return lax.ppermute(value, 'row', [(0, 1), (1, 0)])  13.1 us
  transfers between devices with their start and end apart: 64, of which 30 were waited for; matrix products, arithmetic and copies ran while one was open for 12% of the time, Pallas kernels for 20%

profile of v4, /device:TPU:32, one launch (start us, length us, event | category | flops | bytes accessed | tf_op | source)
XLA Modules:
  0.0 471.3 jit_solution(15047063436083055880)
XLA Ops:
  51.6 6.1 %collective-permute-done.10 = bf16[128,1664]{1,0:T(8,128)(2,1)S(1)} collective-permute-done((bf16[128,1664]{1,0:T(8,128)(2,1)}, bf16[128,1664]{1,0:T(8,128)(2,1)S(1)}, u32[]{:S(2)}, u32[]{:S(2)}) %collective-permute-start.10) | collective-permute-done | bytes 426016 | tf_op jit(solution)/shard_map/ppermute | solution.py:544
  65.0 13.0 %attend.1 = (bf16[1024,1536]{1,0:T(8,128)(2,1)}, bf16[1024,320]{1,0:T(8,128)(2,1)}, bf16[1024,256]{1,0:T(8,128)(2,1)}, f32[8,1024]{1,0:T(8,128)}, bf16[512,1536]{1,0:T(8,128)(2,1)}, /*index=5*/bf16[512,1536]{1,0:T(8,128)(2,1)}) custom-call(s32[8]{0:T(128)} %pad_add_fusion.order_ref, s32[1,1024]{1,0:T(1,128)} %bitcast.97, s32[1024,1]{1,0:T(8,128)} %copy.104.doc_col_ref, ...), custom_call_target="tpu_custom_call" | custom-call | flops 1000000 | bytes 100000 | tf_op jit(solution)/shard_map/attend/pallas_call | solution.py:283
  83.7 4.5 collective-permute-start.16
  88.2 7.9 %collective-permute-done.17 = bf16[128,1536]{1,0:T(8,128)(2,1)S(1)} collective-permute-done((bf16[128,1536]{1,0:T(8,128)(2,1)S(1)}, bf16[128,1536]{1,0:T(8,128)(2,1)S(1)}, u32[]{:S(2)}, u32[]{:S(2)}) %collective-permute-start.17) | collective-permute-done | bytes 393248 | tf_op jit(solution)/shard_map/ppermute | solution.py:544
  96.1 9.6 %collective-permute-done.16 = bf16[128,1536]{1,0:T(8,128)(2,1)S(1)} collective-permute-done((bf16[128,1536]{1,0:T(8,128)(2,1)S(1)}, bf16[128,1536]{1,0:T(8,128)(2,1)S(1)}, u32[]{:S(2)}, u32[]{:S(2)}) %collective-permute-start.16) | collective-permute-done | bytes 393248 | tf_op jit(solution)/shard_map/ppermute | solution.py:544
  114.7 4.3 collective-permute-done.20
  130.1 4.3 collective-permute-done.25
  145.1 46.9 %moe.2 = (bf16[2048,1536]{1,0:T(8,128)(2,1)}, bf16[2048,1664]{1,0:T(8,128)(2,1)}, bf16[8,5,192,768]{3,2,1,0:T(8,128)(2,1)}) custom-call(s32[1]{0:T(128)} %bitcast.6.first_ref, bf16[40,1536]{1,0:T(8,128)(2,1)} %fusion.19.router_ref, bf16[8,3,192,768]{3,2,1,0:T(8,128)(2,1)} %bitcast.84, bf16[512,1536]{1,0:T(8,128)(2,1)} %constant_dynamic-update-slice_fusion.15.refs_0_, ...), custom_call_target="tpu_custom_call" | custom-call | flops 1000000 | bytes 100000 | tf_op jit(solution)/shard_map/moe/pallas_call | solution.py:505
  192.0 8.6 %all-gather.8.cloned.1.call-done = bf16[16,192,768]{2,1,0:T(8,128)(2,1)} async-done(((bf16[2,192,768]{2,1,0:T(8,128)(2,1)}), bf16[16,192,768]{2,1,0:T(8,128)(2,1)}) %all-gather.8.cloned.1.call-update) | async-done | bytes 4718608 | tf_op jit(solution)/shard_map/all_gather | solution.py:664
  200.6 37.5 %moe.3 = (bf16[1024,1536]{1,0:T(8,128)(2,1)}, bf16[1024,1664]{1,0:T(8,128)(2,1)}, bf16[1024,1536]{1,0:T(8,128)(2,1)}, bf16[1024,1664]{1,0:T(8,128)(2,1)}, bf16[8,5,192,768]{3,2,1,0:T(8,128)(2,1)}) custom-call(s32[1]{0:T(128)} %bitcast.6.first_ref, bf16[40,1536]{1,0:T(8,128)(2,1)} %fusion.19.router_ref, ...), custom_call_target="tpu_custom_call", output_to_operand_aliasing={{4}: (13, {})} | custom-call | flops 1000000 | bytes 100000 | tf_op jit(solution)/shard_map/moe/pallas_call | solution.py:505
  238.2 6.2 %collective-permute-done.31 = bf16[1024,1664]{1,0:T(8,128)(2,1)S(1)} collective-permute-done((bf16[1024,1664]{1,0:T(8,128)(2,1)}, bf16[1024,1664]{1,0:T(8,128)(2,1)S(1)}, u32[]{:S(2)}, u32[]{:S(2)}) %collective-permute-start.31) | collective-permute-done | bytes 3407904 | tf_op jit(solution)/shard_map/ppermute | solution.py:548
  253.5 6.9 %collective-permute-done.38 = bf16[128,1664]{1,0:T(8,128)(2,1)S(1)} collective-permute-done((bf16[128,1664]{1,0:T(8,128)(2,1)S(1)}, bf16[128,1664]{1,0:T(8,128)(2,1)S(1)}, u32[]{:S(2)}, u32[]{:S(2)}) %collective-permute-start.38) | collective-permute-done | bytes 426016 | tf_op jit(solution)/shard_map/ppermute | solution.py:544
  262.8 8.3 %collective-permute-done.37 = bf16[128,1664]{1,0:T(8,128)(2,1)S(1)} collective-permute-done((bf16[128,1664]{1,0:T(8,128)(2,1)S(1)}, bf16[128,1664]{1,0:T(8,128)(2,1)S(1)}, u32[]{:S(2)}, u32[]{:S(2)}) %collective-permute-start.37) | collective-permute-done | bytes 426016 | tf_op jit(solution)/shard_map/ppermute | solution.py:544
  280.2 8.5 %collective-permute-done.35 = bf16[128,1664]{1,0:T(8,128)(2,1)S(1)} collective-permute-done((bf16[128,1664]{1,0:T(8,128)(2,1)S(1)}, bf16[128,1664]{1,0:T(8,128)(2,1)S(1)}, u32[]{:S(2)}, u32[]{:S(2)}) %collective-permute-start.35) | collective-permute-done | bytes 426016 | tf_op jit(solution)/shard_map/ppermute | solution.py:544
  297.5 13.9 %collective-permute-done.40.refs_1_ = bf16[128,1536]{1,0:T(8,128)(2,1)} collective-permute-done((bf16[128,1536]{1,0:T(8,128)(2,1)S(1)}, bf16[128,1536]{1,0:T(8,128)(2,1)}, u32[]{:S(2)}, u32[]{:S(2)}) %collective-permute-start.40) | collective-permute-done | bytes 393248 | tf_op jit(solution)/shard_map/ppermute | solution.py:544
  314.6 19.0 %attend_back.1 = (bf16[512,1536]{1,0:T(8,128)(2,1)}, bf16[560,1536]{1,0:T(8,128)(2,1)}, bf16[4,192,512]{2,1,0:T(8,128)(2,1)}, bf16[4,192,512]{2,1,0:T(8,128)(2,1)}) custom-call(s32[8]{0:T(128)} %pad_add_fusion.order_ref, s32[8]{0:T(128)} %iota_xor_fusion.spread_ref, s32[1,1024]{1,0:T(1,128)} %bitcast.98, s32[1024,1]{1,0:T(8,128)} %copy.104.doc_col_ref, ...), custom_call_target="tpu_custom_call" | custom-call | flops 1000000 | bytes 100000 | tf_op jit(solution)/shard_map/attend_back/pallas_call | solution.py:304
  333.7 3.7 collective-permute-done.47
  345.2 21.0 %collective-permute-done.48 = bf16[176,1536]{1,0:T(8,128)(2,1)S(1)} collective-permute-done((bf16[176,1536]{1,0:T(8,128)(2,1)S(1)}, bf16[176,1536]{1,0:T(8,128)(2,1)S(1)}, u32[]{:S(2)}, u32[]{:S(2)}) %collective-permute-start.48) | collective-permute-done | bytes 540704 | tf_op jit(solution)/shard_map/ppermute | solution.py:544
  366.2 3.6 collective-permute-done.50
  374.1 17.5 %collective-permute-start.55 = (bf16[528,512]{1,0:T(8,128)(2,1)}, bf16[528,512]{1,0:T(8,128)(2,1)}, u32[]{:S(2)}, u32[]{:S(2)}) collective-permute-start(bf16[528,512]{1,0:T(8,128)(2,1)} %pad_maximum_fusion.8), channel_id=1, source_target_pairs={{0,32},{16,48},{32,0},{48,16},{64,96},{80,112},{96,64},{112,80},{1... | collective-permute-start | bytes 1622024 | tf_op jit(solution)/shard_map/ppermute | solution.py:557
  396.1 11.0 %update_experts.1 = (f32[3840,128]{1,0:T(8,128)}, f32[3840,128]{1,0:T(8,128)}, f32[3840,128]{1,0:T(8,128)}, f32[5,192,256]{2,1,0:T(8,128)}, f32[5,192,256]{2,1,0:T(8,128)}, /*index=5*/f32[5,192,256]{2,1,0:T(8,128)}) custom-call(bf16[5,192,768]{2,1,0:T(8,128)(2,1)} %bitcast.91, f32[3840,128]{1,0:T(8,128)} %bitcast.83, f32[3840,128]{1,0:T(8,128)} %bitcast.87, ...), custom_call_target="tpu_custom_call" | custom-call | flops 20000000 | bytes 20000000 | tf_op jit(solution)/shard_map/update_experts/pallas_call | solution.py:83
  410.9 16.2 %collective-permute-done.51 = bf16[256,1536]{1,0:T(8,128)(2,1)} collective-permute-done((bf16[256,1536]{1,0:T(8,128)(2,1)}, bf16[256,1536]{1,0:T(8,128)(2,1)}, u32[]{:S(2)}, u32[]{:S(2)}) %collective-permute-start.51) | collective-permute-done | bytes 786464 | tf_op jit(solution)/shard_map/ppermute | solution.py:544
  427.0 3.7 collective-permute-done.53
  437.2 6.1 %collective-permute-done.58 = bf16[336,512]{1,0:T(8,128)(2,1)S(1)} collective-permute-done((bf16[336,512]{1,0:T(8,128)(2,1)S(1)}, bf16[336,512]{1,0:T(8,128)(2,1)S(1)}, u32[]{:S(2)}, u32[]{:S(2)}) %collective-permute-start.58) | collective-permute-done | bytes 344096 | tf_op jit(solution)/shard_map/ppermute | solution.py:552
  (330 shorter events, 167.9 us)
Async XLA Ops:
  7.2 57.8 %all-gather.6.cloned.1.call-start = ((), (), s32[]{:S(2)}) async-start(), calls=%async_computation.1 | async-start | bytes 1769472 | tf_op jit(solution)/shard_map/all_gather | solution.py:656
  10.2 134.8 %all-gather.10.cloned.1.call-start = ((), (), s32[]{:S(2)}) async-start(), calls=%async_computation.4 | async-start | bytes 7962624 | tf_op jit(solution)/shard_map/all_gather | solution.py:664
  17.7 182.9 %all-gather.8.cloned.1.call-start = ((), (), s32[]{:S(2)}) async-start(), calls=%async_computation.3 | async-start | bytes 5308416 | tf_op jit(solution)/shard_map/all_gather | solution.py:664
  21.7 20.1 %collective-permute-start.7 = (bf16[128,1664]{1,0:T(8,128)(2,1)S(1)}, bf16[128,1664]{1,0:T(8,128)(2,1)S(1)}, u32[]{:S(2)}, u32[]{:S(2)}) collective-permute-start(bf16[128,1664]{1,0:T(8,128)(2,1)S(1)} %concatenate.73), channel_id=1, source_target_pairs={{0,6},{1,7},{2,0},{3,1},{4,2},{5,3},{6,4},{7,5},{8,14},{9,15},{10,... | collective-permute-start | bytes 1277960 | tf_op jit(solution)/shard_map/ppermute | solution.py:544
  24.6 20.2 %collective-permute-start.9 = (bf16[128,1664]{1,0:T(8,128)(2,1)S(1)}, bf16[128,1664]{1,0:T(8,128)(2,1)}, u32[]{:S(2)}, u32[]{:S(2)}) collective-permute-start(bf16[128,1664]{1,0:T(8,128)(2,1)S(1)} %concatenate.73), channel_id=1, source_target_pairs={{0,8},{8,0},{1,9},{9,1},{2,10},{10,2},{3,11},{11,3},{4,12},{12,4},... | collective-permute-start | bytes 1277960 | tf_op jit(solution)/shard_map/ppermute | solution.py:552
  28.7 367.4 %reduce-scatter.2.cloned.1.call-start = ((), (), s32[]{:S(2)}) async-start(), calls=%async_computation.2 | async-start | bytes 13271040 | tf_op jit(solution)/shard_map/reduce_scatter | solution.py:700
  78.0 29.3 %collective-permute-start.18 = (bf16[512,1664]{1,0:T(8,128)(2,1)}, bf16[512,1664]{1,0:T(8,128)(2,1)S(1)}, u32[]{:S(2)}, u32[]{:S(2)}) collective-permute-start(bf16[512,1664]{1,0:T(8,128)(2,1)} %copy-done.2), channel_id=1, source_target_pairs={{0,1},{1,0},{2,3},{3,2},{4,5},{5,4},{6,7},{7,6},{8,9},{9,8},{10,11... | collective-permute-start | bytes 5111816 | tf_op jit(solution)/shard_map/ppermute | solution.py:548
  78.5 28.8 %collective-permute-start.19 = (bf16[512,1664]{1,0:T(8,128)(2,1)S(1)}, bf16[512,1664]{1,0:T(8,128)(2,1)S(1)}, u32[]{:S(2)}, u32[]{:S(2)}) collective-permute-start(bf16[512,1664]{1,0:T(8,128)(2,1)S(1)} %constant_dynamic-update-slice_fusion.10.refs_5_), channel_id=1, source_target_pairs={{0,1},{1,0},{2,3},{3,2},{4,5},{5,4},{6,7},{7,6},{8,9},{9,8},{10,11... | collective-permute-start | bytes 5111816 | tf_op jit(solution)/shard_map/ppermute | solution.py:548
  83.7 22.0 %collective-permute-start.16 = (bf16[128,1536]{1,0:T(8,128)(2,1)S(1)}, bf16[128,1536]{1,0:T(8,128)(2,1)S(1)}, u32[]{:S(2)}, u32[]{:S(2)}) collective-permute-start(bf16[128,1536]{1,0:T(8,128)(2,1)S(1)} %get-tuple-element.257), channel_id=1, source_target_pairs={{0,4},{1,5},{2,6},{3,7},{4,0},{5,1},{6,2},{7,3},{8,12},{9,13},{10,... | collective-permute-start | bytes 1179656 | tf_op jit(solution)/shard_map/ppermute | solution.py:544
  244.4 31.0 %collective-permute-start.32 = (bf16[1024,1536]{1,0:T(8,128)(2,1)}, bf16[1024,1536]{1,0:T(8,128)(2,1)S(1)}, u32[]{:S(2)}, u32[]{:S(2)}) collective-permute-start(bf16[1024,1536]{1,0:T(8,128)(2,1)} %get-tuple-element.91), channel_id=1, source_target_pairs={{0,1},{1,0},{2,3},{3,2},{4,5},{5,4},{6,7},{7,6},{8,9},{9,8},{10,11... | collective-permute-start | bytes 9437192 | tf_op jit(solution)/shard_map/ppermute | solution.py:548
  248.6 22.4 %collective-permute-start.37 = (bf16[128,1664]{1,0:T(8,128)(2,1)S(1)}, bf16[128,1664]{1,0:T(8,128)(2,1)S(1)}, u32[]{:S(2)}, u32[]{:S(2)}) collective-permute-start(bf16[128,1664]{1,0:T(8,128)(2,1)S(1)} %get-tuple-element.239), channel_id=1, source_target_pairs={{0,4},{1,5},{2,6},{3,7},{4,0},{5,1},{6,2},{7,3},{8,12},{9,13},{10,... | collective-permute-start | bytes 1277960 | tf_op jit(solution)/shard_map/ppermute | solution.py:544
  251.3 19.8 %collective-permute-start.36 = (bf16[128,1664]{1,0:T(8,128)(2,1)S(1)}, bf16[128,1664]{1,0:T(8,128)(2,1)S(1)}, u32[]{:S(2)}, u32[]{:S(2)}) collective-permute-start(bf16[128,1664]{1,0:T(8,128)(2,1)S(1)} %get-tuple-element.240), channel_id=1, source_target_pairs={{0,6},{1,7},{2,0},{3,1},{4,2},{5,3},{6,4},{7,5},{8,14},{9,15},{10,... | collective-permute-start | bytes 1277960 | tf_op jit(solution)/shard_map/ppermute | solution.py:544
  253.5 26.7 %collective-permute-start.33 = (bf16[128,1664]{1,0:T(8,128)(2,1)S(1)}, bf16[128,1664]{1,0:T(8,128)(2,1)S(1)}, u32[]{:S(2)}, u32[]{:S(2)}) collective-permute-start(bf16[128,1664]{1,0:T(8,128)(2,1)S(1)} %get-tuple-element.242), channel_id=1, source_target_pairs={{0,6},{1,7},{2,0},{3,1},{4,2},{5,3},{6,4},{7,5},{8,14},{9,15},{10,... | collective-permute-start | bytes 1277960 | tf_op jit(solution)/shard_map/ppermute | solution.py:544
  260.4 19.8 %collective-permute-start.34 = (bf16[128,1664]{1,0:T(8,128)(2,1)S(1)}, bf16[128,1664]{1,0:T(8,128)(2,1)S(1)}, u32[]{:S(2)}, u32[]{:S(2)}) collective-permute-start(bf16[128,1664]{1,0:T(8,128)(2,1)S(1)} %get-tuple-element.241), channel_id=1, source_target_pairs={{0,4},{1,5},{2,6},{3,7},{4,0},{5,1},{6,2},{7,3},{8,12},{9,13},{10,... | collective-permute-start | bytes 1277960 | tf_op jit(solution)/shard_map/ppermute | solution.py:544
  290.6 20.8 %collective-permute-start.40 = (bf16[128,1536]{1,0:T(8,128)(2,1)S(1)}, bf16[128,1536]{1,0:T(8,128)(2,1)}, u32[]{:S(2)}, u32[]{:S(2)}) collective-permute-start(bf16[128,1536]{1,0:T(8,128)(2,1)S(1)} %fusion.30.refs_0_), channel_id=1, source_target_pairs={{0,2},{1,3},{2,4},{3,5},{4,6},{5,7},{6,0},{7,1},{8,10},{9,11},{10,... | collective-permute-start | bytes 1179656 | tf_op jit(solution)/shard_map/ppermute | solution.py:544
  340.2 26.0 %collective-permute-start.48 = (bf16[176,1536]{1,0:T(8,128)(2,1)S(1)}, bf16[176,1536]{1,0:T(8,128)(2,1)S(1)}, u32[]{:S(2)}, u32[]{:S(2)}) collective-permute-start(bf16[176,1536]{1,0:T(8,128)(2,1)S(1)} %get-tuple-element.266), channel_id=1, source_target_pairs={{0,6},{1,7},{2,0},{3,1},{4,2},{5,3},{6,4},{7,5},{8,14},{9,15},{10,... | collective-permute-start | bytes 1622024 | tf_op jit(solution)/shard_map/ppermute | solution.py:544
  342.8 23.5 %collective-permute-start.49 = (bf16[176,1536]{1,0:T(8,128)(2,1)S(1)}, bf16[176,1536]{1,0:T(8,128)(2,1)S(1)}, u32[]{:S(2)}, u32[]{:S(2)}) collective-permute-start(bf16[176,1536]{1,0:T(8,128)(2,1)S(1)} %get-tuple-element.265), channel_id=1, source_target_pairs={{0,4},{1,5},{2,6},{3,7},{4,0},{5,1},{6,2},{7,3},{8,12},{9,13},{10,... | collective-permute-start | bytes 1622024 | tf_op jit(solution)/shard_map/ppermute | solution.py:544
  343.3 26.6 %collective-permute-start.50 = (bf16[176,1536]{1,0:T(8,128)(2,1)S(1)}, bf16[176,1536]{1,0:T(8,128)(2,1)S(1)}, u32[]{:S(2)}, u32[]{:S(2)}) collective-permute-start(bf16[176,1536]{1,0:T(8,128)(2,1)S(1)} %get-tuple-element.264), channel_id=1, source_target_pairs={{0,2},{1,3},{2,4},{3,5},{4,6},{5,7},{6,0},{7,1},{8,10},{9,11},{10,... | collective-permute-start | bytes 1622024 | tf_op jit(solution)/shard_map/ppermute | solution.py:544
  343.7 27.8 %collective-permute-start.54 = (bf16[4,192,512]{2,1,0:T(8,128)(2,1)}, bf16[4,192,512]{2,1,0:T(8,128)(2,1)}, u32[]{:S(2)}, u32[]{:S(2)}) collective-permute-start(bf16[4,192,512]{2,1,0:T(8,128)(2,1)} %get-tuple-element.120), channel_id=1, source_target_pairs={{0,64},{16,80},{32,96},{48,112},{64,0},{80,16},{96,32},{112,48},{1... | collective-permute-start | bytes 2359304 | tf_op jit(solution)/shard_map/ppermute | solution.py:561
  374.1 33.1 %collective-permute-start.55 = (bf16[528,512]{1,0:T(8,128)(2,1)}, bf16[528,512]{1,0:T(8,128)(2,1)}, u32[]{:S(2)}, u32[]{:S(2)}) collective-permute-start(bf16[528,512]{1,0:T(8,128)(2,1)} %pad_maximum_fusion.8), channel_id=1, source_target_pairs={{0,32},{16,48},{32,0},{48,16},{64,96},{80,112},{96,64},{112,80},{1... | collective-permute-start | bytes 1622024 | tf_op jit(solution)/shard_map/ppermute | solution.py:557
  391.5 35.5 %collective-permute-start.51 = (bf16[256,1536]{1,0:T(8,128)(2,1)}, bf16[256,1536]{1,0:T(8,128)(2,1)}, u32[]{:S(2)}, u32[]{:S(2)}) collective-permute-start(bf16[256,1536]{1,0:T(8,128)(2,1)} %pad_maximum_fusion.5), channel_id=1, source_target_pairs={{0,6},{1,7},{2,0},{3,1},{4,2},{5,3},{6,4},{7,5},{8,14},{9,15},{10,... | collective-permute-start | bytes 2359304 | tf_op jit(solution)/shard_map/ppermute | solution.py:544
  394.5 32.5 %collective-permute-start.52 = (bf16[256,1536]{1,0:T(8,128)(2,1)}, bf16[256,1536]{1,0:T(8,128)(2,1)}, u32[]{:S(2)}, u32[]{:S(2)}) collective-permute-start(bf16[256,1536]{1,0:T(8,128)(2,1)} %pad_maximum_fusion.6), channel_id=1, source_target_pairs={{0,4},{1,5},{2,6},{3,7},{4,0},{5,1},{6,2},{7,3},{8,12},{9,13},{10,... | collective-permute-start | bytes 2359304 | tf_op jit(solution)/shard_map/ppermute | solution.py:544
  395.4 35.3 %collective-permute-start.53 = (bf16[256,1536]{1,0:T(8,128)(2,1)}, bf16[256,1536]{1,0:T(8,128)(2,1)}, u32[]{:S(2)}, u32[]{:S(2)}) collective-permute-start(bf16[256,1536]{1,0:T(8,128)(2,1)} %pad_maximum_fusion.7), channel_id=1, source_target_pairs={{0,2},{1,3},{2,4},{3,5},{4,6},{5,7},{6,0},{7,1},{8,10},{9,11},{10,... | collective-permute-start | bytes 2359304 | tf_op jit(solution)/shard_map/ppermute | solution.py:544
  408.5 22.2 %collective-permute-start.57 = (bf16[336,512]{1,0:T(8,128)(2,1)S(1)}, bf16[336,512]{1,0:T(8,128)(2,1)S(1)}, u32[]{:S(2)}, u32[]{:S(2)}) collective-permute-start(bf16[336,512]{1,0:T(8,128)(2,1)S(1)} %slice.425), channel_id=1, source_target_pairs={{0,16},{16,0},{32,48},{48,32},{64,80},{80,64},{96,112},{112,96},{1... | collective-permute-start | bytes 1032200 | tf_op jit(solution)/shard_map/ppermute | solution.py:607
  (90 other events, 876.9 us)
Sparse Core Ops, SparseCore 0:
  10.4 42.4 all-gather.5
  55.1 83.3 all-gather.9
  140.7 59.8 all-gather.7
  238.2 127.3 reduce-scatter.1

commit v5 on v4

--- a/solution.py
+++ b/solution.py
@@ -60,7 +60,7 @@
     olds, news = refs[:6], refs[6:]
     for half in range(FF_DEV // 128):
         for kind in range(2):
-            at = pl.ds(2 * half + kind, STORED // 2, stride=4)
+            at = pl.ds(2 * half + kind, STORED, stride=4)
             start = kind * FF_DEV + half * 128
             gradient = g_ref[0, :, start : start + 128].astype(F32)
             weight, first, second = (ref[at, :] for ref in olds[:3])
@@ -75,15 +75,15 @@
 
 
 def update_experts(gradient, gate_up, down):
-    pair_rows = pl.BlockSpec((2 * STORED, 128), lambda e, i: (2 * e + i, 0))
-    down_rows = pl.BlockSpec((1, STORED // 2, FF_DEV), lambda e, i: (e, i, 0))
+    pair_rows = pl.BlockSpec((4 * STORED, 128), lambda i: (i, 0))
+    down_rows = pl.BlockSpec((1, STORED, FF_DEV), lambda i: (i, 0, 0))
     specs = [pair_rows] * 3 + [down_rows] * 3
     pair_shape = jax.ShapeDtypeStruct((EXPERTS_DEV * 4 * STORED, 128), F32)
     down_shape = jax.ShapeDtypeStruct((EXPERTS_DEV, STORED, FF_DEV), F32)
     new = pl.pallas_call(
         adamw_kernel,
-        grid=(EXPERTS_DEV, 2),
-        in_specs=[pl.BlockSpec((1, STORED // 2, 3 * FF_DEV), lambda e, i: (e, i, 0))] + specs,
+        grid=(EXPERTS_DEV,),
+        in_specs=[pl.BlockSpec((1, STORED, 3 * FF_DEV), lambda i: (i, 0, 0))] + specs,
         out_specs=specs,
         out_shape=[pair_shape] * 3 + [down_shape] * 3,
         cost_estimate=pl.CostEstimate(
@@ -760,7 +760,6 @@
         expert_sum, (w_gate_up, gate_up_first, gate_up_second), (w_down, down_first, down_second)
     )
     kept = total([kept, after(along_z(sent, 2), experts_new)]).astype(BF16)
-    mix_moved = after(mix_moved, kept)
     sent = kept[STORED:]
     kept = jnp.concatenate([kept[:STORED], kept[2 * STORED :]], axis=0)
     kept = total([kept, flip_z(sent)]).astype(BF16)
@@ -769,6 +768,7 @@
     small = add_both(kept[STORED:], other_y)
     sum_qkv = attn_sums[:, None, :QKV].astype(F32)
     proj_new = update_proj(attn_sums, w_proj, proj_first, proj_second)
+    mix_moved = after(mix_moved, dtokens, attn_sums)
     mixed = total(mix_moved)
     mix_theirs = after(other_row(mixed[ROWS:].astype(BF16)), proj_new, small)
     mixture = mixed[:ROWS] + mix_theirs.astype(F32)

time: 479 us -> 465 us (0.971)
  waiting for transfers between devices: 160 us -> 148 us
  local copies, waits for them, and re-layouts: 30.1 us -> 25.1 us
    ppermute x38, waiting for transfers between devices: 126 us -> 113 us  [across_col(): return lax.ppermute(value, 'col', pairs)]
    ppermute x1, waiting for transfers between devices: 0.01 us -> 6.48 us  [flip_z(): return lax.ppermute(value, 'dp', [(s, s ^ 1) for s in range(8)])]
    unnamed x127 -> x117, local copies, waits for them, and re-layouts: 14.8 us -> 13.8 us
  transfers between devices with their start and end apart: 64 -> 64, of which waited for: 30 -> 30; matrix products, arithmetic and copies ran while one was open for 12% -> 13% of each run, Pallas kernels for 20% -> 20%
where the time goes in v5:
time: 465 us; the launch traced here: 457 us
  waiting for transfers between devices  148 us (32%)
  Pallas kernels  129 us (28%)
  starting transfers between devices  98.7 us (21%)
  other arithmetic  40 us (9%)
  local copies, waits for them, and re-layouts  25.1 us (5%)
  between operations  15.1 us (3%)
    ppermute x38, waiting for transfers between devices, across_col(): return lax.ppermute(value, 'col', pairs)  113 us
    pallas_call x2, Pallas kernels, moe(): pl.pallas_call(functools.partial(moe_kernel, begin=begin, count=count, mo...  84.5 us
    ppermute x38, starting transfers between devices, across_col(): return lax.ppermute(value, 'col', pairs)  60.9 us
    pallas_call x1, Pallas kernels, attend_back(): pl.pallas_call(attend_back_kernel, in_specs=[smem_spec()] * 2 + [vmem_spe...  19 us
    ppermute x1, starting transfers between devices, along_z(): return lax.ppermute(value, 'dp', pairs)  18 us
    ppermute x13, waiting for transfers between devices, other_core(): return lax.ppermute(value, 'col', [(s, s ^ 1) for s in range(8)])  16.9 us
    ppermute x5, starting transfers between devices, other_row(): return lax.ppermute(value, 'row', [(0, 1), (1, 0)])  15.3 us
    unnamed x117, local copies, waits for them, and re-layouts  13.8 us
  transfers between devices with their start and end apart: 64, of which 30 were waited for; matrix products, arithmetic and copies ran while one was open for 13% of the time, Pallas kernels for 20%

profile of v5, /device:TPU:32, one launch (start us, length us, event | category | flops | bytes accessed | tf_op | source)
XLA Modules:
  0.0 457.4 jit_solution(15977028352748404365)
XLA Ops:
  50.7 6.4 %collective-permute-done.10 = bf16[128,1664]{1,0:T(8,128)(2,1)S(1)} collective-permute-done((bf16[128,1664]{1,0:T(8,128)(2,1)}, bf16[128,1664]{1,0:T(8,128)(2,1)S(1)}, u32[]{:S(2)}, u32[]{:S(2)}) %collective-permute-start.10) | collective-permute-done | bytes 426016 | tf_op jit(solution)/shard_map/ppermute | solution.py:544
  60.8 3.5 collective-permute-done.11
  64.5 13.0 %attend.1 = (bf16[1024,1536]{1,0:T(8,128)(2,1)}, bf16[1024,320]{1,0:T(8,128)(2,1)}, bf16[1024,256]{1,0:T(8,128)(2,1)}, f32[8,1024]{1,0:T(8,128)}, bf16[512,1536]{1,0:T(8,128)(2,1)}, /*index=5*/bf16[512,1536]{1,0:T(8,128)(2,1)}) custom-call(s32[8]{0:T(128)} %pad_add_fusion.order_ref, s32[1,1024]{1,0:T(1,128)} %bitcast.97, s32[1024,1]{1,0:T(8,128)} %copy.104.doc_col_ref, ...), custom_call_target="tpu_custom_call" | custom-call | flops 1000000 | bytes 100000 | tf_op jit(solution)/shard_map/attend/pallas_call | solution.py:283
  87.1 16.1 %collective-permute-done.15 = bf16[128,1536]{1,0:T(8,128)(2,1)S(1)} collective-permute-done((bf16[128,1536]{1,0:T(8,128)(2,1)S(1)}, bf16[128,1536]{1,0:T(8,128)(2,1)S(1)}, u32[]{:S(2)}, u32[]{:S(2)}) %collective-permute-start.15) | collective-permute-done | bytes 393248 | tf_op jit(solution)/shard_map/ppermute | solution.py:544
  115.6 4.8 %collective-permute-done.20 = bf16[128,1536]{1,0:T(8,128)(2,1)S(1)} collective-permute-done((bf16[128,1536]{1,0:T(8,128)(2,1)S(1)}, bf16[128,1536]{1,0:T(8,128)(2,1)S(1)}, u32[]{:S(2)}, u32[]{:S(2)}) %collective-permute-start.20) | collective-permute-done | bytes 393248 | tf_op jit(solution)/shard_map/ppermute | solution.py:544
  131.0 4.7 %collective-permute-done.25 = bf16[128,1536]{1,0:T(8,128)(2,1)S(1)} collective-permute-done((bf16[128,1536]{1,0:T(8,128)(2,1)S(1)}, bf16[128,1536]{1,0:T(8,128)(2,1)S(1)}, u32[]{:S(2)}, u32[]{:S(2)}) %collective-permute-start.25) | collective-permute-done | bytes 393248 | tf_op jit(solution)/shard_map/ppermute | solution.py:544
  139.2 3.5 collective-permute-done.26
  146.4 47.0 %moe.2 = (bf16[2048,1536]{1,0:T(8,128)(2,1)}, bf16[2048,1664]{1,0:T(8,128)(2,1)}, bf16[8,5,192,768]{3,2,1,0:T(8,128)(2,1)}) custom-call(s32[1]{0:T(128)} %bitcast.6.first_ref, bf16[40,1536]{1,0:T(8,128)(2,1)} %fusion.19.router_ref, bf16[8,3,192,768]{3,2,1,0:T(8,128)(2,1)} %bitcast.84, bf16[512,1536]{1,0:T(8,128)(2,1)} %constant_dynamic-update-slice_fusion.15.refs_0_, ...), custom_call_target="tpu_custom_call" | custom-call | flops 1000000 | bytes 100000 | tf_op jit(solution)/shard_map/moe/pallas_call | solution.py:505
  193.4 7.2 %all-gather.8.cloned.1.call-done = bf16[16,192,768]{2,1,0:T(8,128)(2,1)} async-done(((bf16[2,192,768]{2,1,0:T(8,128)(2,1)}), bf16[16,192,768]{2,1,0:T(8,128)(2,1)}) %all-gather.8.cloned.1.call-update) | async-done | bytes 4718608 | tf_op jit(solution)/shard_map/all_gather | solution.py:664
  200.6 37.5 %moe.3 = (bf16[1024,1536]{1,0:T(8,128)(2,1)}, bf16[1024,1664]{1,0:T(8,128)(2,1)}, bf16[1024,1536]{1,0:T(8,128)(2,1)}, bf16[1024,1664]{1,0:T(8,128)(2,1)}, bf16[8,5,192,768]{3,2,1,0:T(8,128)(2,1)}) custom-call(s32[1]{0:T(128)} %bitcast.6.first_ref, bf16[40,1536]{1,0:T(8,128)(2,1)} %fusion.19.router_ref, ...), custom_call_target="tpu_custom_call", output_to_operand_aliasing={{4}: (13, {})} | custom-call | flops 1000000 | bytes 100000 | tf_op jit(solution)/shard_map/moe/pallas_call | solution.py:505
  238.2 6.2 %collective-permute-done.31 = bf16[1024,1664]{1,0:T(8,128)(2,1)S(1)} collective-permute-done((bf16[1024,1664]{1,0:T(8,128)(2,1)}, bf16[1024,1664]{1,0:T(8,128)(2,1)S(1)}, u32[]{:S(2)}, u32[]{:S(2)}) %collective-permute-start.31) | collective-permute-done | bytes 3407904 | tf_op jit(solution)/shard_map/ppermute | solution.py:548
  254.7 14.3 %collective-permute-done.36 = bf16[128,1664]{1,0:T(8,128)(2,1)S(1)} collective-permute-done((bf16[128,1664]{1,0:T(8,128)(2,1)S(1)}, bf16[128,1664]{1,0:T(8,128)(2,1)S(1)}, u32[]{:S(2)}, u32[]{:S(2)}) %collective-permute-start.36) | collective-permute-done | bytes 426016 | tf_op jit(solution)/shard_map/ppermute | solution.py:544
  269.0 4.7 %collective-permute-start.35 = (bf16[128,1664]{1,0:T(8,128)(2,1)S(1)}, bf16[128,1664]{1,0:T(8,128)(2,1)S(1)}, u32[]{:S(2)}, u32[]{:S(2)}) collective-permute-start(bf16[128,1664]{1,0:T(8,128)(2,1)S(1)} %get-tuple-element.237), channel_id=1, source_target_pairs={{0,2},{1,3},{2,4},{3,5},{4,6},{5,7},{6,0},{7,1},{8,10},{9,11},{10,... | collective-permute-start | bytes 1277960 | tf_op jit(solution)/shard_map/ppermute | solution.py:544
  282.8 4.0 collective-permute-done.33
  286.9 3.7 collective-permute-done.35
  298.0 15.2 %collective-permute-done.40.refs_1_ = bf16[128,1536]{1,0:T(8,128)(2,1)} collective-permute-done((bf16[128,1536]{1,0:T(8,128)(2,1)S(1)}, bf16[128,1536]{1,0:T(8,128)(2,1)}, u32[]{:S(2)}, u32[]{:S(2)}) %collective-permute-start.40) | collective-permute-done | bytes 393248 | tf_op jit(solution)/shard_map/ppermute | solution.py:544
  316.4 19.0 %attend_back.1 = (bf16[512,1536]{1,0:T(8,128)(2,1)}, bf16[560,1536]{1,0:T(8,128)(2,1)}, bf16[4,192,512]{2,1,0:T(8,128)(2,1)}, bf16[4,192,512]{2,1,0:T(8,128)(2,1)}) custom-call(s32[8]{0:T(128)} %pad_add_fusion.order_ref, s32[8]{0:T(128)} %iota_xor_fusion.spread_ref, s32[1,1024]{1,0:T(1,128)} %bitcast.98, s32[1024,1]{1,0:T(8,128)} %copy.104.doc_col_ref, ...), custom_call_target="tpu_custom_call" | custom-call | flops 1000000 | bytes 100000 | tf_op jit(solution)/shard_map/attend_back/pallas_call | solution.py:304
  335.5 3.7 collective-permute-done.47
  346.9 21.0 %collective-permute-done.48 = bf16[176,1536]{1,0:T(8,128)(2,1)S(1)} collective-permute-done((bf16[176,1536]{1,0:T(8,128)(2,1)S(1)}, bf16[176,1536]{1,0:T(8,128)(2,1)S(1)}, u32[]{:S(2)}, u32[]{:S(2)}) %collective-permute-start.48) | collective-permute-done | bytes 540704 | tf_op jit(solution)/shard_map/ppermute | solution.py:544
  375.5 18.0 %collective-permute-start.55 = (bf16[528,512]{1,0:T(8,128)(2,1)}, bf16[528,512]{1,0:T(8,128)(2,1)}, u32[]{:S(2)}, u32[]{:S(2)}) collective-permute-start(bf16[528,512]{1,0:T(8,128)(2,1)} %pad_maximum_fusion.8), channel_id=1, source_target_pairs={{0,32},{16,48},{32,0},{48,16},{64,96},{80,112},{96,64},{112,80},{1... | collective-permute-start | bytes 1622024 | tf_op jit(solution)/shard_map/ppermute | solution.py:557
  397.8 9.9 %update_experts.1 = (f32[3840,128]{1,0:T(8,128)}, f32[3840,128]{1,0:T(8,128)}, f32[3840,128]{1,0:T(8,128)}, f32[5,192,256]{2,1,0:T(8,128)}, f32[5,192,256]{2,1,0:T(8,128)}, /*index=5*/f32[5,192,256]{2,1,0:T(8,128)}) custom-call(bf16[5,192,768]{2,1,0:T(8,128)(2,1)} %bitcast.91, f32[3840,128]{1,0:T(8,128)} %bitcast.83, f32[3840,128]{1,0:T(8,128)} %bitcast.87, ...), custom_call_target="tpu_custom_call" | custom-call | flops 20000000 | bytes 20000000 | tf_op jit(solution)/shard_map/update_experts/pallas_call | solution.py:83
  411.0 6.5 %collective-permute-done.56 = bf16[336,512]{1,0:T(8,128)(2,1)S(1)} collective-permute-done((bf16[336,512]{1,0:T(8,128)(2,1)S(1)}, bf16[336,512]{1,0:T(8,128)(2,1)S(1)}, u32[]{:S(2)}, u32[]{:S(2)}) %collective-permute-start.56) | collective-permute-done | bytes 344096 | tf_op jit(solution)/shard_map/ppermute | solution.py:607
  423.0 3.6 collective-permute-done.57
  429.5 3.7 collective-permute-done.53
  (321 shorter events, 165.2 us)
Async XLA Ops:
  7.2 57.2 %all-gather.6.cloned.1.call-start = ((), (), s32[]{:S(2)}) async-start(), calls=%async_computation.1 | async-start | bytes 1769472 | tf_op jit(solution)/shard_map/all_gather | solution.py:656
  10.2 136.2 %all-gather.10.cloned.1.call-start = ((), (), s32[]{:S(2)}) async-start(), calls=%async_computation.4 | async-start | bytes 7962624 | tf_op jit(solution)/shard_map/all_gather | solution.py:664
  17.7 182.8 %all-gather.8.cloned.1.call-start = ((), (), s32[]{:S(2)}) async-start(), calls=%async_computation.3 | async-start | bytes 5308416 | tf_op jit(solution)/shard_map/all_gather | solution.py:664
  21.3 22.5 %collective-permute-start.9 = (bf16[128,1664]{1,0:T(8,128)(2,1)S(1)}, bf16[128,1664]{1,0:T(8,128)(2,1)}, u32[]{:S(2)}, u32[]{:S(2)}) collective-permute-start(bf16[128,1664]{1,0:T(8,128)(2,1)S(1)} %concatenate.73), channel_id=1, source_target_pairs={{0,8},{8,0},{1,9},{9,1},{2,10},{10,2},{3,11},{11,3},{4,12},{12,4},... | collective-permute-start | bytes 1277960 | tf_op jit(solution)/shard_map/ppermute | solution.py:552
  28.7 369.1 %reduce-scatter.2.cloned.1.call-start = ((), (), s32[]{:S(2)}) async-start(), calls=%async_computation.2 | async-start | bytes 13271040 | tf_op jit(solution)/shard_map/reduce_scatter | solution.py:700
  77.5 30.8 %collective-permute-start.18 = (bf16[512,1664]{1,0:T(8,128)(2,1)}, bf16[512,1664]{1,0:T(8,128)(2,1)S(1)}, u32[]{:S(2)}, u32[]{:S(2)}) collective-permute-start(bf16[512,1664]{1,0:T(8,128)(2,1)} %copy-done.2), channel_id=1, source_target_pairs={{0,1},{1,0},{2,3},{3,2},{4,5},{5,4},{6,7},{7,6},{8,9},{9,8},{10,11... | collective-permute-start | bytes 5111816 | tf_op jit(solution)/shard_map/ppermute | solution.py:548
  78.0 30.3 %collective-permute-start.19 = (bf16[512,1664]{1,0:T(8,128)(2,1)S(1)}, bf16[512,1664]{1,0:T(8,128)(2,1)S(1)}, u32[]{:S(2)}, u32[]{:S(2)}) collective-permute-start(bf16[512,1664]{1,0:T(8,128)(2,1)S(1)} %constant_dynamic-update-slice_fusion.10.refs_5_), channel_id=1, source_target_pairs={{0,1},{1,0},{2,3},{3,2},{4,5},{5,4},{6,7},{7,6},{8,9},{9,8},{10,11... | collective-permute-start | bytes 5111816 | tf_op jit(solution)/shard_map/ppermute | solution.py:548
  82.7 20.6 %collective-permute-start.15 = (bf16[128,1536]{1,0:T(8,128)(2,1)S(1)}, bf16[128,1536]{1,0:T(8,128)(2,1)S(1)}, u32[]{:S(2)}, u32[]{:S(2)}) collective-permute-start(bf16[128,1536]{1,0:T(8,128)(2,1)S(1)} %get-tuple-element.255), channel_id=1, source_target_pairs={{0,6},{1,7},{2,0},{3,1},{4,2},{5,3},{6,4},{7,5},{8,14},{9,15},{10,... | collective-permute-start | bytes 1179656 | tf_op jit(solution)/shard_map/ppermute | solution.py:544
  86.1 20.5 %collective-permute-start.17 = (bf16[128,1536]{1,0:T(8,128)(2,1)S(1)}, bf16[128,1536]{1,0:T(8,128)(2,1)S(1)}, u32[]{:S(2)}, u32[]{:S(2)}) collective-permute-start(bf16[128,1536]{1,0:T(8,128)(2,1)S(1)} %get-tuple-element.256), channel_id=1, source_target_pairs={{0,2},{1,3},{2,4},{3,5},{4,6},{5,7},{6,0},{7,1},{8,10},{9,11},{10,... | collective-permute-start | bytes 1179656 | tf_op jit(solution)/shard_map/ppermute | solution.py:544
  244.4 33.7 %collective-permute-start.32 = (bf16[1024,1536]{1,0:T(8,128)(2,1)}, bf16[1024,1536]{1,0:T(8,128)(2,1)S(1)}, u32[]{:S(2)}, u32[]{:S(2)}) collective-permute-start(bf16[1024,1536]{1,0:T(8,128)(2,1)} %get-tuple-element.91), channel_id=1, source_target_pairs={{0,1},{1,0},{2,3},{3,2},{4,5},{5,4},{6,7},{7,6},{8,9},{9,8},{10,11... | collective-permute-start | bytes 9437192 | tf_op jit(solution)/shard_map/ppermute | solution.py:548
  247.1 21.9 %collective-permute-start.36 = (bf16[128,1664]{1,0:T(8,128)(2,1)S(1)}, bf16[128,1664]{1,0:T(8,128)(2,1)S(1)}, u32[]{:S(2)}, u32[]{:S(2)}) collective-permute-start(bf16[128,1664]{1,0:T(8,128)(2,1)S(1)} %get-tuple-element.240), channel_id=1, source_target_pairs={{0,6},{1,7},{2,0},{3,1},{4,2},{5,3},{6,4},{7,5},{8,14},{9,15},{10,... | collective-permute-start | bytes 1277960 | tf_op jit(solution)/shard_map/ppermute | solution.py:544
  250.7 23.0 %collective-permute-start.38 = (bf16[128,1664]{1,0:T(8,128)(2,1)S(1)}, bf16[128,1664]{1,0:T(8,128)(2,1)S(1)}, u32[]{:S(2)}, u32[]{:S(2)}) collective-permute-start(bf16[128,1664]{1,0:T(8,128)(2,1)S(1)} %get-tuple-element.238), channel_id=1, source_target_pairs={{0,2},{1,3},{2,4},{3,5},{4,6},{5,7},{6,0},{7,1},{8,10},{9,11},{10,... | collective-permute-start | bytes 1277960 | tf_op jit(solution)/shard_map/ppermute | solution.py:544
  252.3 34.6 %collective-permute-start.33 = (bf16[128,1664]{1,0:T(8,128)(2,1)S(1)}, bf16[128,1664]{1,0:T(8,128)(2,1)S(1)}, u32[]{:S(2)}, u32[]{:S(2)}) collective-permute-start(bf16[128,1664]{1,0:T(8,128)(2,1)S(1)} %get-tuple-element.242), channel_id=1, source_target_pairs={{0,6},{1,7},{2,0},{3,1},{4,2},{5,3},{6,4},{7,5},{8,14},{9,15},{10,... | collective-permute-start | bytes 1277960 | tf_op jit(solution)/shard_map/ppermute | solution.py:544
  269.0 21.5 %collective-permute-start.35 = (bf16[128,1664]{1,0:T(8,128)(2,1)S(1)}, bf16[128,1664]{1,0:T(8,128)(2,1)S(1)}, u32[]{:S(2)}, u32[]{:S(2)}) collective-permute-start(bf16[128,1664]{1,0:T(8,128)(2,1)S(1)} %get-tuple-element.237), channel_id=1, source_target_pairs={{0,2},{1,3},{2,4},{3,5},{4,6},{5,7},{6,0},{7,1},{8,10},{9,11},{10,... | collective-permute-start | bytes 1277960 | tf_op jit(solution)/shard_map/ppermute | solution.py:544
  292.4 20.8 %collective-permute-start.40 = (bf16[128,1536]{1,0:T(8,128)(2,1)S(1)}, bf16[128,1536]{1,0:T(8,128)(2,1)}, u32[]{:S(2)}, u32[]{:S(2)}) collective-permute-start(bf16[128,1536]{1,0:T(8,128)(2,1)S(1)} %fusion.30.refs_0_), channel_id=1, source_target_pairs={{0,2},{1,3},{2,4},{3,5},{4,6},{5,7},{6,0},{7,1},{8,10},{9,11},{10,... | collective-permute-start | bytes 1179656 | tf_op jit(solution)/shard_map/ppermute | solution.py:544
  292.5 20.7 %collective-permute-start.41 = (bf16[128,1536]{1,0:T(8,128)(2,1)S(1)}, bf16[128,1536]{1,0:T(8,128)(2,1)}, u32[]{:S(2)}, u32[]{:S(2)}) collective-permute-start(bf16[128,1536]{1,0:T(8,128)(2,1)S(1)} %fusion.30.refs_0_), channel_id=1, source_target_pairs={{0,4},{1,5},{2,6},{3,7},{4,0},{5,1},{6,2},{7,3},{8,12},{9,13},{10,... | collective-permute-start | bytes 1179656 | tf_op jit(solution)/shard_map/ppermute | solution.py:544
  342.0 25.9 %collective-permute-start.48 = (bf16[176,1536]{1,0:T(8,128)(2,1)S(1)}, bf16[176,1536]{1,0:T(8,128)(2,1)S(1)}, u32[]{:S(2)}, u32[]{:S(2)}) collective-permute-start(bf16[176,1536]{1,0:T(8,128)(2,1)S(1)} %get-tuple-element.264), channel_id=1, source_target_pairs={{0,6},{1,7},{2,0},{3,1},{4,2},{5,3},{6,4},{7,5},{8,14},{9,15},{10,... | collective-permute-start | bytes 1622024 | tf_op jit(solution)/shard_map/ppermute | solution.py:544
  344.4 23.5 %collective-permute-start.49 = (bf16[176,1536]{1,0:T(8,128)(2,1)S(1)}, bf16[176,1536]{1,0:T(8,128)(2,1)S(1)}, u32[]{:S(2)}, u32[]{:S(2)}) collective-permute-start(bf16[176,1536]{1,0:T(8,128)(2,1)S(1)} %get-tuple-element.263), channel_id=1, source_target_pairs={{0,4},{1,5},{2,6},{3,7},{4,0},{5,1},{6,2},{7,3},{8,12},{9,13},{10,... | collective-permute-start | bytes 1622024 | tf_op jit(solution)/shard_map/ppermute | solution.py:544
  344.4 26.8 %collective-permute-start.50 = (bf16[176,1536]{1,0:T(8,128)(2,1)S(1)}, bf16[176,1536]{1,0:T(8,128)(2,1)S(1)}, u32[]{:S(2)}, u32[]{:S(2)}) collective-permute-start(bf16[176,1536]{1,0:T(8,128)(2,1)S(1)} %get-tuple-element.262), channel_id=1, source_target_pairs={{0,2},{1,3},{2,4},{3,5},{4,6},{5,7},{6,0},{7,1},{8,10},{9,11},{10,... | collective-permute-start | bytes 1622024 | tf_op jit(solution)/shard_map/ppermute | solution.py:544
  345.4 27.5 %collective-permute-start.54 = (bf16[4,192,512]{2,1,0:T(8,128)(2,1)}, bf16[4,192,512]{2,1,0:T(8,128)(2,1)}, u32[]{:S(2)}, u32[]{:S(2)}) collective-permute-start(bf16[4,192,512]{2,1,0:T(8,128)(2,1)} %get-tuple-element.120), channel_id=1, source_target_pairs={{0,64},{16,80},{32,96},{48,112},{64,0},{80,16},{96,32},{112,48},{1... | collective-permute-start | bytes 2359304 | tf_op jit(solution)/shard_map/ppermute | solution.py:561
  375.5 32.3 %collective-permute-start.55 = (bf16[528,512]{1,0:T(8,128)(2,1)}, bf16[528,512]{1,0:T(8,128)(2,1)}, u32[]{:S(2)}, u32[]{:S(2)}) collective-permute-start(bf16[528,512]{1,0:T(8,128)(2,1)} %pad_maximum_fusion.8), channel_id=1, source_target_pairs={{0,32},{16,48},{32,0},{48,16},{64,96},{80,112},{96,64},{112,80},{1... | collective-permute-start | bytes 1622024 | tf_op jit(solution)/shard_map/ppermute | solution.py:557
  393.4 36.1 %collective-permute-start.51 = (bf16[256,1536]{1,0:T(8,128)(2,1)}, bf16[256,1536]{1,0:T(8,128)(2,1)}, u32[]{:S(2)}, u32[]{:S(2)}) collective-permute-start(bf16[256,1536]{1,0:T(8,128)(2,1)} %pad_maximum_fusion.5), channel_id=1, source_target_pairs={{0,6},{1,7},{2,0},{3,1},{4,2},{5,3},{6,4},{7,5},{8,14},{9,15},{10,... | collective-permute-start | bytes 2359304 | tf_op jit(solution)/shard_map/ppermute | solution.py:544
  396.1 33.4 %collective-permute-start.52 = (bf16[256,1536]{1,0:T(8,128)(2,1)}, bf16[256,1536]{1,0:T(8,128)(2,1)}, u32[]{:S(2)}, u32[]{:S(2)}) collective-permute-start(bf16[256,1536]{1,0:T(8,128)(2,1)} %pad_maximum_fusion.6), channel_id=1, source_target_pairs={{0,4},{1,5},{2,6},{3,7},{4,0},{5,1},{6,2},{7,3},{8,12},{9,13},{10,... | collective-permute-start | bytes 2359304 | tf_op jit(solution)/shard_map/ppermute | solution.py:544
  397.0 36.2 %collective-permute-start.53 = (bf16[256,1536]{1,0:T(8,128)(2,1)}, bf16[256,1536]{1,0:T(8,128)(2,1)}, u32[]{:S(2)}, u32[]{:S(2)}) collective-permute-start(bf16[256,1536]{1,0:T(8,128)(2,1)} %pad_maximum_fusion.7), channel_id=1, source_target_pairs={{0,2},{1,3},{2,4},{3,5},{4,6},{5,7},{6,0},{7,1},{8,10},{9,11},{10,... | collective-permute-start | bytes 2359304 | tf_op jit(solution)/shard_map/ppermute | solution.py:544
  (85 other events, 970.8 us)
Sparse Core Ops, SparseCore 0:
  10.4 42.7 all-gather.5
  55.4 82.1 all-gather.9
  139.8 60.6 all-gather.7
  238.2 127.4 reduce-scatter.1
